TPU v7x, 32 devices: a whole 2x2x4 slice. The times are simulated.
32 devices in a mesh: grp: 2 (over y), sub: 16 (over z, x, core).
Axes of the slice: x: 2, y: 2, z: 4, core: 2. Of those that a mesh axis runs over, the one named last changes fastest.
Arguments:
- right_sides: float32 [16384, 128], P(('grp', 'sub')), may hold values from -6 to 6
- basis_u: bfloat16 [5, 16384, 256], P(None, ('grp', 'sub')), may hold values from -0.15625 to 0.15625
- basis_v: bfloat16 [5, 16384, 256], P(None, ('grp', 'sub')), may hold values from -0.25 to 0.25
- coupling: bfloat16 [5, 8192, 512], P(None, ('grp', 'sub')), may hold values from -0.13258252 to 0.13258252, as said below
Outputs:
- solution: float32 [16384, 128], P(('grp', 'sub'))
Inputs may be any that keep to these rules, and one draw needn't show every extreme that they name: For level l the 256 rows of coupling on a device equal those on every device whose index (grp major) agrees with it in all bits from bit 5 - 5 + l upwards. Entries of level l are independent, of mean 0 and deviation (2 * 256 * 2**(0 + l))**-0.5, and lie within three such deviations.
All inputs are finite; a program needn't handle non-finite values.
Results may differ from a plain program's by a relative error of at most 0.0003.
Values sent between devices are 32-bit elements; how exact they have to be, the bound alone decides.
No kernel may reach another device: no remote copies, remote signals or barrier semaphores. Data moves between devices by JAX's collectives and lax.ppermute only.
A program may use at most 64 MiB of HBM per device.

v0:
```python
import jax
import jax.numpy as jnp
from jax import lax
from jax.sharding import PartitionSpec as P


def swapped(value, axis, bit):
    mask = 2**bit
    pairs = [(source, source ^ mask) for source in range(lax.axis_size(axis))]
    return lax.ppermute(value, axis, pairs)


def partner(value, bit, sub_bits):
    if bit < sub_bits:
        return swapped(value, "sub", bit)
    return swapped(value, "grp", bit - sub_bits)


def pairwise(own_sum, first_bit, span_bits, sub_bits, lower_half):
    for bit in range(first_bit, span_bits):
        own_sum = own_sum + partner(own_sum, bit, sub_bits)
    other_sum = partner(own_sum, span_bits, sub_bits)
    first_half = jnp.where(lower_half, own_sum, other_sum)
    second_half = jnp.where(lower_half, other_sum, own_sum)
    return jnp.concatenate([first_half, second_half], axis=0)


def per_device(right_sides, basis_u, basis_v, coupling):
    highest = lax.Precision.HIGHEST
    sub_bits = lax.axis_size("sub").bit_length() - 1
    all_bits = sub_bits + lax.axis_size("grp").bit_length() - 1
    levels = basis_u.shape[0]
    position = lax.axis_index("grp") * lax.axis_size("sub") + lax.axis_index("sub")
    current = right_sides
    for height in range(levels):
        span_bits = all_bits - levels + height
        v_basis = basis_v[height].astype(jnp.float32)
        own_sum = jnp.einsum("pr,pn->rn", v_basis, current, precision=highest)
        lower_half = jnp.bitwise_and(jnp.right_shift(position, span_bits), 1) == 0
        node_sum = pairwise(own_sum, 0, span_bits, sub_bits, lower_half)
        weights = jnp.dot(coupling[height].astype(jnp.float32), node_sum, precision=highest)
        current = current - jnp.dot(basis_u[height].astype(jnp.float32), weights, precision=highest)
    return current


def solution(mesh):
    in_specs = (
        P(("grp", "sub"), None),
        P(None, ("grp", "sub"), None),
        P(None, ("grp", "sub"), None),
        P(None, ("grp", "sub"), None),
    )
    out_specs = P(("grp", "sub"), None)
    return jax.shard_map(
        per_device, mesh=mesh, in_specs=in_specs, out_specs=out_specs, check_vma=False
    )
```

profile of v0, /device:TPU:0, one launch (start us, length us, event | category | flops | bytes accessed | tf_op | source)
XLA Modules:
  0.0 78.7 jit_solution(15781377082067031790)
XLA Ops:
  0.0 1.6 %fusion.39 = f32[256,128]{1,0:T(8,128)S(1)} fusion(f32[512,128]{1,0:T(8,128)} %param.4, bf16[5,512,256]{2,1,0:T(8,128)(2,1)} %param.6), kind=kOutput, calls=%fused_computation.48 | convolution fusion | flops 201326592 | bytes 655360 | tf_op jit(solution)/shard_map/pr,pn->rn/dot_general | solution.py:38
  3.3 1.4 %fusion.5 = f32[128,256]{1,0:T(8,128)S(1)} fusion(f32[256,128]{1,0:T(8,128)S(1)} %get-tuple-element.14, f32[256,128]{1,0:T(8,128)S(1)} %get-tuple-element.13, bf16[5,256,512]{2,1,0:T(8,128)(2,1)} %param.7), kind=kOutput, calls=%fused_computation.14 | convolution fusion | flops 201392128 | bytes 655360 | tf_op jit(solution)/shard_map/dot_general | solution.py:41
  6.8 2.7 %collective-permute-start.2 = (f32[256,128]{0,1:T(8,128)S(1)}, f32[256,128]{0,1:T(8,128)S(1)}, u32[]{:S(2)}, u32[]{:S(2)}) collective-permute-start(f32[256,128]{0,1:T(8,128)S(1)} %add.34), channel_id=1, source_target_pairs={{0,2},{1,3},{2,0},{3,1},{4,6},{5,7},{6,4},{7,5},{8,10},{9,11},{10,... | collective-permute-start | bytes 393224 | tf_op jit(solution)/shard_map/ppermute | solution.py:10
  9.6 4.0 %collective-permute-done.2 = f32[256,128]{0,1:T(8,128)S(1)} collective-permute-done((f32[256,128]{0,1:T(8,128)S(1)}, f32[256,128]{0,1:T(8,128)S(1)}, u32[]{:S(2)}, u32[]{:S(2)}) %collective-permute-start.2) | collective-permute-done | bytes 131104 | tf_op jit(solution)/shard_map/ppermute | solution.py:10
  13.6 1.4 %fusion.9 = f32[128,256]{1,0:T(8,128)S(1)} fusion(f32[256,128]{0,1:T(8,128)S(1)} %get-tuple-element.12, f32[256,128]{0,1:T(8,128)S(1)} %get-tuple-element.11, bf16[5,256,512]{2,1,0:T(8,128)(2,1)} %param.7), kind=kOutput, calls=%fused_computation.18 | convolution fusion | flops 201392128 | bytes 655360 | tf_op jit(solution)/shard_map/dot_general | solution.py:41
  17.1 1.8 %collective-permute-start.4 = (f32[256,128]{0,1:T(8,128)S(1)}, f32[256,128]{0,1:T(8,128)S(1)}, u32[]{:S(2)}, u32[]{:S(2)}) collective-permute-start(f32[256,128]{0,1:T(8,128)S(1)} %add.35), channel_id=1, source_target_pairs={{0,2},{1,3},{2,0},{3,1},{4,6},{5,7},{6,4},{7,5},{8,10},{9,11},{10,... | collective-permute-start | bytes 393224 | tf_op jit(solution)/shard_map/ppermute | solution.py:10
  18.9 3.8 %collective-permute-done.4 = f32[256,128]{0,1:T(8,128)S(1)} collective-permute-done((f32[256,128]{0,1:T(8,128)S(1)}, f32[256,128]{0,1:T(8,128)S(1)}, u32[]{:S(2)}, u32[]{:S(2)}) %collective-permute-start.4) | collective-permute-done | bytes 131104 | tf_op jit(solution)/shard_map/ppermute | solution.py:10
  22.7 1.9 %collective-permute-start.5 = (f32[256,128]{0,1:T(8,128)S(1)}, f32[256,128]{0,1:T(8,128)S(1)}, u32[]{:S(2)}, u32[]{:S(2)}) collective-permute-start(f32[256,128]{0,1:T(8,128)S(1)} %add.36), channel_id=1, source_target_pairs={{0,4},{1,5},{2,6},{3,7},{4,0},{5,1},{6,2},{7,3},{8,12},{9,13},{10,... | collective-permute-start | bytes 393224 | tf_op jit(solution)/shard_map/ppermute | solution.py:10
  24.6 3.2 %collective-permute-done.5 = f32[256,128]{0,1:T(8,128)S(1)} collective-permute-done((f32[256,128]{0,1:T(8,128)S(1)}, f32[256,128]{0,1:T(8,128)S(1)}, u32[]{:S(2)}, u32[]{:S(2)}) %collective-permute-start.5) | collective-permute-done | bytes 131104 | tf_op jit(solution)/shard_map/ppermute | solution.py:10
  27.8 1.3 %fusion.13 = f32[128,256]{1,0:T(8,128)S(1)} fusion(f32[256,128]{0,1:T(8,128)S(1)} %get-tuple-element.10, f32[256,128]{0,1:T(8,128)S(1)} %get-tuple-element.9, bf16[5,256,512]{2,1,0:T(8,128)(2,1)} %param.7), kind=kOutput, calls=%fused_computation.22 | convolution fusion | flops 201392128 | bytes 655360 | tf_op jit(solution)/shard_map/dot_general | solution.py:41
  31.2 1.8 %collective-permute-start.7 = (f32[256,128]{0,1:T(8,128)S(1)}, f32[256,128]{0,1:T(8,128)S(1)}, u32[]{:S(2)}, u32[]{:S(2)}) collective-permute-start(f32[256,128]{0,1:T(8,128)S(1)} %add.37), channel_id=1, source_target_pairs={{0,2},{1,3},{2,0},{3,1},{4,6},{5,7},{6,4},{7,5},{8,10},{9,11},{10,... | collective-permute-start | bytes 393224 | tf_op jit(solution)/shard_map/ppermute | solution.py:10
  33.0 3.8 %collective-permute-done.7 = f32[256,128]{0,1:T(8,128)S(1)} collective-permute-done((f32[256,128]{0,1:T(8,128)S(1)}, f32[256,128]{0,1:T(8,128)S(1)}, u32[]{:S(2)}, u32[]{:S(2)}) %collective-permute-start.7) | collective-permute-done | bytes 131104 | tf_op jit(solution)/shard_map/ppermute | solution.py:10
  36.9 1.9 %collective-permute-start.8 = (f32[256,128]{0,1:T(8,128)S(1)}, f32[256,128]{0,1:T(8,128)S(1)}, u32[]{:S(2)}, u32[]{:S(2)}) collective-permute-start(f32[256,128]{0,1:T(8,128)S(1)} %add.38), channel_id=1, source_target_pairs={{0,4},{1,5},{2,6},{3,7},{4,0},{5,1},{6,2},{7,3},{8,12},{9,13},{10,... | collective-permute-start | bytes 393224 | tf_op jit(solution)/shard_map/ppermute | solution.py:10
  38.8 3.2 %collective-permute-done.8 = f32[256,128]{0,1:T(8,128)S(1)} collective-permute-done((f32[256,128]{0,1:T(8,128)S(1)}, f32[256,128]{0,1:T(8,128)S(1)}, u32[]{:S(2)}, u32[]{:S(2)}) %collective-permute-start.8) | collective-permute-done | bytes 131104 | tf_op jit(solution)/shard_map/ppermute | solution.py:10
  41.9 2.9 %collective-permute-start.9 = (f32[256,128]{0,1:T(8,128)S(1)}, f32[256,128]{0,1:T(8,128)S(1)}, u32[]{:S(2)}, u32[]{:S(2)}) collective-permute-start(f32[256,128]{0,1:T(8,128)S(1)} %add.39), channel_id=1, source_target_pairs={{0,8},{1,9},{2,10},{3,11},{4,12},{5,13},{6,14},{7,15},{8,0},{9,1},... | collective-permute-start | bytes 393224 | tf_op jit(solution)/shard_map/ppermute | solution.py:10
  44.8 4.6 %collective-permute-done.9 = f32[256,128]{0,1:T(8,128)S(1)} collective-permute-done((f32[256,128]{0,1:T(8,128)S(1)}, f32[256,128]{0,1:T(8,128)S(1)}, u32[]{:S(2)}, u32[]{:S(2)}) %collective-permute-start.9) | collective-permute-done | bytes 131104 | tf_op jit(solution)/shard_map/ppermute | solution.py:10
  49.5 1.4 %fusion.17 = f32[128,256]{1,0:T(8,128)S(1)} fusion(f32[256,128]{0,1:T(8,128)S(1)} %get-tuple-element.8, f32[256,128]{0,1:T(8,128)S(1)} %get-tuple-element.7, bf16[5,256,512]{2,1,0:T(8,128)(2,1)} %param.7), kind=kOutput, calls=%fused_computation.26 | convolution fusion | flops 201392128 | bytes 655360 | tf_op jit(solution)/shard_map/dot_general | solution.py:41
  53.0 1.6 %collective-permute-start.11 = (f32[256,128]{0,1:T(8,128)S(1)}, f32[256,128]{0,1:T(8,128)S(1)}, u32[]{:S(2)}, u32[]{:S(2)}) collective-permute-start(f32[256,128]{0,1:T(8,128)S(1)} %add.40), channel_id=1, source_target_pairs={{0,2},{1,3},{2,0},{3,1},{4,6},{5,7},{6,4},{7,5},{8,10},{9,11},{10,... | collective-permute-start | bytes 393224 | tf_op jit(solution)/shard_map/ppermute | solution.py:10
  54.6 4.0 %collective-permute-done.11 = f32[256,128]{0,1:T(8,128)S(1)} collective-permute-done((f32[256,128]{0,1:T(8,128)S(1)}, f32[256,128]{0,1:T(8,128)S(1)}, u32[]{:S(2)}, u32[]{:S(2)}) %collective-permute-start.11) | collective-permute-done | bytes 131104 | tf_op jit(solution)/shard_map/ppermute | solution.py:10
  59.4 4.2 %collective-permute-done.12 = f32[256,128]{0,1:T(8,128)S(1)} collective-permute-done((f32[256,128]{0,1:T(8,128)S(1)}, f32[256,128]{0,1:T(8,128)S(1)}, u32[]{:S(2)}, u32[]{:S(2)}) %collective-permute-start.12) | collective-permute-done | bytes 131104 | tf_op jit(solution)/shard_map/ppermute | solution.py:10
  63.7 2.2 %collective-permute-start.13 = (f32[256,128]{0,1:T(8,128)S(1)}, f32[256,128]{0,1:T(8,128)S(1)}, u32[]{:S(2)}, u32[]{:S(2)}) collective-permute-start(f32[256,128]{0,1:T(8,128)S(1)} %add.42), channel_id=1, source_target_pairs={{0,8},{1,9},{2,10},{3,11},{4,12},{5,13},{6,14},{7,15},{8,0},{9,1},... | collective-permute-start | bytes 393224 | tf_op jit(solution)/shard_map/ppermute | solution.py:10
  65.8 5.2 %collective-permute-done.13 = f32[256,128]{0,1:T(8,128)S(1)} collective-permute-done((f32[256,128]{0,1:T(8,128)S(1)}, f32[256,128]{0,1:T(8,128)S(1)}, u32[]{:S(2)}, u32[]{:S(2)}) %collective-permute-start.13) | collective-permute-done | bytes 131104 | tf_op jit(solution)/shard_map/ppermute | solution.py:10
  71.0 1.6 %collective-permute-start.14 = (f32[256,128]{0,1:T(8,128)S(1)}, f32[256,128]{0,1:T(8,128)S(1)}, u32[]{:S(2)}, u32[]{:S(2)}) collective-permute-start(f32[256,128]{0,1:T(8,128)S(1)} %add.43), channel_id=1, source_target_pairs={{0,16},{16,0},{1,17},{17,1},{2,18},{18,2},{3,19},{19,3},{4,20},{20... | collective-permute-start | bytes 393224 | tf_op jit(solution)/shard_map/ppermute | solution.py:10
  72.7 3.4 %collective-permute-done.14 = f32[256,128]{0,1:T(8,128)S(1)} collective-permute-done((f32[256,128]{0,1:T(8,128)S(1)}, f32[256,128]{0,1:T(8,128)S(1)}, u32[]{:S(2)}, u32[]{:S(2)}) %collective-permute-start.14) | collective-permute-done | bytes 131104 | tf_op jit(solution)/shard_map/ppermute | solution.py:10
  (42 shorter events, 13.7 us)
Async XLA Ops:
  0.0 4.7 %copy-start = (bf16[5,512,256]{2,1,0:T(8,128)(2,1)S(1)}, bf16[5,512,256]{2,1,0:T(8,128)(2,1)}, u32[]{:S(2)}) copy-start(bf16[5,512,256]{2,1,0:T(8,128)(2,1)} %param.5) | copy-start | bytes 3932164
  1.6 1.7 %collective-permute-start = (f32[256,128]{1,0:T(8,128)S(1)}, f32[256,128]{1,0:T(8,128)S(1)}, u32[]{:S(2)}, u32[]{:S(2)}) collective-permute-start(f32[256,128]{1,0:T(8,128)S(1)} %fusion.39), channel_id=1, source_target_pairs={{0,1},{1,0},{2,3},{3,2},{4,5},{5,4},{6,7},{7,6},{8,9},{9,8},{10,11... | collective-permute-start | bytes 393224 | tf_op jit(solution)/shard_map/ppermute | solution.py:10
  2.1 3.0 %copy-start.1 = (bf16[5,512,256]{2,1,0:T(8,128)(2,1)S(1)}, bf16[5,512,256]{2,1,0:T(8,128)(2,1)}, u32[]{:S(2)}) copy-start(bf16[5,512,256]{2,1,0:T(8,128)(2,1)} %param.6) | copy-start | bytes 3932164
  5.4 1.4 %collective-permute-start.1 = (f32[256,128]{0,1:T(8,128)S(1)}, f32[256,128]{0,1:T(8,128)S(1)}, u32[]{:S(2)}, u32[]{:S(2)}) collective-permute-start(f32[256,128]{0,1:T(8,128)S(1)} %convolution_bitcast_fusion.8), channel_id=1, source_target_pairs={{0,1},{1,0},{2,3},{3,2},{4,5},{5,4},{6,7},{7,6},{8,9},{9,8},{10,11... | collective-permute-start | bytes 393224 | tf_op jit(solution)/shard_map/ppermute | solution.py:10
  6.8 6.7 %collective-permute-start.2 = (f32[256,128]{0,1:T(8,128)S(1)}, f32[256,128]{0,1:T(8,128)S(1)}, u32[]{:S(2)}, u32[]{:S(2)}) collective-permute-start(f32[256,128]{0,1:T(8,128)S(1)} %add.34), channel_id=1, source_target_pairs={{0,2},{1,3},{2,0},{3,1},{4,6},{5,7},{6,4},{7,5},{8,10},{9,11},{10,... | collective-permute-start | bytes 393224 | tf_op jit(solution)/shard_map/ppermute | solution.py:10
  15.6 1.4 %collective-permute-start.3 = (f32[256,128]{0,1:T(8,128)S(1)}, f32[256,128]{0,1:T(8,128)S(1)}, u32[]{:S(2)}, u32[]{:S(2)}) collective-permute-start(f32[256,128]{0,1:T(8,128)S(1)} %convolution_bitcast_fusion.7), channel_id=1, source_target_pairs={{0,1},{1,0},{2,3},{3,2},{4,5},{5,4},{6,7},{7,6},{8,9},{9,8},{10,11... | collective-permute-start | bytes 393224 | tf_op jit(solution)/shard_map/ppermute | solution.py:10
  17.1 5.6 %collective-permute-start.4 = (f32[256,128]{0,1:T(8,128)S(1)}, f32[256,128]{0,1:T(8,128)S(1)}, u32[]{:S(2)}, u32[]{:S(2)}) collective-permute-start(f32[256,128]{0,1:T(8,128)S(1)} %add.35), channel_id=1, source_target_pairs={{0,2},{1,3},{2,0},{3,1},{4,6},{5,7},{6,4},{7,5},{8,10},{9,11},{10,... | collective-permute-start | bytes 393224 | tf_op jit(solution)/shard_map/ppermute | solution.py:10
  22.7 5.0 %collective-permute-start.5 = (f32[256,128]{0,1:T(8,128)S(1)}, f32[256,128]{0,1:T(8,128)S(1)}, u32[]{:S(2)}, u32[]{:S(2)}) collective-permute-start(f32[256,128]{0,1:T(8,128)S(1)} %add.36), channel_id=1, source_target_pairs={{0,4},{1,5},{2,6},{3,7},{4,0},{5,1},{6,2},{7,3},{8,12},{9,13},{10,... | collective-permute-start | bytes 393224 | tf_op jit(solution)/shard_map/ppermute | solution.py:10
  29.8 1.4 %collective-permute-start.6 = (f32[256,128]{0,1:T(8,128)S(1)}, f32[256,128]{0,1:T(8,128)S(1)}, u32[]{:S(2)}, u32[]{:S(2)}) collective-permute-start(f32[256,128]{0,1:T(8,128)S(1)} %convolution_bitcast_fusion.6), channel_id=1, source_target_pairs={{0,1},{1,0},{2,3},{3,2},{4,5},{5,4},{6,7},{7,6},{8,9},{9,8},{10,11... | collective-permute-start | bytes 393224 | tf_op jit(solution)/shard_map/ppermute | solution.py:10
  31.2 5.6 %collective-permute-start.7 = (f32[256,128]{0,1:T(8,128)S(1)}, f32[256,128]{0,1:T(8,128)S(1)}, u32[]{:S(2)}, u32[]{:S(2)}) collective-permute-start(f32[256,128]{0,1:T(8,128)S(1)} %add.37), channel_id=1, source_target_pairs={{0,2},{1,3},{2,0},{3,1},{4,6},{5,7},{6,4},{7,5},{8,10},{9,11},{10,... | collective-permute-start | bytes 393224 | tf_op jit(solution)/shard_map/ppermute | solution.py:10
  36.9 5.0 %collective-permute-start.8 = (f32[256,128]{0,1:T(8,128)S(1)}, f32[256,128]{0,1:T(8,128)S(1)}, u32[]{:S(2)}, u32[]{:S(2)}) collective-permute-start(f32[256,128]{0,1:T(8,128)S(1)} %add.38), channel_id=1, source_target_pairs={{0,4},{1,5},{2,6},{3,7},{4,0},{5,1},{6,2},{7,3},{8,12},{9,13},{10,... | collective-permute-start | bytes 393224 | tf_op jit(solution)/shard_map/ppermute | solution.py:10
  41.9 7.5 %collective-permute-start.9 = (f32[256,128]{0,1:T(8,128)S(1)}, f32[256,128]{0,1:T(8,128)S(1)}, u32[]{:S(2)}, u32[]{:S(2)}) collective-permute-start(f32[256,128]{0,1:T(8,128)S(1)} %add.39), channel_id=1, source_target_pairs={{0,8},{1,9},{2,10},{3,11},{4,12},{5,13},{6,14},{7,15},{8,0},{9,1},... | collective-permute-start | bytes 393224 | tf_op jit(solution)/shard_map/ppermute | solution.py:10
  51.5 1.4 %collective-permute-start.10 = (f32[256,128]{0,1:T(8,128)S(1)}, f32[256,128]{0,1:T(8,128)S(1)}, u32[]{:S(2)}, u32[]{:S(2)}) collective-permute-start(f32[256,128]{0,1:T(8,128)S(1)} %convolution_bitcast_fusion.5), channel_id=1, source_target_pairs={{0,1},{1,0},{2,3},{3,2},{4,5},{5,4},{6,7},{7,6},{8,9},{9,8},{10,11... | collective-permute-start | bytes 393224 | tf_op jit(solution)/shard_map/ppermute | solution.py:10
  53.0 5.6 %collective-permute-start.11 = (f32[256,128]{0,1:T(8,128)S(1)}, f32[256,128]{0,1:T(8,128)S(1)}, u32[]{:S(2)}, u32[]{:S(2)}) collective-permute-start(f32[256,128]{0,1:T(8,128)S(1)} %add.40), channel_id=1, source_target_pairs={{0,2},{1,3},{2,0},{3,1},{4,6},{5,7},{6,4},{7,5},{8,10},{9,11},{10,... | collective-permute-start | bytes 393224 | tf_op jit(solution)/shard_map/ppermute | solution.py:10
  58.6 5.0 %collective-permute-start.12 = (f32[256,128]{0,1:T(8,128)S(1)}, f32[256,128]{0,1:T(8,128)S(1)}, u32[]{:S(2)}, u32[]{:S(2)}) collective-permute-start(f32[256,128]{0,1:T(8,128)S(1)} %add.41), channel_id=1, source_target_pairs={{0,4},{1,5},{2,6},{3,7},{4,0},{5,1},{6,2},{7,3},{8,12},{9,13},{10,... | collective-permute-start | bytes 393224 | tf_op jit(solution)/shard_map/ppermute | solution.py:10
  63.7 7.3 %collective-permute-start.13 = (f32[256,128]{0,1:T(8,128)S(1)}, f32[256,128]{0,1:T(8,128)S(1)}, u32[]{:S(2)}, u32[]{:S(2)}) collective-permute-start(f32[256,128]{0,1:T(8,128)S(1)} %add.42), channel_id=1, source_target_pairs={{0,8},{1,9},{2,10},{3,11},{4,12},{5,13},{6,14},{7,15},{8,0},{9,1},... | collective-permute-start | bytes 393224 | tf_op jit(solution)/shard_map/ppermute | solution.py:10
  71.0 5.0 %collective-permute-start.14 = (f32[256,128]{0,1:T(8,128)S(1)}, f32[256,128]{0,1:T(8,128)S(1)}, u32[]{:S(2)}, u32[]{:S(2)}) collective-permute-start(f32[256,128]{0,1:T(8,128)S(1)} %add.43), channel_id=1, source_target_pairs={{0,16},{16,0},{1,17},{17,1},{2,18},{18,2},{3,19},{19,3},{4,20},{20... | collective-permute-start | bytes 393224 | tf_op jit(solution)/shard_map/ppermute | solution.py:10
where the time goes:
time: 79 us; the launch traced here: 78.7 us
  waiting for transfers between devices  44.6 us (56%)
  starting transfers between devices  20.1 us (25%)
  matrix products  11.4 us (14%)
  local copies, waits for them, and re-layouts  2.02 us (3%)
    ppermute x15, waiting for transfers between devices, swapped(): return lax.ppermute(value, axis, pairs)  44.6 us
    ppermute x15, starting transfers between devices, swapped(): return lax.ppermute(value, axis, pairs)  20.1 us
    dot_general x5, matrix products, per_device(): jnp.dot(coupling[height].astype(jnp.float32), node_sum, precision=highest)  6.75 us
    dot_general x5, matrix products, per_device(): own_sum = jnp.einsum('pr,pn->rn', v_basis, current, precision=highest)  2.67 us
    dot_general x5, matrix products, per_device(): jnp.dot(basis_u[height].astype(jnp.float32), weights, precision=highest)  1.97 us
  transfers between devices with their start and end apart: 15, of which 14 were waited for; matrix products, arithmetic and copies ran while one was open for 2% of the time, Pallas kernels for 0%

commit v1 on v0

v1 whole, which is shorter than its diff:
```python
import functools

import jax
import jax.numpy as jnp
from jax import lax
from jax.experimental import pallas as pl
from jax.experimental.pallas import tpu as pltpu
from jax.sharding import PartitionSpec as P

F32 = jnp.float32
BF16 = jnp.bfloat16
AXES = ("grp", "sub")


def swapped(value, axis, bit):
    mask = 2**bit
    pairs = [(source, source ^ mask) for source in range(lax.axis_size(axis))]
    return lax.ppermute(value, axis, pairs)


def partner(value, bit, sub_bits):
    if bit < sub_bits:
        return swapped(value, "sub", bit)
    return swapped(value, "grp", bit - sub_bits)


def pairwise(own_sum, first_bit, span_bits, sub_bits, lower_half):
    for bit in range(first_bit, span_bits):
        own_sum = own_sum + partner(own_sum, bit, sub_bits)
    other_sum = partner(own_sum, span_bits, sub_bits)
    first_half = jnp.where(lower_half, own_sum, other_sum)
    second_half = jnp.where(lower_half, other_sum, own_sum)
    return jnp.concatenate([first_half, second_half], axis=0)


def bit_by_bit(right_sides, basis_u, basis_v, coupling):
    highest = lax.Precision.HIGHEST
    sub_bits = lax.axis_size("sub").bit_length() - 1
    all_bits = sub_bits + lax.axis_size("grp").bit_length() - 1
    levels = basis_u.shape[0]
    position = lax.axis_index("grp") * lax.axis_size("sub") + lax.axis_index("sub")
    current = right_sides
    for height in range(levels):
        span_bits = all_bits - levels + height
        v_basis = basis_v[height].astype(F32)
        own_sum = jnp.einsum("pr,pn->rn", v_basis, current, precision=highest)
        lower_half = jnp.bitwise_and(jnp.right_shift(position, span_bits), 1) == 0
        node_sum = pairwise(own_sum, 0, span_bits, sub_bits, lower_half)
        weights = jnp.dot(coupling[height].astype(F32), node_sum, precision=highest)
        current = current - jnp.dot(basis_u[height].astype(F32), weights, precision=highest)
    return current


def split(value):
    high = value.astype(BF16)
    low = (value - high.astype(F32)).astype(BF16)
    return high, low


def stacked(value):
    return jnp.concatenate(split(value), axis=0)


def folded(value):
    half = value.shape[0] // 2
    return value[:half] + value[half:]


def dot(left, right):
    return lax.dot_general(left, right, (((1,), (0,)), ((), ())), preferred_element_type=F32)


def dot_transposed(left, right):
    return lax.dot_general(left, right, (((1,), (1,)), ((), ())), preferred_element_type=F32)


def weights_of(lower, upper, couple):
    rank = couple.shape[0]
    lower, upper = stacked(lower), stacked(upper)
    return folded(dot_transposed(lower, couple[:, :rank]) + dot_transposed(upper, couple[:, rank:]))


def correction(weights, cross):
    high, low = split(cross)
    both = stacked(weights)
    return folded(dot(both, high) + dot(both, low))


def bit_is_set(axis, bit):
    return jnp.bitwise_and(jnp.right_shift(lax.axis_index(axis), bit), 1) == 1


def ordered(flag, own, other):
    return jnp.where(flag, other, own), jnp.where(flag, own, other)


def start_kernel(right_hbm, u_hbm, v_hbm, c_hbm, current_ref, sum_ref, u_ref, v_ref, c_ref, right_ref,
                 first_ref, sems):
    sources = [right_hbm, v_hbm.at[0], v_hbm.at[1], u_hbm.at[0], c_hbm.at[0]]
    targets = [right_ref, first_ref, v_ref, u_ref, c_ref]
    copies = [pltpu.make_async_copy(*pair, sems.at[place]) for place, pair in enumerate(zip(sources, targets))]
    for copy in copies:
        copy.start()
    copies[0].wait()
    current = right_ref[...].T
    current_ref[...] = current
    copies[1].wait()
    sum_ref[...] = folded(dot(stacked(current), first_ref[...]))
    for copy in copies[2:]:
        copy.wait()


def first_sum_kernel(current_ref, u_ref, v_ref, sum_ref, cross_ref):
    sum_ref[...] = folded(dot(stacked(current_ref[...]), v_ref[...]))
    cross_ref[...] = dot(u_ref[...].T, v_ref[...])


def pair_kernel(own_ref, other_ref, c_ref, sum_ref, cross_ref, weights_ref, keep_ref, send_ref):
    upper_core = bit_is_set("sub", 0)
    half = keep_ref.shape[0]
    weights = weights_of(*ordered(upper_core, own_ref[...], other_ref[...]), c_ref[...])
    weights_ref[...] = weights
    later = sum_ref[...] - correction(weights, cross_ref[...])
    keep_ref[...], send_ref[...] = ordered(upper_core, later[:half], later[half:])


def later_sums_kernel(current_ref, weights_ref, u_ref, v_ref, keep_ref, send_ref):
    upper_core = bit_is_set("sub", 0)
    half = keep_ref.shape[1]
    current = current_ref[...] - folded(dot_transposed(stacked(weights_ref[...]), u_ref[0]))
    current = stacked(current)
    for place in range(keep_ref.shape[0]):
        later = folded(dot(current, v_ref[place + 2]))
        keep_ref[place], send_ref[place] = ordered(upper_core, later[:half], later[half:])


def cross_kernel(u_ref, v_ref, early_ref, late_ref, keep_ref, send_ref):
    upper_core = bit_is_set("sub", 0)
    first, second, third = u_ref[1].T, u_ref[2].T, u_ref[3].T
    early_ref[0] = dot(first, v_ref[2])
    early_ref[1] = dot(first, v_ref[3])
    late_ref[0] = dot(first, v_ref[4])
    late_ref[1] = dot(second, v_ref[4])
    keep_ref[...], send_ref[...] = ordered(upper_core, dot(second, v_ref[3]), dot(third, v_ref[4]))


def first_weights_kernel(own_ref, across_ref, c_ref, weights_ref):
    lower, upper = ordered(bit_is_set("sub", 1), own_ref[...], across_ref[...])
    weights_ref[...] = weights_of(lower, upper, c_ref[1])


def square_weights_kernel(level, axis, bit, own_count, *refs):
    *part_refs, c_ref, weights_ref = refs
    parts = [ref[0] if len(ref.shape) == 3 else ref[...] for ref in part_refs]
    own, other = sum(parts[1:own_count], parts[0]), sum(parts[own_count + 1 :], parts[own_count])
    weights_ref[...] = weights_of(*ordered(bit_is_set(axis, bit), own, other), c_ref[level])


def in_turn(first, second):
    return ordered(bit_is_set("sub", 0), first, second)


def second_weights_kernel(own_ref, first_ref, second_ref, both_ref, c_ref, weights_ref):
    beside, across = in_turn(first_ref[0], second_ref[0])
    own, other = own_ref[...] + beside, across + both_ref[...]
    weights_ref[...] = weights_of(*ordered(bit_is_set("sub", 2), own, other), c_ref[2])


def second_third_kernel(weights_ref, early_ref, got_ref, sums_ref, got_sums_ref, second_ref, pair_ref):
    weights = weights_ref[...]
    second_ref[...] = sums_ref[0] + got_sums_ref[0] - correction(weights, early_ref[0] + got_ref[0])
    pair_ref[0] = second_ref[...]
    pair_ref[1] = sums_ref[1] + got_sums_ref[1] - correction(weights, early_ref[1] + got_ref[1])


def fourth_kernel(weights_ref, late_ref, got_ref, sums_ref, got_sums_ref, fourth_ref, cross_ref):
    fourth_ref[...] = sums_ref[2] + got_sums_ref[2] - correction(weights_ref[...], late_ref[0] + got_ref[0])
    cross_ref[...] = late_ref[1] + got_ref[1]


def third_fourth_kernel(weights_ref, mixed_ref, mixed_got_ref, pair_ref, first_ref, second_ref, fourth_ref, cross_ref,
                        third_ref, later_ref):
    weights = weights_ref[...]
    cross, _ = ordered(bit_is_set("sub", 0), mixed_ref[...], mixed_got_ref[...])
    beside, _ = in_turn(first_ref[1], second_ref[1])
    third_ref[...] = pair_ref[1] + beside - correction(weights, cross)
    later_ref[...] = fourth_ref[...] - correction(weights, cross_ref[...])


def last_sum_kernel(weights_ref, sum_ref, cross_ref, cross_got_ref, later_ref):
    _, cross = ordered(bit_is_set("sub", 0), cross_ref[...], cross_got_ref[...])
    later_ref[...] = sum_ref[...] - correction(weights_ref[...], cross)


def stack_kernel(first_ref, second_ref, third_ref, out_ref):
    out_ref[0], out_ref[1], out_ref[2] = first_ref[...], second_ref[...], third_ref[...]


def columns_of(own, other):
    lower, upper = ordered(bit_is_set("sub", 0), own, other)
    return jnp.concatenate(split(jnp.concatenate([lower, upper], axis=0).T), axis=1)


def fold_columns(value):
    half = value.shape[1] // 2
    return value[:, :half] + value[:, half:]


def gather_kernel(right_ref, u_ref, first_ref, own_ref, other_ref, out_ref):
    total = dot(u_ref[0], jnp.concatenate(split(first_ref[...].T), axis=1))
    for place in range(own_ref.shape[0]):
        total = total + dot(u_ref[place + 1], columns_of(own_ref[place], other_ref[place]))
    out_ref[...] = right_ref[...] - fold_columns(total)


def last_kernel(level, chunks, partial_ref, own_ref, other_ref, u_ref, out_hbm, out_ref, sems):
    weights = columns_of(own_ref[...], other_ref[...])
    rows = out_ref.shape[0] // chunks
    copies = []
    for place in range(chunks):
        part = pl.ds(place * rows, rows)
        out_ref[part] = partial_ref[part] - fold_columns(dot(u_ref[level, part], weights))
        copies.append(pltpu.make_async_copy(out_ref.at[part], out_hbm.at[part], sems.at[place]))
        copies[-1].start()
    for copy in copies:
        copy.wait()


def run_last(level, partial, own, other, basis_u):
    vmem, chunks = pl.BlockSpec(memory_space=pltpu.VMEM), 4
    return pl.pallas_call(
        functools.partial(last_kernel, level, chunks),
        out_shape=jax.ShapeDtypeStruct(partial.shape, F32),
        in_specs=[vmem] * 4,
        out_specs=pl.BlockSpec(memory_space=pl.ANY),
        scratch_shapes=[pltpu.VMEM(partial.shape, F32), pltpu.SemaphoreType.DMA((chunks,))],
        compiler_params=pltpu.CompilerParams(vmem_limit_bytes=2 * 2**20),
    )(partial, own, other, basis_u)


def run(kernel, outs, *args, after=(), flops=0):
    vmem, unread = pl.BlockSpec(memory_space=pltpu.VMEM), pl.BlockSpec(memory_space=pl.ANY)
    return pl.pallas_call(
        lambda *refs: kernel(*refs[: len(args)], *refs[len(args) + len(after) :]),
        out_shape=[jax.ShapeDtypeStruct(shape, F32) for shape in outs],
        in_specs=[vmem] * len(args) + [unread] * len(after),
        out_specs=[vmem] * len(outs),
        cost_estimate=pl.CostEstimate(flops=flops, bytes_accessed=0, transcendentals=0) if flops else None,
        compiler_params=pltpu.CompilerParams(vmem_limit_bytes=2 * 2**20),
    )(*args, *after)


def add_kernel(first_ref, second_ref, out_ref):
    out_ref[...] = first_ref[...] + second_ref[...]


def first_of_kernel(first_ref, second_ref, out_ref):
    out_ref[...] = first_ref[...] + second_ref[0]


def added(first, second, **options):
    return run(add_kernel, [first.shape], first, second, **options)[0]


def run_start(right_sides, basis_u, basis_v, coupling):
    columns, (points, rank) = right_sides.shape[1], basis_u.shape[1:]
    shape = jax.ShapeDtypeStruct
    arrays = [pltpu.with_memory_space_constraint(value, pltpu.HBM)
              for value in (right_sides, basis_u, basis_v, coupling)]
    outs = [shape((columns, points), F32), shape((columns, rank), F32), shape((points, rank), BF16),
            shape((points, rank), BF16), shape(coupling.shape[1:], BF16), shape((points, columns), F32)]
    return pl.pallas_call(
        start_kernel,
        out_shape=outs,
        in_specs=[pl.BlockSpec(memory_space=pl.ANY)] * len(arrays),
        out_specs=[pl.BlockSpec(memory_space=pltpu.VMEM)] * len(outs),
        scratch_shapes=[pltpu.VMEM((points, rank), BF16), pltpu.SemaphoreType.DMA((5,))],
        compiler_params=pltpu.CompilerParams(vmem_limit_bytes=4 * 2**20),
    )(*arrays)


def tied(value, *others):
    return lax.optimization_barrier((value,) + others)[0]


def traded(value, mask):
    if mask < lax.axis_size("sub"):
        return lax.ppermute(value, "sub", [(source, source ^ mask) for source in range(lax.axis_size("sub"))])
    devices = lax.axis_size("grp") * lax.axis_size("sub")
    return lax.ppermute(value, AXES, [(source, source ^ mask) for source in range(devices)])


def crossed(value, even, odd):
    pairs = [(source, source ^ (odd if source & 1 else even)) for source in range(lax.axis_size("sub"))]
    return lax.ppermute(value, "sub", pairs)


def tree(right_sides, basis_u, basis_v, coupling):
    points, rank = basis_u.shape[1:]
    columns = right_sides.shape[1]
    half = columns // 2
    square, block = (rank, rank), (half, rank)

    current, own, u_first, v_second, couple, right_near = run_start(right_sides, basis_u, basis_v, coupling)
    other = traded(own, 1)
    first_sum, first_cross = run(first_sum_kernel, [(columns, rank), square], current, u_first, v_second)
    weights0, keep, send = run(
        pair_kernel, [(columns, rank), block, block], own, other, couple, first_sum, first_cross
    )
    got = traded(send, 1)
    early, late, keep_cross, send_cross = run(
        cross_kernel, [(2,) + square, (2,) + square, square, square], basis_u, basis_v, after=[weights0], flops=2 * 10**9
    )
    sums, sums_send = run(
        later_sums_kernel, [(3,) + block, (3,) + block], current, weights0, basis_u, basis_v,
        after=[keep_cross], flops=2 * 10**9,
    )
    sum1 = added(keep, got, after=[sums])

    across = traded(sum1, 2)
    cross_got = traded(tied(send_cross, sum1), 1)
    early_got = traded(tied(early, sum1), 1)
    sums_got = traded(tied(sums_send, sum1), 1)
    late_got = traded(tied(late, sum1), 1)
    mixed = added(keep_cross, cross_got, flops=2 * 10**9)
    mixed_across = crossed(mixed, 2, 4)
    (weights1,) = run(first_weights_kernel, [block], sum1, across, coupling, flops=8 * 10**9)
    second, pair = run(
        second_third_kernel, [block, (2,) + block], weights1, early, early_got, sums, sums_got
    )

    both, first_turn, second_turn = traded(second, 6), crossed(pair, 2, 4), crossed(pair, 4, 2)
    fourth, cross42 = run(
        fourth_kernel, [block, square], weights1, late, late_got, sums, sums_got, flops=2 * 10**9
    )
    mixed = added(mixed, mixed_across, after=[fourth])
    mixed_got = traded(mixed, 1)
    (weights2,) = run(
        second_weights_kernel, [block], second, first_turn, second_turn, both, coupling, flops=8 * 10**9
    )
    odd = [(source, source ^ 2) for source in range(1, lax.axis_size("sub"), 2)]
    cross43_got = lax.ppermute(mixed, "sub", odd)
    third, later4 = run(
        third_fourth_kernel, [block, block],
        weights2, mixed, mixed_got, pair, first_turn, second_turn, fourth, cross42,
    )

    sum4 = added(later4, traded(later4, 2), after=[third])
    sum4_got = traded(sum4, 4)
    both, across, beside = traded(third, 12), traded(third, 8), traded(third, 4)
    cross43 = added(mixed, cross43_got, after=[third])
    cross43_got = traded(cross43, 1)
    (weights3,) = run(
        functools.partial(square_weights_kernel, 3, "sub", 3, 2), [block], third, beside, across, both, coupling
    )
    sum4 = added(sum4, sum4_got, after=[weights3], flops=8 * 10**9)
    (sum4,) = run(last_sum_kernel, [block], weights3, sum4, cross43, cross43_got)

    both, beside, across = traded(sum4, 24), traded(sum4, 8), traded(sum4, 16)
    (three,) = run(stack_kernel, [(3,) + block], weights1, weights2, weights3, after=[sum4])
    three_got = traded(three, 1)
    (partial,) = run(
        gather_kernel, [(points, columns)], right_near, basis_u, weights0, three, three_got, flops=2 * 10**9
    )
    own_sum = added(sum4, beside, after=[both], flops=4 * 10**9)
    (weights4,) = run(
        functools.partial(square_weights_kernel, 4, "grp", 0, 1), [block], own_sum, across, both, coupling
    )
    return run_last(4, partial, weights4, traded(weights4, 1), basis_u)


def solution(mesh):
    n_grp, n_sub = mesh.shape["grp"], mesh.shape["sub"]

    def per_device(right_sides, basis_u, basis_v, coupling):
        if basis_u.shape[0] == 5 and n_grp == 2 and n_sub == 16:
            return tree(right_sides, basis_u, basis_v, coupling)
        return bit_by_bit(right_sides, basis_u, basis_v, coupling)

    in_specs = (P(AXES, None), P(None, AXES, None), P(None, AXES, None), P(None, AXES, None))
    return jax.shard_map(
        per_device, mesh=mesh, in_specs=in_specs, out_specs=P(AXES, None), check_vma=False
    )
```

time: 79 us -> 43.2 us (0.55)
  waiting for transfers between devices: 44.6 us -> 15.2 us
  matrix products: 11.4 us -> 0 us
  Pallas kernels: 0 us -> 7.05 us
  local copies, waits for them, and re-layouts: 2.02 us -> 0.01 us
    ppermute x15 -> x24, waiting for transfers between devices: 44.6 us -> 15.2 us  [the longest x18 10.5 us: traded(): lax.ppermute(value, 'sub', [(source, source ^ mask) for source in range(l...]
    dot_general x15 -> x0, matrix products: 11.4 us -> none  [the longest x5 6.75 us: per_device(): jnp.dot(coupling[height].astype(jnp.float32), node_sum, precision=highest)]
    pallas_call x0 -> x23, Pallas kernels: none -> 7.05 us  [the longest x21 4.56 us: run(): pl.pallas_call(lambda *refs: kernel(*refs[:len(args)], *refs[len(args) +...]
    unnamed x5 -> x6, local copies, waits for them, and re-layouts: 1.19 us -> 0.01 us
    sub x1 -> x0, local copies, waits for them, and re-layouts: 0.84 us -> none  [per_device(): current - jnp.dot(basis_u[height].astype(jnp.float32), weights, precision...]
    ppermute x15 -> x24, starting transfers between devices: 20.1 us -> 20.6 us  [the longest x18 12.7 us: traded(): lax.ppermute(value, 'sub', [(source, source ^ mask) for source in range(l...]
  transfers between devices with their start and end apart: 15 -> 24, of which waited for: 14 -> 10; matrix products, arithmetic and copies ran while one was open for 2% -> 0% of each run, Pallas kernels for 0% -> 9%
where the time goes in v1:
time: 43.2 us; the launch traced here: 43.1 us
  starting transfers between devices  20.6 us (48%)
  waiting for transfers between devices  15.2 us (35%)
  Pallas kernels  7.05 us (16%)
    ppermute x18, starting transfers between devices, traded(): lax.ppermute(value, 'sub', [(source, source ^ mask) for source in range(l...  12.7 us
    ppermute x18, waiting for transfers between devices, traded(): lax.ppermute(value, 'sub', [(source, source ^ mask) for source in range(l...  10.5 us
    pallas_call x21, Pallas kernels, run(): pl.pallas_call(lambda *refs: kernel(*refs[:len(args)], *refs[len(args) +...  4.56 us
    ppermute x3, starting transfers between devices, crossed(): return lax.ppermute(value, 'sub', pairs)  4.21 us
    ppermute x2, waiting for transfers between devices, traded(): lax.ppermute(value, AXES, [(source, source ^ mask) for source in range(de...  3 us
    ppermute x2, starting transfers between devices, traded(): lax.ppermute(value, AXES, [(source, source ^ mask) for source in range(de...  2.95 us
    ppermute x3, waiting for transfers between devices, crossed(): return lax.ppermute(value, 'sub', pairs)  1.64 us
    pallas_call x1, Pallas kernels, run_start(): pl.pallas_call(start_kernel, out_shape=outs, in_specs=[pl.BlockSpec(memor...  1.47 us
  transfers between devices with their start and end apart: 24, of which 10 were waited for; matrix products, arithmetic and copies ran while one was open for 0% of the time, Pallas kernels for 9%

profile of v1, /device:TPU:0, one launch (start us, length us, event | category | flops | bytes accessed | tf_op | source)
XLA Modules:
  0.0 43.1 jit_solution(3781950961367036537)
XLA Ops:
  0.0 1.5 %shard_map.46 = (f32[128,512]{1,0:T(8,128)S(1)}, f32[128,256]{1,0:T(8,128)S(1)}, bf16[512,256]{1,0:T(8,128)(2,1)S(1)}, bf16[512,256]{1,0:T(8,128)(2,1)S(1)}, bf1...) custom-call(f32[512,128]{1,0:T(8,128)} %right_hbm.1, bf16[5,512,256]{2,1,0:T(8,128)(2,1)} %u_ref.1, ...), custom_call_target="tpu_custom_call" | custom-call | tf_op jit(solution)/shard_map/pallas_call | solution.py:272
  2.3 0.7 %collective-permute-done.refs_1_ = f32[128,256]{1,0:T(8,128)S(1)} collective-permute-done((f32[128,256]{1,0:T(8,128)S(1)}, f32[128,256]{1,0:T(8,128)S(1)}, u32[]{:S(2)}, u32[]{:S(2)}) %collective-permute-start) | collective-permute-done | bytes 131104 | tf_op jit(solution)/shard_map/ppermute | solution.py:288
  4.0 0.6 %shard_map.49 = (f32[2,256,256]{2,1,0:T(8,128)S(1)}, f32[2,256,256]{2,1,0:T(8,128)S(1)}, f32[256,256]{1,0:T(8,128)S(1)}, f32[256,256]{1,0:T(8,128)S(1)}) custom-call(bf16[5,512,256]{2,1,0:T(8,128)(2,1)S(1)} %copy-done.1, bf16[5,512,256]{2,1,0:T(8,128)(2,1)S(1)} %copy-done.2, f32[128,256]{1,0:T(8,128)S(1)} %get-tuple-element.40.refs_2_.refs_1_), custom_call_target="tpu_custom_call" | custom-call | flops 2000000000 | tf_op jit(solution)/shard_map/pallas_call | solution.py:243
  4.6 0.6 %shard_map.50 = (f32[3,64,256]{2,1,0:T(8,128)S(1)}, f32[3,64,256]{2,1,0:T(8,128)S(1)}) custom-call(f32[128,512]{1,0:T(8,128)S(1)} %get-tuple-element.35.refs_0_, f32[128,256]{1,0:T(8,128)S(1)} %get-tuple-element.40.refs_2_.refs_1_, bf16[5,512,256]{2,1,0:T(8,128)(2,1)S(1)} %copy-done.1, bf16[5,512,256]{2,1,0:T(8,128)(2,1)S(1)} %copy-done.2, ...), custom_call_target="tpu_custom_call" | custom-call | flops 2000000000 | tf_op jit(solution)/shard_map/pallas_call | solution.py:243
  5.4 2.9 %collective-permute-start.2 = (f32[64,256]{1,0:T(8,128)S(1)}, f32[64,256]{1,0:T(8,128)S(1)}, u32[]{:S(2)}, u32[]{:S(2)}) collective-permute-start(f32[64,256]{1,0:T(8,128)S(1)} %shard_map.51.refs_0_), channel_id=1, source_target_pairs={{0,2},{1,3},{2,0},{3,1},{4,6},{5,7},{6,4},{7,5},{8,10},{9,11},{10,... | collective-permute-start | bytes 196616 | tf_op jit(solution)/shard_map/ppermute | solution.py:288
  8.9 0.7 %collective-permute-start.9 = (f32[256,256]{1,0:T(8,128)S(1)}, f32[256,256]{1,0:T(8,128)S(1)}, u32[]{:S(2)}, u32[]{:S(2)}) collective-permute-start(f32[256,256]{1,0:T(8,128)S(1)} %shard_map.55.refs_0_), channel_id=1, source_target_pairs={{0,2},{1,5},{2,0},{3,7},{4,6},{5,1},{6,4},{7,3},{8,10},{9,13},{10,... | collective-permute-start | bytes 786440 | tf_op jit(solution)/shard_map/ppermute | solution.py:295
  9.6 1.1 %collective-permute-done.2.refs_1_ = f32[64,256]{1,0:T(8,128)S(1)} collective-permute-done((f32[64,256]{1,0:T(8,128)S(1)}, f32[64,256]{1,0:T(8,128)S(1)}, u32[]{:S(2)}, u32[]{:S(2)}) %collective-permute-start.2) | collective-permute-done | bytes 65568 | tf_op jit(solution)/shard_map/ppermute | solution.py:288
  11.2 2.0 %collective-permute-start.6 = (f32[2,64,256]{2,1,0:T(8,128)S(1)}, f32[2,64,256]{2,1,0:T(8,128)S(1)}, u32[]{:S(2)}, u32[]{:S(2)}) collective-permute-start(f32[2,64,256]{2,1,0:T(8,128)S(1)} %get-tuple-element.50.refs_3_), channel_id=1, source_target_pairs={{0,4},{1,3},{2,6},{3,1},{4,0},{5,7},{6,2},{7,5},{8,12},{9,11},{10,... | collective-permute-start | bytes 393224 | tf_op jit(solution)/shard_map/ppermute | solution.py:295
  13.2 1.5 %collective-permute-start.5 = (f32[2,64,256]{2,1,0:T(8,128)S(1)}, f32[2,64,256]{2,1,0:T(8,128)S(1)}, u32[]{:S(2)}, u32[]{:S(2)}) collective-permute-start(f32[2,64,256]{2,1,0:T(8,128)S(1)} %get-tuple-element.50.refs_3_), channel_id=1, source_target_pairs={{0,2},{1,5},{2,0},{3,7},{4,6},{5,1},{6,4},{7,3},{8,10},{9,13},{10,... | collective-permute-start | bytes 393224 | tf_op jit(solution)/shard_map/ppermute | solution.py:295
  15.0 1.6 %collective-permute-done.9.refs_1_ = f32[256,256]{1,0:T(8,128)S(1)} collective-permute-done((f32[256,256]{1,0:T(8,128)S(1)}, f32[256,256]{1,0:T(8,128)S(1)}, u32[]{:S(2)}, u32[]{:S(2)}) %collective-permute-start.9) | collective-permute-done | bytes 262176 | tf_op jit(solution)/shard_map/ppermute | solution.py:295
  16.7 0.7 %collective-permute-start.17 = (f32[256,256]{1,0:T(8,128)S(1)}, f32[256,256]{1,0:T(8,128)S(1)}, u32[]{:S(2)}, u32[]{:S(2)}) collective-permute-start(f32[256,256]{1,0:T(8,128)S(1)} %shard_map.57.refs_1_.refs_0_), channel_id=1, source_target_pairs={{1,3},{3,1},{5,7},{7,5},{9,11},{11,9},{13,15},{15,13},{17,19},{19,... | collective-permute-start | bytes 786440 | tf_op jit(solution)/shard_map/ppermute | solution.py:342
  17.4 2.5 %collective-permute-done.7.refs_3_ = f32[64,256]{1,0:T(8,128)S(1)} collective-permute-done((f32[64,256]{1,0:T(8,128)S(1)}, f32[64,256]{1,0:T(8,128)S(1)}, u32[]{:S(2)}, u32[]{:S(2)}) %collective-permute-start.7) | collective-permute-done | bytes 65568 | tf_op jit(solution)/shard_map/ppermute | solution.py:288
  20.4 1.7 %collective-permute-start.15 = (f32[64,256]{1,0:T(8,128)S(1)}, f32[64,256]{1,0:T(8,128)S(1)}, u32[]{:S(2)}, u32[]{:S(2)}) collective-permute-start(f32[64,256]{1,0:T(8,128)S(1)} %get-tuple-element.58.refs_0_), channel_id=1, source_target_pairs={{0,2},{1,3},{2,0},{3,1},{4,6},{5,7},{6,4},{7,5},{8,10},{9,11},{10,... | collective-permute-start | bytes 196616 | tf_op jit(solution)/shard_map/ppermute | solution.py:288
  22.1 2.6 %collective-permute-start.14 = (f32[64,256]{1,0:T(8,128)S(1)}, f32[64,256]{1,0:T(8,128)S(1)}, u32[]{:S(2)}, u32[]{:S(2)}) collective-permute-start(f32[64,256]{1,0:T(8,128)S(1)} %get-tuple-element.57.refs_0_.refs_2_), channel_id=1, source_target_pairs={{0,12},{1,13},{2,14},{3,15},{4,8},{5,9},{6,10},{7,11},{8,4},{9,5},... | collective-permute-start | bytes 196616 | tf_op jit(solution)/shard_map/ppermute | solution.py:288
  24.7 1.8 %collective-permute-start.12 = (f32[64,256]{1,0:T(8,128)S(1)}, f32[64,256]{1,0:T(8,128)S(1)}, u32[]{:S(2)}, u32[]{:S(2)}) collective-permute-start(f32[64,256]{1,0:T(8,128)S(1)} %get-tuple-element.57.refs_0_.refs_2_), channel_id=1, source_target_pairs={{0,4},{1,5},{2,6},{3,7},{4,0},{5,1},{6,2},{7,3},{8,12},{9,13},{10,... | collective-permute-start | bytes 196616 | tf_op jit(solution)/shard_map/ppermute | solution.py:288
  27.0 1.4 %collective-permute-done.14.refs_3_ = f32[64,256]{1,0:T(8,128)S(1)} collective-permute-done((f32[64,256]{1,0:T(8,128)S(1)}, f32[64,256]{1,0:T(8,128)S(1)}, u32[]{:S(2)}, u32[]{:S(2)}) %collective-permute-start.14) | collective-permute-done | bytes 65568 | tf_op jit(solution)/shard_map/ppermute | solution.py:288
  28.3 2.3 %collective-permute-done.13.refs_2_ = f32[64,256]{1,0:T(8,128)S(1)} collective-permute-done((f32[64,256]{1,0:T(8,128)S(1)}, f32[64,256]{1,0:T(8,128)S(1)}, u32[]{:S(2)}, u32[]{:S(2)}) %collective-permute-start.13) | collective-permute-done | bytes 65568 | tf_op jit(solution)/shard_map/ppermute | solution.py:288
  31.5 2.4 %collective-permute-start.21 = (f32[64,256]{1,0:T(8,128)S(1)}, f32[64,256]{1,0:T(8,128)S(1)}, u32[]{:S(2)}, u32[]{:S(2)}) collective-permute-start(f32[64,256]{1,0:T(8,128)S(1)} %shard_map.63.refs_3_.refs_0_), channel_id=1, source_target_pairs={{0,24},{1,25},{2,26},{3,27},{4,28},{5,29},{6,30},{7,31},{8,16},{9,... | collective-permute-start | bytes 196616 | tf_op jit(solution)/shard_map/ppermute | solution.py:290
  33.9 1.6 %collective-permute-start.20 = (f32[64,256]{1,0:T(8,128)S(1)}, f32[64,256]{1,0:T(8,128)S(1)}, u32[]{:S(2)}, u32[]{:S(2)}) collective-permute-start(f32[64,256]{1,0:T(8,128)S(1)} %shard_map.63.refs_3_.refs_0_), channel_id=1, source_target_pairs={{0,8},{1,9},{2,10},{3,11},{4,12},{5,13},{6,14},{7,15},{8,0},{9,1},... | collective-permute-start | bytes 196616 | tf_op jit(solution)/shard_map/ppermute | solution.py:288
  35.5 0.6 %collective-permute-start.22 = (f32[64,256]{1,0:T(8,128)S(1)}, f32[64,256]{1,0:T(8,128)S(1)}, u32[]{:S(2)}, u32[]{:S(2)}) collective-permute-start(f32[64,256]{1,0:T(8,128)S(1)} %shard_map.63.refs_3_.refs_0_), channel_id=1, source_target_pairs={{0,16},{1,17},{2,18},{3,19},{4,20},{5,21},{6,22},{7,23},{8,24},{9,... | collective-permute-start | bytes 196616 | tf_op jit(solution)/shard_map/ppermute | solution.py:290
  36.0 3.0 %collective-permute-done.21.refs_2_ = f32[64,256]{1,0:T(8,128)S(1)} collective-permute-done((f32[64,256]{1,0:T(8,128)S(1)}, f32[64,256]{1,0:T(8,128)S(1)}, u32[]{:S(2)}, u32[]{:S(2)}) %collective-permute-start.21) | collective-permute-done | bytes 65568 | tf_op jit(solution)/shard_map/ppermute | solution.py:290
  39.0 1.5 %collective-permute-done.20.refs_1_ = f32[64,256]{1,0:T(8,128)S(1)} collective-permute-done((f32[64,256]{1,0:T(8,128)S(1)}, f32[64,256]{1,0:T(8,128)S(1)}, u32[]{:S(2)}, u32[]{:S(2)}) %collective-permute-start.20) | collective-permute-done | bytes 65568 | tf_op jit(solution)/shard_map/ppermute | solution.py:288
  41.4 0.7 %collective-permute-done.23.other_ref = f32[64,256]{1,0:T(8,128)S(1)} collective-permute-done((f32[64,256]{1,0:T(8,128)S(1)}, f32[64,256]{1,0:T(8,128)S(1)}, u32[]{:S(2)}, u32[]{:S(2)}) %collective-permute-start.23) | collective-permute-done | bytes 65568 | tf_op jit(solution)/shard_map/ppermute | solution.py:288
  42.1 1.0 %shard_map.68 = f32[512,128]{1,0:T(8,128)} custom-call(f32[512,128]{1,0:T(8,128)S(1)} %shard_map.65.partial_ref, f32[64,256]{1,0:T(8,128)S(1)} %shard_map.67.own_ref, f32[64,256]{1,0:T(8,128)S(1)} %collective-permute-done.23.other_ref, bf16[5,512,256]{2,1,0:T(8,128)(2,1)S(1)} %copy-done.1), custom_call_target="tpu_custom_call" | custom-call | tf_op jit(solution)/shard_map/pallas_call | solution.py:231
  (53 shorter events, 6.1 us)
Async XLA Ops:
  1.5 1.5 %collective-permute-start = (f32[128,256]{1,0:T(8,128)S(1)}, f32[128,256]{1,0:T(8,128)S(1)}, u32[]{:S(2)}, u32[]{:S(2)}) collective-permute-start(f32[128,256]{1,0:T(8,128)S(1)} %get-tuple-element.33.refs_0_), channel_id=1, source_target_pairs={{0,1},{1,0},{2,3},{3,2},{4,5},{5,4},{6,7},{7,6},{8,9},{9,8},{10,11... | collective-permute-start | bytes 393224 | tf_op jit(solution)/shard_map/ppermute | solution.py:288
  3.5 1.7 %collective-permute-start.1 = (f32[64,256]{1,0:T(8,128)S(1)}, f32[64,256]{1,0:T(8,128)S(1)}, u32[]{:S(2)}, u32[]{:S(2)}) collective-permute-start(f32[64,256]{1,0:T(8,128)S(1)} %get-tuple-element.42), channel_id=1, source_target_pairs={{0,1},{1,0},{2,3},{3,2},{4,5},{5,4},{6,7},{7,6},{8,9},{9,8},{10,11... | collective-permute-start | bytes 196616 | tf_op jit(solution)/shard_map/ppermute | solution.py:288
  5.2 3.6 %collective-permute-start.8 = (f32[256,256]{1,0:T(8,128)S(1)}, f32[256,256]{1,0:T(8,128)S(1)}, u32[]{:S(2)}, u32[]{:S(2)}) collective-permute-start(f32[256,256]{1,0:T(8,128)S(1)} %get-tuple-element.52), channel_id=1, source_target_pairs={{0,1},{1,0},{2,3},{3,2},{4,5},{5,4},{6,7},{7,6},{8,9},{9,8},{10,11... | collective-permute-start | bytes 786440 | tf_op jit(solution)/shard_map/ppermute | solution.py:288
  5.4 5.3 %collective-permute-start.2 = (f32[64,256]{1,0:T(8,128)S(1)}, f32[64,256]{1,0:T(8,128)S(1)}, u32[]{:S(2)}, u32[]{:S(2)}) collective-permute-start(f32[64,256]{1,0:T(8,128)S(1)} %shard_map.51.refs_0_), channel_id=1, source_target_pairs={{0,2},{1,3},{2,0},{3,1},{4,6},{5,7},{6,4},{7,5},{8,10},{9,11},{10,... | collective-permute-start | bytes 196616 | tf_op jit(solution)/shard_map/ppermute | solution.py:288
  8.3 2.6 %collective-permute-start.4 = (f32[3,64,256]{2,1,0:T(8,128)S(1)}, f32[3,64,256]{2,1,0:T(8,128)S(1)}, u32[]{:S(2)}, u32[]{:S(2)}) collective-permute-start(f32[3,64,256]{2,1,0:T(8,128)S(1)} %get-tuple-element.48), channel_id=1, source_target_pairs={{0,1},{1,0},{2,3},{3,2},{4,5},{5,4},{6,7},{7,6},{8,9},{9,8},{10,11... | collective-permute-start | bytes 589832 | tf_op jit(solution)/shard_map/ppermute | solution.py:288
  8.3 2.6 %collective-permute-start.3 = (f32[2,256,256]{2,1,0:T(8,128)S(1)}, f32[2,256,256]{2,1,0:T(8,128)S(1)}, u32[]{:S(2)}, u32[]{:S(2)}) collective-permute-start(f32[2,256,256]{2,1,0:T(8,128)S(1)} %get-tuple-element.46.refs_1_), channel_id=1, source_target_pairs={{0,1},{1,0},{2,3},{3,2},{4,5},{5,4},{6,7},{7,6},{8,9},{9,8},{10,11... | collective-permute-start | bytes 1572872 | tf_op jit(solution)/shard_map/ppermute | solution.py:288
  8.8 6.0 %collective-permute-start.10 = (f32[2,256,256]{2,1,0:T(8,128)S(1)}, f32[2,256,256]{2,1,0:T(8,128)S(1)}, u32[]{:S(2)}, u32[]{:S(2)}) collective-permute-start(f32[2,256,256]{2,1,0:T(8,128)S(1)} %get-tuple-element.54.refs_1_), channel_id=1, source_target_pairs={{0,1},{1,0},{2,3},{3,2},{4,5},{5,4},{6,7},{7,6},{8,9},{9,8},{10,11... | collective-permute-start | bytes 1572872 | tf_op jit(solution)/shard_map/ppermute | solution.py:288
  8.9 7.8 %collective-permute-start.9 = (f32[256,256]{1,0:T(8,128)S(1)}, f32[256,256]{1,0:T(8,128)S(1)}, u32[]{:S(2)}, u32[]{:S(2)}) collective-permute-start(f32[256,256]{1,0:T(8,128)S(1)} %shard_map.55.refs_0_), channel_id=1, source_target_pairs={{0,2},{1,5},{2,0},{3,7},{4,6},{5,1},{6,4},{7,3},{8,10},{9,13},{10,... | collective-permute-start | bytes 786440 | tf_op jit(solution)/shard_map/ppermute | solution.py:295
  11.2 8.7 %collective-permute-start.6 = (f32[2,64,256]{2,1,0:T(8,128)S(1)}, f32[2,64,256]{2,1,0:T(8,128)S(1)}, u32[]{:S(2)}, u32[]{:S(2)}) collective-permute-start(f32[2,64,256]{2,1,0:T(8,128)S(1)} %get-tuple-element.50.refs_3_), channel_id=1, source_target_pairs={{0,4},{1,3},{2,6},{3,1},{4,0},{5,7},{6,2},{7,5},{8,12},{9,11},{10,... | collective-permute-start | bytes 393224 | tf_op jit(solution)/shard_map/ppermute | solution.py:295
  13.2 6.7 %collective-permute-start.5 = (f32[2,64,256]{2,1,0:T(8,128)S(1)}, f32[2,64,256]{2,1,0:T(8,128)S(1)}, u32[]{:S(2)}, u32[]{:S(2)}) collective-permute-start(f32[2,64,256]{2,1,0:T(8,128)S(1)} %get-tuple-element.50.refs_3_), channel_id=1, source_target_pairs={{0,2},{1,5},{2,0},{3,7},{4,6},{5,1},{6,4},{7,3},{8,10},{9,13},{10,... | collective-permute-start | bytes 393224 | tf_op jit(solution)/shard_map/ppermute | solution.py:295
  14.7 5.2 %collective-permute-start.7 = (f32[64,256]{1,0:T(8,128)S(1)}, f32[64,256]{1,0:T(8,128)S(1)}, u32[]{:S(2)}, u32[]{:S(2)}) collective-permute-start(f32[64,256]{1,0:T(8,128)S(1)} %get-tuple-element.49.refs_0_), channel_id=1, source_target_pairs={{0,6},{1,7},{2,4},{3,5},{4,2},{5,3},{6,0},{7,1},{8,14},{9,15},{10,... | collective-permute-start | bytes 196616 | tf_op jit(solution)/shard_map/ppermute | solution.py:288
  16.7 10.2 %collective-permute-start.17 = (f32[256,256]{1,0:T(8,128)S(1)}, f32[256,256]{1,0:T(8,128)S(1)}, u32[]{:S(2)}, u32[]{:S(2)}) collective-permute-start(f32[256,256]{1,0:T(8,128)S(1)} %shard_map.57.refs_1_.refs_0_), channel_id=1, source_target_pairs={{1,3},{3,1},{5,7},{7,5},{9,11},{11,9},{13,15},{15,13},{17,19},{19,... | collective-permute-start | bytes 786440 | tf_op jit(solution)/shard_map/ppermute | solution.py:342
  17.3 2.8 %collective-permute-start.11 = (f32[256,256]{1,0:T(8,128)S(1)}, f32[256,256]{1,0:T(8,128)S(1)}, u32[]{:S(2)}, u32[]{:S(2)}) collective-permute-start(f32[256,256]{1,0:T(8,128)S(1)} %shard_map.57.refs_1_.refs_0_), channel_id=1, source_target_pairs={{0,1},{1,0},{2,3},{3,2},{4,5},{5,4},{6,7},{7,6},{8,9},{9,8},{10,11... | collective-permute-start | bytes 786440 | tf_op jit(solution)/shard_map/ppermute | solution.py:288
  20.4 6.0 %collective-permute-start.15 = (f32[64,256]{1,0:T(8,128)S(1)}, f32[64,256]{1,0:T(8,128)S(1)}, u32[]{:S(2)}, u32[]{:S(2)}) collective-permute-start(f32[64,256]{1,0:T(8,128)S(1)} %get-tuple-element.58.refs_0_), channel_id=1, source_target_pairs={{0,2},{1,3},{2,0},{3,1},{4,6},{5,7},{6,4},{7,5},{8,10},{9,11},{10,... | collective-permute-start | bytes 196616 | tf_op jit(solution)/shard_map/ppermute | solution.py:288
  22.1 6.2 %collective-permute-start.14 = (f32[64,256]{1,0:T(8,128)S(1)}, f32[64,256]{1,0:T(8,128)S(1)}, u32[]{:S(2)}, u32[]{:S(2)}) collective-permute-start(f32[64,256]{1,0:T(8,128)S(1)} %get-tuple-element.57.refs_0_.refs_2_), channel_id=1, source_target_pairs={{0,12},{1,13},{2,14},{3,15},{4,8},{5,9},{6,10},{7,11},{8,4},{9,5},... | collective-permute-start | bytes 196616 | tf_op jit(solution)/shard_map/ppermute | solution.py:288
  24.7 5.8 %collective-permute-start.13 = (f32[64,256]{1,0:T(8,128)S(1)}, f32[64,256]{1,0:T(8,128)S(1)}, u32[]{:S(2)}, u32[]{:S(2)}) collective-permute-start(f32[64,256]{1,0:T(8,128)S(1)} %get-tuple-element.57.refs_0_.refs_2_), channel_id=1, source_target_pairs={{0,8},{1,9},{2,10},{3,11},{4,12},{5,13},{6,14},{7,15},{8,0},{9,1},... | collective-permute-start | bytes 196616 | tf_op jit(solution)/shard_map/ppermute | solution.py:288
  24.7 5.8 %collective-permute-start.12 = (f32[64,256]{1,0:T(8,128)S(1)}, f32[64,256]{1,0:T(8,128)S(1)}, u32[]{:S(2)}, u32[]{:S(2)}) collective-permute-start(f32[64,256]{1,0:T(8,128)S(1)} %get-tuple-element.57.refs_0_.refs_2_), channel_id=1, source_target_pairs={{0,4},{1,5},{2,6},{3,7},{4,0},{5,1},{6,2},{7,3},{8,12},{9,13},{10,... | collective-permute-start | bytes 196616 | tf_op jit(solution)/shard_map/ppermute | solution.py:288
  26.5 4.8 %collective-permute-start.16 = (f32[64,256]{1,0:T(8,128)S(1)}, f32[64,256]{1,0:T(8,128)S(1)}, u32[]{:S(2)}, u32[]{:S(2)}) collective-permute-start(f32[64,256]{1,0:T(8,128)S(1)} %shard_map.60.refs_0_), channel_id=1, source_target_pairs={{0,4},{1,5},{2,6},{3,7},{4,0},{5,1},{6,2},{7,3},{8,12},{9,13},{10,... | collective-permute-start | bytes 196616 | tf_op jit(solution)/shard_map/ppermute | solution.py:288
  26.9 4.4 %collective-permute-start.18 = (f32[256,256]{1,0:T(8,128)S(1)}, f32[256,256]{1,0:T(8,128)S(1)}, u32[]{:S(2)}, u32[]{:S(2)}) collective-permute-start(f32[256,256]{1,0:T(8,128)S(1)} %shard_map.62.refs_2_), channel_id=1, source_target_pairs={{0,1},{1,0},{2,3},{3,2},{4,5},{5,4},{6,7},{7,6},{8,9},{9,8},{10,11... | collective-permute-start | bytes 786440 | tf_op jit(solution)/shard_map/ppermute | solution.py:288
  31.5 7.5 %collective-permute-start.21 = (f32[64,256]{1,0:T(8,128)S(1)}, f32[64,256]{1,0:T(8,128)S(1)}, u32[]{:S(2)}, u32[]{:S(2)}) collective-permute-start(f32[64,256]{1,0:T(8,128)S(1)} %shard_map.63.refs_3_.refs_0_), channel_id=1, source_target_pairs={{0,24},{1,25},{2,26},{3,27},{4,28},{5,29},{6,30},{7,31},{8,16},{9,... | collective-permute-start | bytes 196616 | tf_op jit(solution)/shard_map/ppermute | solution.py:290
  33.9 6.6 %collective-permute-start.20 = (f32[64,256]{1,0:T(8,128)S(1)}, f32[64,256]{1,0:T(8,128)S(1)}, u32[]{:S(2)}, u32[]{:S(2)}) collective-permute-start(f32[64,256]{1,0:T(8,128)S(1)} %shard_map.63.refs_3_.refs_0_), channel_id=1, source_target_pairs={{0,8},{1,9},{2,10},{3,11},{4,12},{5,13},{6,14},{7,15},{8,0},{9,1},... | collective-permute-start | bytes 196616 | tf_op jit(solution)/shard_map/ppermute | solution.py:288
  35.5 5.0 %collective-permute-start.22 = (f32[64,256]{1,0:T(8,128)S(1)}, f32[64,256]{1,0:T(8,128)S(1)}, u32[]{:S(2)}, u32[]{:S(2)}) collective-permute-start(f32[64,256]{1,0:T(8,128)S(1)} %shard_map.63.refs_3_.refs_0_), channel_id=1, source_target_pairs={{0,16},{1,17},{2,18},{3,19},{4,20},{5,21},{6,22},{7,23},{8,24},{9,... | collective-permute-start | bytes 196616 | tf_op jit(solution)/shard_map/ppermute | solution.py:290
  36.0 4.8 %collective-permute-start.19 = (f32[3,64,256]{2,1,0:T(8,128)S(1)}, f32[3,64,256]{2,1,0:T(8,128)S(1)}, u32[]{:S(2)}, u32[]{:S(2)}) collective-permute-start(f32[3,64,256]{2,1,0:T(8,128)S(1)} %shard_map.64.refs_3_), channel_id=1, source_target_pairs={{0,1},{1,0},{2,3},{3,2},{4,5},{5,4},{6,7},{7,6},{8,9},{9,8},{10,11... | collective-permute-start | bytes 589832 | tf_op jit(solution)/shard_map/ppermute | solution.py:288
  40.7 1.3 %collective-permute-start.23 = (f32[64,256]{1,0:T(8,128)S(1)}, f32[64,256]{1,0:T(8,128)S(1)}, u32[]{:S(2)}, u32[]{:S(2)}) collective-permute-start(f32[64,256]{1,0:T(8,128)S(1)} %shard_map.67.own_ref), channel_id=1, source_target_pairs={{0,1},{1,0},{2,3},{3,2},{4,5},{5,4},{6,7},{7,6},{8,9},{9,8},{10,11... | collective-permute-start | bytes 196616 | tf_op jit(solution)/shard_map/ppermute | solution.py:288
  (3 other events, 8.9 us)

commit v2 on v1

--- a/solution.py
+++ b/solution.py
@@ -134,14 +134,29 @@
         keep_ref[place], send_ref[place] = ordered(upper_core, later[:half], later[half:])
 
 
-def cross_kernel(u_ref, v_ref, early_ref, late_ref, keep_ref, send_ref):
+def cross_kernel(u_ref, v_ref, early_ref, keep_ref, send_ref):
     upper_core = bit_is_set("sub", 0)
     first, second, third = u_ref[1].T, u_ref[2].T, u_ref[3].T
     early_ref[0] = dot(first, v_ref[2])
     early_ref[1] = dot(first, v_ref[3])
-    late_ref[0] = dot(first, v_ref[4])
-    late_ref[1] = dot(second, v_ref[4])
-    keep_ref[...], send_ref[...] = ordered(upper_core, dot(second, v_ref[3]), dot(third, v_ref[4]))
+    early_ref[2] = dot(first, v_ref[4])
+    early_ref[3] = dot(second, v_ref[4])
+    rows = keep_ref.shape[1]
+    for place, cross in enumerate((dot(second, v_ref[3]), dot(third, v_ref[4]))):
+        keep_ref[place], send_ref[place] = ordered(upper_core, cross[:rows], cross[rows:])
+
+
+def mix_kernel(keep_ref, got_ref, third_ref, fourth_ref):
+    third_ref[...], fourth_ref[...] = keep_ref[0] + got_ref[0], keep_ref[1] + got_ref[1]
+
+
+def both_added_kernel(third_ref, third_got_ref, fourth_ref, fourth_got_ref, third_out_ref, fourth_out_ref):
+    third_out_ref[...] = third_ref[...] + third_got_ref[...]
+    fourth_out_ref[...] = fourth_ref[...] + fourth_got_ref[...]
+
+
+def whole(half_ref, got_ref):
+    return jnp.concatenate(ordered(bit_is_set("sub", 0), half_ref[...], got_ref[...]), axis=0)
 
 
 def first_weights_kernel(own_ref, across_ref, c_ref, weights_ref):
@@ -156,16 +171,6 @@
     weights_ref[...] = weights_of(*ordered(bit_is_set(axis, bit), own, other), c_ref[level])
 
 
-def in_turn(first, second):
-    return ordered(bit_is_set("sub", 0), first, second)
-
-
-def second_weights_kernel(own_ref, first_ref, second_ref, both_ref, c_ref, weights_ref):
-    beside, across = in_turn(first_ref[0], second_ref[0])
-    own, other = own_ref[...] + beside, across + both_ref[...]
-    weights_ref[...] = weights_of(*ordered(bit_is_set("sub", 2), own, other), c_ref[2])
-
-
 def second_third_kernel(weights_ref, early_ref, got_ref, sums_ref, got_sums_ref, second_ref, pair_ref):
     weights = weights_ref[...]
     second_ref[...] = sums_ref[0] + got_sums_ref[0] - correction(weights, early_ref[0] + got_ref[0])
@@ -173,23 +178,21 @@
     pair_ref[1] = sums_ref[1] + got_sums_ref[1] - correction(weights, early_ref[1] + got_ref[1])
 
 
-def fourth_kernel(weights_ref, late_ref, got_ref, sums_ref, got_sums_ref, fourth_ref, cross_ref):
-    fourth_ref[...] = sums_ref[2] + got_sums_ref[2] - correction(weights_ref[...], late_ref[0] + got_ref[0])
-    cross_ref[...] = late_ref[1] + got_ref[1]
-
-
-def third_fourth_kernel(weights_ref, mixed_ref, mixed_got_ref, pair_ref, first_ref, second_ref, fourth_ref, cross_ref,
+def fourth_kernel(weights_ref, early_ref, got_ref, sums_ref, got_sums_ref, fourth_ref, cross_ref):
+    fourth_ref[...] = sums_ref[2] + got_sums_ref[2] - correction(weights_ref[...], early_ref[2] + got_ref[2])
+    cross_ref[...] = early_ref[3] + got_ref[3]
+
+
+def third_fourth_kernel(weights_ref, half_ref, half_got_ref, pair_ref, beside_ref, fourth_ref, cross_ref,
                         third_ref, later_ref):
     weights = weights_ref[...]
-    cross, _ = ordered(bit_is_set("sub", 0), mixed_ref[...], mixed_got_ref[...])
-    beside, _ = in_turn(first_ref[1], second_ref[1])
-    third_ref[...] = pair_ref[1] + beside - correction(weights, cross)
+    cross = whole(half_ref, half_got_ref)
+    third_ref[...] = pair_ref[1] + beside_ref[1] - correction(weights, cross)
     later_ref[...] = fourth_ref[...] - correction(weights, cross_ref[...])
 
 
-def last_sum_kernel(weights_ref, sum_ref, cross_ref, cross_got_ref, later_ref):
-    _, cross = ordered(bit_is_set("sub", 0), cross_ref[...], cross_got_ref[...])
-    later_ref[...] = sum_ref[...] - correction(weights_ref[...], cross)
+def last_sum_kernel(weights_ref, sum_ref, half_ref, half_got_ref, later_ref):
+    later_ref[...] = sum_ref[...] - correction(weights_ref[...], whole(half_ref, half_got_ref))
 
 
 def stack_kernel(first_ref, second_ref, third_ref, out_ref):
@@ -290,16 +293,11 @@
     return lax.ppermute(value, AXES, [(source, source ^ mask) for source in range(devices)])
 
 
-def crossed(value, even, odd):
-    pairs = [(source, source ^ (odd if source & 1 else even)) for source in range(lax.axis_size("sub"))]
-    return lax.ppermute(value, "sub", pairs)
-
-
 def tree(right_sides, basis_u, basis_v, coupling):
     points, rank = basis_u.shape[1:]
     columns = right_sides.shape[1]
     half = columns // 2
-    square, block = (rank, rank), (half, rank)
+    square, block, rows = (rank, rank), (half, rank), (rank // 2, rank)
 
     current, own, u_first, v_second, couple, right_near = run_start(right_sides, basis_u, basis_v, coupling)
     other = traded(own, 1)
@@ -308,8 +306,8 @@
         pair_kernel, [(columns, rank), block, block], own, other, couple, first_sum, first_cross
     )
     got = traded(send, 1)
-    early, late, keep_cross, send_cross = run(
-        cross_kernel, [(2,) + square, (2,) + square, square, square], basis_u, basis_v, after=[weights0], flops=2 * 10**9
+    early, keep_cross, send_cross = run(
+        cross_kernel, [(4,) + square, (2,) + rows, (2,) + rows], basis_u, basis_v, after=[weights0], flops=2 * 10**9
     )
     sums, sums_send = run(
         later_sums_kernel, [(3,) + block, (3,) + block], current, weights0, basis_u, basis_v,
@@ -321,34 +319,36 @@
     cross_got = traded(tied(send_cross, sum1), 1)
     early_got = traded(tied(early, sum1), 1)
     sums_got = traded(tied(sums_send, sum1), 1)
-    late_got = traded(tied(late, sum1), 1)
-    mixed = added(keep_cross, cross_got, flops=2 * 10**9)
-    mixed_across = crossed(mixed, 2, 4)
+    cross32, cross43 = run(mix_kernel, [rows, rows], keep_cross, cross_got, flops=2 * 10**9)
+    cross32_across = traded(cross32, 2)
+    cross43_across = traded(cross43, 4)
     (weights1,) = run(first_weights_kernel, [block], sum1, across, coupling, flops=8 * 10**9)
     second, pair = run(
         second_third_kernel, [block, (2,) + block], weights1, early, early_got, sums, sums_got
     )
 
-    both, first_turn, second_turn = traded(second, 6), crossed(pair, 2, 4), crossed(pair, 4, 2)
+    both, beside, across = traded(second, 6), traded(pair, 2), traded(second, 4)
     fourth, cross42 = run(
-        fourth_kernel, [block, square], weights1, late, late_got, sums, sums_got, flops=2 * 10**9
-    )
-    mixed = added(mixed, mixed_across, after=[fourth])
-    mixed_got = traded(mixed, 1)
+        fourth_kernel, [block, square], weights1, early, early_got, sums, sums_got, flops=800 * 10**6
+    )
+    cross32, cross43 = run(
+        both_added_kernel, [rows, rows], cross32, cross32_across, cross43, cross43_across, after=[fourth]
+    )
+    cross32_got = traded(cross32, 1)
     (weights2,) = run(
-        second_weights_kernel, [block], second, first_turn, second_turn, both, coupling, flops=8 * 10**9
-    )
-    odd = [(source, source ^ 2) for source in range(1, lax.axis_size("sub"), 2)]
-    cross43_got = lax.ppermute(mixed, "sub", odd)
+        functools.partial(square_weights_kernel, 2, "sub", 2, 2), [block], second, beside, across, both, coupling,
+        flops=8 * 10**9,
+    )
+    cross43_across = traded(cross43, 2)
     third, later4 = run(
         third_fourth_kernel, [block, block],
-        weights2, mixed, mixed_got, pair, first_turn, second_turn, fourth, cross42,
+        weights2, cross32, cross32_got, pair, beside, fourth, cross42,
     )
 
     sum4 = added(later4, traded(later4, 2), after=[third])
     sum4_got = traded(sum4, 4)
     both, across, beside = traded(third, 12), traded(third, 8), traded(third, 4)
-    cross43 = added(mixed, cross43_got, after=[third])
+    cross43 = added(cross43, cross43_across, after=[third])
     cross43_got = traded(cross43, 1)
     (weights3,) = run(
         functools.partial(square_weights_kernel, 3, "sub", 3, 2), [block], third, beside, across, both, coupling

time: 43.2 us -> 41.9 us (0.970)
  waiting for transfers between devices: 15.2 us -> 10.5 us
  starting transfers between devices: 20.6 us -> 23.9 us
    ppermute x18 -> x22, starting transfers between devices: 12.7 us -> 20.7 us  [traded(): lax.ppermute(value, 'sub', [(source, source ^ mask) for source in range(l...]
    ppermute x4 -> x0, starting transfers between devices: 4.89 us -> none  [the longest x3 4.21 us: crossed(): return lax.ppermute(value, 'sub', pairs)]
    ppermute x18 -> x22, waiting for transfers between devices: 10.5 us -> 7.56 us  [traded(): lax.ppermute(value, 'sub', [(source, source ^ mask) for source in range(l...]
    ppermute x4 -> x0, waiting for transfers between devices: 1.65 us -> none  [the longest x3 1.64 us: crossed(): return lax.ppermute(value, 'sub', pairs)]
where the time goes in v2:
time: 41.9 us; the launch traced here: 41.8 us
  starting transfers between devices  23.9 us (57%)
  waiting for transfers between devices  10.5 us (25%)
  Pallas kernels  7.05 us (17%)
    ppermute x22, starting transfers between devices, traded(): lax.ppermute(value, 'sub', [(source, source ^ mask) for source in range(l...  20.7 us
    ppermute x22, waiting for transfers between devices, traded(): lax.ppermute(value, 'sub', [(source, source ^ mask) for source in range(l...  7.56 us
    pallas_call x21, Pallas kernels, run(): pl.pallas_call(lambda *refs: kernel(*refs[:len(args)], *refs[len(args) +...  4.55 us
    ppermute x2, starting transfers between devices, traded(): lax.ppermute(value, AXES, [(source, source ^ mask) for source in range(de...  3.19 us
    ppermute x2, waiting for transfers between devices, traded(): lax.ppermute(value, AXES, [(source, source ^ mask) for source in range(de...  2.98 us
    pallas_call x1, Pallas kernels, run_start(): pl.pallas_call(start_kernel, out_shape=outs, in_specs=[pl.BlockSpec(memor...  1.47 us
    pallas_call x1, Pallas kernels, run_last(): pl.pallas_call(functools.partial(last_kernel, level, chunks), out_shape=j...  1.02 us
  transfers between devices with their start and end apart: 24, of which 10 were waited for; matrix products, arithmetic and copies ran while one was open for 0% of the time, Pallas kernels for 9%

profile of v2, /device:TPU:0, one launch (start us, length us, event | category | flops | bytes accessed | tf_op | source)
XLA Modules:
  0.0 41.8 jit_solution(15583013812441989317)
XLA Ops:
  0.0 1.5 %shard_map.46 = (f32[128,512]{1,0:T(8,128)S(1)}, f32[128,256]{1,0:T(8,128)S(1)}, bf16[512,256]{1,0:T(8,128)(2,1)S(1)}, bf16[512,256]{1,0:T(8,128)(2,1)S(1)}, bf1...) custom-call(f32[512,128]{1,0:T(8,128)} %right_hbm.1, bf16[5,512,256]{2,1,0:T(8,128)(2,1)} %u_ref.1, ...), custom_call_target="tpu_custom_call" | custom-call | tf_op jit(solution)/shard_map/pallas_call | solution.py:275
  2.3 0.7 %collective-permute-done.refs_1_ = f32[128,256]{1,0:T(8,128)S(1)} collective-permute-done((f32[128,256]{1,0:T(8,128)S(1)}, f32[128,256]{1,0:T(8,128)S(1)}, u32[]{:S(2)}, u32[]{:S(2)}) %collective-permute-start) | collective-permute-done | bytes 131104 | tf_op jit(solution)/shard_map/ppermute | solution.py:291
  4.0 0.6 %shard_map.49 = (f32[4,256,256]{2,1,0:T(8,128)S(1)}, f32[2,128,256]{2,1,0:T(8,128)S(1)}, f32[2,128,256]{2,1,0:T(8,128)S(1)}) custom-call(bf16[5,512,256]{2,1,0:T(8,128)(2,1)S(1)} %copy-done.1, bf16[5,512,256]{2,1,0:T(8,128)(2,1)S(1)} %copy-done.2, f32[128,256]{1,0:T(8,128)S(1)} %get-tuple-element.42.refs_2_.refs_1_), custom_call_target="tpu_custom_call" | custom-call | flops 2000000000 | tf_op jit(solution)/shard_map/pallas_call | solution.py:246
  4.6 0.6 %shard_map.50 = (f32[3,64,256]{2,1,0:T(8,128)S(1)}, f32[3,64,256]{2,1,0:T(8,128)S(1)}) custom-call(f32[128,512]{1,0:T(8,128)S(1)} %get-tuple-element.37.refs_0_, f32[128,256]{1,0:T(8,128)S(1)} %get-tuple-element.42.refs_2_.refs_1_, bf16[5,512,256]{2,1,0:T(8,128)(2,1)S(1)} %copy-done.1, bf16[5,512,256]{2,1,0:T(8,128)(2,1)S(1)} %copy-done.2, ...), custom_call_target="tpu_custom_call" | custom-call | flops 2000000000 | tf_op jit(solution)/shard_map/pallas_call | solution.py:246
  5.8 2.6 %collective-permute-start.2 = (f32[64,256]{1,0:T(8,128)S(1)}, f32[64,256]{1,0:T(8,128)S(1)}, u32[]{:S(2)}, u32[]{:S(2)}) collective-permute-start(f32[64,256]{1,0:T(8,128)S(1)} %shard_map.51.refs_0_), channel_id=1, source_target_pairs={{0,2},{1,3},{2,0},{3,1},{4,6},{5,7},{6,4},{7,5},{8,10},{9,11},{10,... | collective-permute-start | bytes 196616 | tf_op jit(solution)/shard_map/ppermute | solution.py:291
  8.6 1.0 %collective-permute-start.9 = (f32[128,256]{1,0:T(8,128)S(1)}, f32[128,256]{1,0:T(8,128)S(1)}, u32[]{:S(2)}, u32[]{:S(2)}) collective-permute-start(f32[128,256]{1,0:T(8,128)S(1)} %get-tuple-element.55.refs_0_), channel_id=1, source_target_pairs={{0,2},{1,3},{2,0},{3,1},{4,6},{5,7},{6,4},{7,5},{8,10},{9,11},{10,... | collective-permute-start | bytes 393224 | tf_op jit(solution)/shard_map/ppermute | solution.py:291
  9.6 1.6 %collective-permute-start.10 = (f32[128,256]{1,0:T(8,128)S(1)}, f32[128,256]{1,0:T(8,128)S(1)}, u32[]{:S(2)}, u32[]{:S(2)}) collective-permute-start(f32[128,256]{1,0:T(8,128)S(1)} %get-tuple-element.56.refs_2_), channel_id=1, source_target_pairs={{0,4},{1,5},{2,6},{3,7},{4,0},{5,1},{6,2},{7,3},{8,12},{9,13},{10,... | collective-permute-start | bytes 393224 | tf_op jit(solution)/shard_map/ppermute | solution.py:291
  11.7 2.1 %collective-permute-start.5 = (f32[2,64,256]{2,1,0:T(8,128)S(1)}, f32[2,64,256]{2,1,0:T(8,128)S(1)}, u32[]{:S(2)}, u32[]{:S(2)}) collective-permute-start(f32[2,64,256]{2,1,0:T(8,128)S(1)} %get-tuple-element.52.refs_3_), channel_id=1, source_target_pairs={{0,2},{1,3},{2,0},{3,1},{4,6},{5,7},{6,4},{7,5},{8,10},{9,11},{10,... | collective-permute-start | bytes 393224 | tf_op jit(solution)/shard_map/ppermute | solution.py:291
  13.7 1.2 %collective-permute-start.7 = (f32[64,256]{1,0:T(8,128)S(1)}, f32[64,256]{1,0:T(8,128)S(1)}, u32[]{:S(2)}, u32[]{:S(2)}) collective-permute-start(f32[64,256]{1,0:T(8,128)S(1)} %get-tuple-element.51.refs_0_), channel_id=1, source_target_pairs={{0,6},{1,7},{2,4},{3,5},{4,2},{5,3},{6,0},{7,1},{8,14},{9,15},{10,... | collective-permute-start | bytes 196616 | tf_op jit(solution)/shard_map/ppermute | solution.py:291
  15.7 2.0 %collective-permute-start.17 = (f32[128,256]{1,0:T(8,128)S(1)}, f32[128,256]{1,0:T(8,128)S(1)}, u32[]{:S(2)}, u32[]{:S(2)}) collective-permute-start(f32[128,256]{1,0:T(8,128)S(1)} %get-tuple-element.62.refs_0_), channel_id=1, source_target_pairs={{0,2},{1,3},{2,0},{3,1},{4,6},{5,7},{6,4},{7,5},{8,10},{9,11},{10,... | collective-permute-start | bytes 393224 | tf_op jit(solution)/shard_map/ppermute | solution.py:291
  17.6 1.3 %collective-permute-done.7.refs_3_ = f32[64,256]{1,0:T(8,128)S(1)} collective-permute-done((f32[64,256]{1,0:T(8,128)S(1)}, f32[64,256]{1,0:T(8,128)S(1)}, u32[]{:S(2)}, u32[]{:S(2)}) %collective-permute-start.7) | collective-permute-done | bytes 65568 | tf_op jit(solution)/shard_map/ppermute | solution.py:291
  19.7 1.9 %collective-permute-start.15 = (f32[64,256]{1,0:T(8,128)S(1)}, f32[64,256]{1,0:T(8,128)S(1)}, u32[]{:S(2)}, u32[]{:S(2)}) collective-permute-start(f32[64,256]{1,0:T(8,128)S(1)} %get-tuple-element.61.refs_0_), channel_id=1, source_target_pairs={{0,2},{1,3},{2,0},{3,1},{4,6},{5,7},{6,4},{7,5},{8,10},{9,11},{10,... | collective-permute-start | bytes 196616 | tf_op jit(solution)/shard_map/ppermute | solution.py:291
  21.6 2.7 %collective-permute-start.14 = (f32[64,256]{1,0:T(8,128)S(1)}, f32[64,256]{1,0:T(8,128)S(1)}, u32[]{:S(2)}, u32[]{:S(2)}) collective-permute-start(f32[64,256]{1,0:T(8,128)S(1)} %get-tuple-element.60.refs_0_.refs_2_), channel_id=1, source_target_pairs={{0,12},{1,13},{2,14},{3,15},{4,8},{5,9},{6,10},{7,11},{8,4},{9,5},... | collective-permute-start | bytes 196616 | tf_op jit(solution)/shard_map/ppermute | solution.py:291
  24.4 1.7 %collective-permute-start.12 = (f32[64,256]{1,0:T(8,128)S(1)}, f32[64,256]{1,0:T(8,128)S(1)}, u32[]{:S(2)}, u32[]{:S(2)}) collective-permute-start(f32[64,256]{1,0:T(8,128)S(1)} %get-tuple-element.60.refs_0_.refs_2_), channel_id=1, source_target_pairs={{0,4},{1,5},{2,6},{3,7},{4,0},{5,1},{6,2},{7,3},{8,12},{9,13},{10,... | collective-permute-start | bytes 196616 | tf_op jit(solution)/shard_map/ppermute | solution.py:291
  26.6 1.7 %collective-permute-done.14.refs_3_ = f32[64,256]{1,0:T(8,128)S(1)} collective-permute-done((f32[64,256]{1,0:T(8,128)S(1)}, f32[64,256]{1,0:T(8,128)S(1)}, u32[]{:S(2)}, u32[]{:S(2)}) %collective-permute-start.14) | collective-permute-done | bytes 65568 | tf_op jit(solution)/shard_map/ppermute | solution.py:291
  28.3 2.0 %collective-permute-done.13.refs_2_ = f32[64,256]{1,0:T(8,128)S(1)} collective-permute-done((f32[64,256]{1,0:T(8,128)S(1)}, f32[64,256]{1,0:T(8,128)S(1)}, u32[]{:S(2)}, u32[]{:S(2)}) %collective-permute-start.13) | collective-permute-done | bytes 65568 | tf_op jit(solution)/shard_map/ppermute | solution.py:291
  30.9 2.6 %collective-permute-start.21 = (f32[64,256]{1,0:T(8,128)S(1)}, f32[64,256]{1,0:T(8,128)S(1)}, u32[]{:S(2)}, u32[]{:S(2)}) collective-permute-start(f32[64,256]{1,0:T(8,128)S(1)} %shard_map.63.refs_3_.refs_0_), channel_id=1, source_target_pairs={{0,24},{1,25},{2,26},{3,27},{4,28},{5,29},{6,30},{7,31},{8,16},{9,... | collective-permute-start | bytes 196616 | tf_op jit(solution)/shard_map/ppermute | solution.py:293
  33.5 1.3 %collective-permute-start.20 = (f32[64,256]{1,0:T(8,128)S(1)}, f32[64,256]{1,0:T(8,128)S(1)}, u32[]{:S(2)}, u32[]{:S(2)}) collective-permute-start(f32[64,256]{1,0:T(8,128)S(1)} %shard_map.63.refs_3_.refs_0_), channel_id=1, source_target_pairs={{0,8},{1,9},{2,10},{3,11},{4,12},{5,13},{6,14},{7,15},{8,0},{9,1},... | collective-permute-start | bytes 196616 | tf_op jit(solution)/shard_map/ppermute | solution.py:291
  34.9 0.6 %collective-permute-start.22 = (f32[64,256]{1,0:T(8,128)S(1)}, f32[64,256]{1,0:T(8,128)S(1)}, u32[]{:S(2)}, u32[]{:S(2)}) collective-permute-start(f32[64,256]{1,0:T(8,128)S(1)} %shard_map.63.refs_3_.refs_0_), channel_id=1, source_target_pairs={{0,16},{1,17},{2,18},{3,19},{4,20},{5,21},{6,22},{7,23},{8,24},{9,... | collective-permute-start | bytes 196616 | tf_op jit(solution)/shard_map/ppermute | solution.py:293
  35.4 2.6 %collective-permute-done.21.refs_2_ = f32[64,256]{1,0:T(8,128)S(1)} collective-permute-done((f32[64,256]{1,0:T(8,128)S(1)}, f32[64,256]{1,0:T(8,128)S(1)}, u32[]{:S(2)}, u32[]{:S(2)}) %collective-permute-start.21) | collective-permute-done | bytes 65568 | tf_op jit(solution)/shard_map/ppermute | solution.py:293
  38.0 0.8 %collective-permute-done.20.refs_1_ = f32[64,256]{1,0:T(8,128)S(1)} collective-permute-done((f32[64,256]{1,0:T(8,128)S(1)}, f32[64,256]{1,0:T(8,128)S(1)}, u32[]{:S(2)}, u32[]{:S(2)}) %collective-permute-start.20) | collective-permute-done | bytes 65568 | tf_op jit(solution)/shard_map/ppermute | solution.py:291
  39.5 0.6 %shard_map.65.partial_ref = f32[512,128]{1,0:T(8,128)S(1)} custom-call(f32[512,128]{1,0:T(8,128)S(1)} %get-tuple-element.34.refs_0_, bf16[5,512,256]{2,1,0:T(8,128)(2,1)S(1)} %copy-done.1, f32[128,256]{1,0:T(8,128)S(1)} %get-tuple-element.42.refs_2_.refs_1_, f32[3,64,256]{2,1,0:T(8,128)S(1)} %shard_map.64.refs_3_, ...), custom_call_target="tpu_custom_call" | custom-call | flops 2000000000 | tf_op jit(solution)/shard_map/pallas_call | solution.py:246
  40.1 0.7 %collective-permute-done.23.other_ref = f32[64,256]{1,0:T(8,128)S(1)} collective-permute-done((f32[64,256]{1,0:T(8,128)S(1)}, f32[64,256]{1,0:T(8,128)S(1)}, u32[]{:S(2)}, u32[]{:S(2)}) %collective-permute-start.23) | collective-permute-done | bytes 65568 | tf_op jit(solution)/shard_map/ppermute | solution.py:291
  40.7 1.0 %shard_map.68 = f32[512,128]{1,0:T(8,128)} custom-call(f32[512,128]{1,0:T(8,128)S(1)} %shard_map.65.partial_ref, f32[64,256]{1,0:T(8,128)S(1)} %shard_map.67.own_ref, f32[64,256]{1,0:T(8,128)S(1)} %collective-permute-done.23.other_ref, bf16[5,512,256]{2,1,0:T(8,128)(2,1)S(1)} %copy-done.1), custom_call_target="tpu_custom_call" | custom-call | tf_op jit(solution)/shard_map/pallas_call | solution.py:234
  (53 shorter events, 6.3 us)
Async XLA Ops:
  1.5 1.5 %collective-permute-start = (f32[128,256]{1,0:T(8,128)S(1)}, f32[128,256]{1,0:T(8,128)S(1)}, u32[]{:S(2)}, u32[]{:S(2)}) collective-permute-start(f32[128,256]{1,0:T(8,128)S(1)} %get-tuple-element.35.refs_0_), channel_id=1, source_target_pairs={{0,1},{1,0},{2,3},{3,2},{4,5},{5,4},{6,7},{7,6},{8,9},{9,8},{10,11... | collective-permute-start | bytes 393224 | tf_op jit(solution)/shard_map/ppermute | solution.py:291
  3.5 1.7 %collective-permute-start.1 = (f32[64,256]{1,0:T(8,128)S(1)}, f32[64,256]{1,0:T(8,128)S(1)}, u32[]{:S(2)}, u32[]{:S(2)}) collective-permute-start(f32[64,256]{1,0:T(8,128)S(1)} %get-tuple-element.44), channel_id=1, source_target_pairs={{0,1},{1,0},{2,3},{3,2},{4,5},{5,4},{6,7},{7,6},{8,9},{9,8},{10,11... | collective-permute-start | bytes 196616 | tf_op jit(solution)/shard_map/ppermute | solution.py:291
  5.2 3.3 %collective-permute-start.8 = (f32[2,128,256]{2,1,0:T(8,128)S(1)}, f32[2,128,256]{2,1,0:T(8,128)S(1)}, u32[]{:S(2)}, u32[]{:S(2)}) collective-permute-start(f32[2,128,256]{2,1,0:T(8,128)S(1)} %get-tuple-element.54), channel_id=1, source_target_pairs={{0,1},{1,0},{2,3},{3,2},{4,5},{5,4},{6,7},{7,6},{8,9},{9,8},{10,11... | collective-permute-start | bytes 786440 | tf_op jit(solution)/shard_map/ppermute | solution.py:291
  5.5 6.0 %collective-permute-start.3 = (f32[4,256,256]{2,1,0:T(8,128)S(1)}, f32[4,256,256]{2,1,0:T(8,128)S(1)}, u32[]{:S(2)}, u32[]{:S(2)}) collective-permute-start(f32[4,256,256]{2,1,0:T(8,128)S(1)} %get-tuple-element.48.refs_1_), channel_id=1, source_target_pairs={{0,1},{1,0},{2,3},{3,2},{4,5},{5,4},{6,7},{7,6},{8,9},{9,8},{10,11... | collective-permute-start | bytes 3145736 | tf_op jit(solution)/shard_map/ppermute | solution.py:291
  5.8 5.4 %collective-permute-start.2 = (f32[64,256]{1,0:T(8,128)S(1)}, f32[64,256]{1,0:T(8,128)S(1)}, u32[]{:S(2)}, u32[]{:S(2)}) collective-permute-start(f32[64,256]{1,0:T(8,128)S(1)} %shard_map.51.refs_0_), channel_id=1, source_target_pairs={{0,2},{1,3},{2,0},{3,1},{4,6},{5,7},{6,4},{7,5},{8,10},{9,11},{10,... | collective-permute-start | bytes 196616 | tf_op jit(solution)/shard_map/ppermute | solution.py:291
  8.5 2.9 %collective-permute-start.4 = (f32[3,64,256]{2,1,0:T(8,128)S(1)}, f32[3,64,256]{2,1,0:T(8,128)S(1)}, u32[]{:S(2)}, u32[]{:S(2)}) collective-permute-start(f32[3,64,256]{2,1,0:T(8,128)S(1)} %get-tuple-element.50), channel_id=1, source_target_pairs={{0,1},{1,0},{2,3},{3,2},{4,5},{5,4},{6,7},{7,6},{8,9},{9,8},{10,11... | collective-permute-start | bytes 589832 | tf_op jit(solution)/shard_map/ppermute | solution.py:291
  8.6 7.0 %collective-permute-start.9 = (f32[128,256]{1,0:T(8,128)S(1)}, f32[128,256]{1,0:T(8,128)S(1)}, u32[]{:S(2)}, u32[]{:S(2)}) collective-permute-start(f32[128,256]{1,0:T(8,128)S(1)} %get-tuple-element.55.refs_0_), channel_id=1, source_target_pairs={{0,2},{1,3},{2,0},{3,1},{4,6},{5,7},{6,4},{7,5},{8,10},{9,11},{10,... | collective-permute-start | bytes 393224 | tf_op jit(solution)/shard_map/ppermute | solution.py:291
  9.6 6.0 %collective-permute-start.10 = (f32[128,256]{1,0:T(8,128)S(1)}, f32[128,256]{1,0:T(8,128)S(1)}, u32[]{:S(2)}, u32[]{:S(2)}) collective-permute-start(f32[128,256]{1,0:T(8,128)S(1)} %get-tuple-element.56.refs_2_), channel_id=1, source_target_pairs={{0,4},{1,5},{2,6},{3,7},{4,0},{5,1},{6,2},{7,3},{8,12},{9,13},{10,... | collective-permute-start | bytes 393224 | tf_op jit(solution)/shard_map/ppermute | solution.py:291
  11.7 7.5 %collective-permute-start.5 = (f32[2,64,256]{2,1,0:T(8,128)S(1)}, f32[2,64,256]{2,1,0:T(8,128)S(1)}, u32[]{:S(2)}, u32[]{:S(2)}) collective-permute-start(f32[2,64,256]{2,1,0:T(8,128)S(1)} %get-tuple-element.52.refs_3_), channel_id=1, source_target_pairs={{0,2},{1,3},{2,0},{3,1},{4,6},{5,7},{6,4},{7,5},{8,10},{9,11},{10,... | collective-permute-start | bytes 393224 | tf_op jit(solution)/shard_map/ppermute | solution.py:291
  13.7 5.2 %collective-permute-start.7 = (f32[64,256]{1,0:T(8,128)S(1)}, f32[64,256]{1,0:T(8,128)S(1)}, u32[]{:S(2)}, u32[]{:S(2)}) collective-permute-start(f32[64,256]{1,0:T(8,128)S(1)} %get-tuple-element.51.refs_0_), channel_id=1, source_target_pairs={{0,6},{1,7},{2,4},{3,5},{4,2},{5,3},{6,0},{7,1},{8,14},{9,15},{10,... | collective-permute-start | bytes 196616 | tf_op jit(solution)/shard_map/ppermute | solution.py:291
  15.0 4.3 %collective-permute-start.6 = (f32[64,256]{1,0:T(8,128)S(1)}, f32[64,256]{1,0:T(8,128)S(1)}, u32[]{:S(2)}, u32[]{:S(2)}) collective-permute-start(f32[64,256]{1,0:T(8,128)S(1)} %get-tuple-element.51.refs_0_), channel_id=1, source_target_pairs={{0,4},{1,5},{2,6},{3,7},{4,0},{5,1},{6,2},{7,3},{8,12},{9,13},{10,... | collective-permute-start | bytes 196616 | tf_op jit(solution)/shard_map/ppermute | solution.py:291
  15.6 3.9 %collective-permute-start.11 = (f32[128,256]{1,0:T(8,128)S(1)}, f32[128,256]{1,0:T(8,128)S(1)}, u32[]{:S(2)}, u32[]{:S(2)}) collective-permute-start(f32[128,256]{1,0:T(8,128)S(1)} %get-tuple-element.58.refs_1_), channel_id=1, source_target_pairs={{0,1},{1,0},{2,3},{3,2},{4,5},{5,4},{6,7},{7,6},{8,9},{9,8},{10,11... | collective-permute-start | bytes 393224 | tf_op jit(solution)/shard_map/ppermute | solution.py:291
  15.7 10.8 %collective-permute-start.17 = (f32[128,256]{1,0:T(8,128)S(1)}, f32[128,256]{1,0:T(8,128)S(1)}, u32[]{:S(2)}, u32[]{:S(2)}) collective-permute-start(f32[128,256]{1,0:T(8,128)S(1)} %get-tuple-element.62.refs_0_), channel_id=1, source_target_pairs={{0,2},{1,3},{2,0},{3,1},{4,6},{5,7},{6,4},{7,5},{8,10},{9,11},{10,... | collective-permute-start | bytes 393224 | tf_op jit(solution)/shard_map/ppermute | solution.py:291
  19.7 6.3 %collective-permute-start.15 = (f32[64,256]{1,0:T(8,128)S(1)}, f32[64,256]{1,0:T(8,128)S(1)}, u32[]{:S(2)}, u32[]{:S(2)}) collective-permute-start(f32[64,256]{1,0:T(8,128)S(1)} %get-tuple-element.61.refs_0_), channel_id=1, source_target_pairs={{0,2},{1,3},{2,0},{3,1},{4,6},{5,7},{6,4},{7,5},{8,10},{9,11},{10,... | collective-permute-start | bytes 196616 | tf_op jit(solution)/shard_map/ppermute | solution.py:291
  21.6 6.6 %collective-permute-start.14 = (f32[64,256]{1,0:T(8,128)S(1)}, f32[64,256]{1,0:T(8,128)S(1)}, u32[]{:S(2)}, u32[]{:S(2)}) collective-permute-start(f32[64,256]{1,0:T(8,128)S(1)} %get-tuple-element.60.refs_0_.refs_2_), channel_id=1, source_target_pairs={{0,12},{1,13},{2,14},{3,15},{4,8},{5,9},{6,10},{7,11},{8,4},{9,5},... | collective-permute-start | bytes 196616 | tf_op jit(solution)/shard_map/ppermute | solution.py:291
  24.4 5.9 %collective-permute-start.13 = (f32[64,256]{1,0:T(8,128)S(1)}, f32[64,256]{1,0:T(8,128)S(1)}, u32[]{:S(2)}, u32[]{:S(2)}) collective-permute-start(f32[64,256]{1,0:T(8,128)S(1)} %get-tuple-element.60.refs_0_.refs_2_), channel_id=1, source_target_pairs={{0,8},{1,9},{2,10},{3,11},{4,12},{5,13},{6,14},{7,15},{8,0},{9,1},... | collective-permute-start | bytes 196616 | tf_op jit(solution)/shard_map/ppermute | solution.py:291
  24.4 5.9 %collective-permute-start.12 = (f32[64,256]{1,0:T(8,128)S(1)}, f32[64,256]{1,0:T(8,128)S(1)}, u32[]{:S(2)}, u32[]{:S(2)}) collective-permute-start(f32[64,256]{1,0:T(8,128)S(1)} %get-tuple-element.60.refs_0_.refs_2_), channel_id=1, source_target_pairs={{0,4},{1,5},{2,6},{3,7},{4,0},{5,1},{6,2},{7,3},{8,12},{9,13},{10,... | collective-permute-start | bytes 196616 | tf_op jit(solution)/shard_map/ppermute | solution.py:291
  26.0 4.6 %collective-permute-start.16 = (f32[64,256]{1,0:T(8,128)S(1)}, f32[64,256]{1,0:T(8,128)S(1)}, u32[]{:S(2)}, u32[]{:S(2)}) collective-permute-start(f32[64,256]{1,0:T(8,128)S(1)} %shard_map.60.refs_0_), channel_id=1, source_target_pairs={{0,4},{1,5},{2,6},{3,7},{4,0},{5,1},{6,2},{7,3},{8,12},{9,13},{10,... | collective-permute-start | bytes 196616 | tf_op jit(solution)/shard_map/ppermute | solution.py:291
  26.5 4.2 %collective-permute-start.18 = (f32[128,256]{1,0:T(8,128)S(1)}, f32[128,256]{1,0:T(8,128)S(1)}, u32[]{:S(2)}, u32[]{:S(2)}) collective-permute-start(f32[128,256]{1,0:T(8,128)S(1)} %shard_map.62.refs_2_), channel_id=1, source_target_pairs={{0,1},{1,0},{2,3},{3,2},{4,5},{5,4},{6,7},{7,6},{8,9},{9,8},{10,11... | collective-permute-start | bytes 393224 | tf_op jit(solution)/shard_map/ppermute | solution.py:291
  30.9 7.1 %collective-permute-start.21 = (f32[64,256]{1,0:T(8,128)S(1)}, f32[64,256]{1,0:T(8,128)S(1)}, u32[]{:S(2)}, u32[]{:S(2)}) collective-permute-start(f32[64,256]{1,0:T(8,128)S(1)} %shard_map.63.refs_3_.refs_0_), channel_id=1, source_target_pairs={{0,24},{1,25},{2,26},{3,27},{4,28},{5,29},{6,30},{7,31},{8,16},{9,... | collective-permute-start | bytes 196616 | tf_op jit(solution)/shard_map/ppermute | solution.py:293
  33.5 5.3 %collective-permute-start.20 = (f32[64,256]{1,0:T(8,128)S(1)}, f32[64,256]{1,0:T(8,128)S(1)}, u32[]{:S(2)}, u32[]{:S(2)}) collective-permute-start(f32[64,256]{1,0:T(8,128)S(1)} %shard_map.63.refs_3_.refs_0_), channel_id=1, source_target_pairs={{0,8},{1,9},{2,10},{3,11},{4,12},{5,13},{6,14},{7,15},{8,0},{9,1},... | collective-permute-start | bytes 196616 | tf_op jit(solution)/shard_map/ppermute | solution.py:291
  34.9 4.3 %collective-permute-start.22 = (f32[64,256]{1,0:T(8,128)S(1)}, f32[64,256]{1,0:T(8,128)S(1)}, u32[]{:S(2)}, u32[]{:S(2)}) collective-permute-start(f32[64,256]{1,0:T(8,128)S(1)} %shard_map.63.refs_3_.refs_0_), channel_id=1, source_target_pairs={{0,16},{1,17},{2,18},{3,19},{4,20},{5,21},{6,22},{7,23},{8,24},{9,... | collective-permute-start | bytes 196616 | tf_op jit(solution)/shard_map/ppermute | solution.py:293
  35.4 4.1 %collective-permute-start.19 = (f32[3,64,256]{2,1,0:T(8,128)S(1)}, f32[3,64,256]{2,1,0:T(8,128)S(1)}, u32[]{:S(2)}, u32[]{:S(2)}) collective-permute-start(f32[3,64,256]{2,1,0:T(8,128)S(1)} %shard_map.64.refs_3_), channel_id=1, source_target_pairs={{0,1},{1,0},{2,3},{3,2},{4,5},{5,4},{6,7},{7,6},{8,9},{9,8},{10,11... | collective-permute-start | bytes 589832 | tf_op jit(solution)/shard_map/ppermute | solution.py:291
  39.4 1.3 %collective-permute-start.23 = (f32[64,256]{1,0:T(8,128)S(1)}, f32[64,256]{1,0:T(8,128)S(1)}, u32[]{:S(2)}, u32[]{:S(2)}) collective-permute-start(f32[64,256]{1,0:T(8,128)S(1)} %shard_map.67.own_ref), channel_id=1, source_target_pairs={{0,1},{1,0},{2,3},{3,2},{4,5},{5,4},{6,7},{7,6},{8,9},{9,8},{10,11... | collective-permute-start | bytes 196616 | tf_op jit(solution)/shard_map/ppermute | solution.py:291
  (3 other events, 9.2 us)

commit v3 on v2

--- a/solution.py
+++ b/solution.py
@@ -309,16 +309,16 @@
     early, keep_cross, send_cross = run(
         cross_kernel, [(4,) + square, (2,) + rows, (2,) + rows], basis_u, basis_v, after=[weights0], flops=2 * 10**9
     )
+    sum1 = added(keep, got, after=[keep_cross])
     sums, sums_send = run(
         later_sums_kernel, [(3,) + block, (3,) + block], current, weights0, basis_u, basis_v,
-        after=[keep_cross], flops=2 * 10**9,
-    )
-    sum1 = added(keep, got, after=[sums])
+        after=[sum1], flops=2 * 10**9,
+    )
 
     across = traded(sum1, 2)
     cross_got = traded(tied(send_cross, sum1), 1)
     early_got = traded(tied(early, sum1), 1)
-    sums_got = traded(tied(sums_send, sum1), 1)
+    sums_got = traded(sums_send, 1)
     cross32, cross43 = run(mix_kernel, [rows, rows], keep_cross, cross_got, flops=2 * 10**9)
     cross32_across = traded(cross32, 2)
     cross43_across = traded(cross43, 4)

time: 41.9 us -> 41.9 us (level)
  waiting for transfers between devices: 10.5 us -> 11.4 us
  starting transfers between devices: 23.9 us -> 23.1 us
    ppermute x22, starting transfers between devices: 20.7 us -> 19.7 us  [traded(): lax.ppermute(value, 'sub', [(source, source ^ mask) for source in range(l...]
    ppermute x22, waiting for transfers between devices: 7.56 us -> 8.39 us  [traded(): lax.ppermute(value, 'sub', [(source, source ^ mask) for source in range(l...]
where the time goes in v3:
time: 41.9 us; the launch traced here: 41.8 us
  starting transfers between devices  23.1 us (55%)
  waiting for transfers between devices  11.4 us (27%)
  Pallas kernels  7.05 us (17%)
    ppermute x22, starting transfers between devices, traded(): lax.ppermute(value, 'sub', [(source, source ^ mask) for source in range(l...  19.7 us
    ppermute x22, waiting for transfers between devices, traded(): lax.ppermute(value, 'sub', [(source, source ^ mask) for source in range(l...  8.39 us
    pallas_call x21, Pallas kernels, run(): pl.pallas_call(lambda *refs: kernel(*refs[:len(args)], *refs[len(args) +...  4.55 us
    ppermute x2, starting transfers between devices, traded(): lax.ppermute(value, AXES, [(source, source ^ mask) for source in range(de...  3.36 us
    ppermute x2, waiting for transfers between devices, traded(): lax.ppermute(value, AXES, [(source, source ^ mask) for source in range(de...  3 us
    pallas_call x1, Pallas kernels, run_start(): pl.pallas_call(start_kernel, out_shape=outs, in_specs=[pl.BlockSpec(memor...  1.47 us
    pallas_call x1, Pallas kernels, run_last(): pl.pallas_call(functools.partial(last_kernel, level, chunks), out_shape=j...  1.02 us
  transfers between devices with their start and end apart: 24, of which 10 were waited for; matrix products, arithmetic and copies ran while one was open for 0% of the time, Pallas kernels for 9%

profile of v3, /device:TPU:0, one launch (start us, length us, event | category | flops | bytes accessed | tf_op | source)
XLA Modules:
  0.0 41.8 jit_solution(14472544293986596461)
XLA Ops:
  0.0 1.5 %shard_map.46 = (f32[128,512]{1,0:T(8,128)S(1)}, f32[128,256]{1,0:T(8,128)S(1)}, bf16[512,256]{1,0:T(8,128)(2,1)S(1)}, bf16[512,256]{1,0:T(8,128)(2,1)S(1)}, bf1...) custom-call(f32[512,128]{1,0:T(8,128)} %right_hbm.1, bf16[5,512,256]{2,1,0:T(8,128)(2,1)} %u_ref.1, ...), custom_call_target="tpu_custom_call" | custom-call | tf_op jit(solution)/shard_map/pallas_call | solution.py:275
  2.3 0.7 %collective-permute-done.refs_1_ = f32[128,256]{1,0:T(8,128)S(1)} collective-permute-done((f32[128,256]{1,0:T(8,128)S(1)}, f32[128,256]{1,0:T(8,128)S(1)}, u32[]{:S(2)}, u32[]{:S(2)}) %collective-permute-start) | collective-permute-done | bytes 131104 | tf_op jit(solution)/shard_map/ppermute | solution.py:291
  4.0 0.6 %shard_map.49 = (f32[4,256,256]{2,1,0:T(8,128)S(1)}, f32[2,128,256]{2,1,0:T(8,128)S(1)}, f32[2,128,256]{2,1,0:T(8,128)S(1)}) custom-call(bf16[5,512,256]{2,1,0:T(8,128)(2,1)S(1)} %copy-done.1, bf16[5,512,256]{2,1,0:T(8,128)(2,1)S(1)} %copy-done.2, f32[128,256]{1,0:T(8,128)S(1)} %get-tuple-element.41.refs_2_.refs_1_), custom_call_target="tpu_custom_call" | custom-call | flops 2000000000 | tf_op jit(solution)/shard_map/pallas_call | solution.py:246
  5.3 2.6 %collective-permute-start.2 = (f32[64,256]{1,0:T(8,128)S(1)}, f32[64,256]{1,0:T(8,128)S(1)}, u32[]{:S(2)}, u32[]{:S(2)}) collective-permute-start(f32[64,256]{1,0:T(8,128)S(1)} %shard_map.50.refs_0_.refs_4_), channel_id=1, source_target_pairs={{0,2},{1,3},{2,0},{3,1},{4,6},{5,7},{6,4},{7,5},{8,10},{9,11},{10,... | collective-permute-start | bytes 196616 | tf_op jit(solution)/shard_map/ppermute | solution.py:291
  8.0 0.6 %shard_map.52 = (f32[3,64,256]{2,1,0:T(8,128)S(1)}, f32[3,64,256]{2,1,0:T(8,128)S(1)}) custom-call(f32[128,512]{1,0:T(8,128)S(1)} %get-tuple-element.36.refs_0_, f32[128,256]{1,0:T(8,128)S(1)} %get-tuple-element.41.refs_2_.refs_1_, bf16[5,512,256]{2,1,0:T(8,128)(2,1)S(1)} %copy-done.1, bf16[5,512,256]{2,1,0:T(8,128)(2,1)S(1)} %copy-done.2, ...), custom_call_target="tpu_custom_call" | custom-call | flops 2000000000 | tf_op jit(solution)/shard_map/pallas_call | solution.py:246
  9.4 2.0 %collective-permute-start.10 = (f32[128,256]{1,0:T(8,128)S(1)}, f32[128,256]{1,0:T(8,128)S(1)}, u32[]{:S(2)}, u32[]{:S(2)}) collective-permute-start(f32[128,256]{1,0:T(8,128)S(1)} %get-tuple-element.54.refs_2_), channel_id=1, source_target_pairs={{0,4},{1,5},{2,6},{3,7},{4,0},{5,1},{6,2},{7,3},{8,12},{9,13},{10,... | collective-permute-start | bytes 393224 | tf_op jit(solution)/shard_map/ppermute | solution.py:291
  11.9 1.5 %collective-permute-start.5 = (f32[2,64,256]{2,1,0:T(8,128)S(1)}, f32[2,64,256]{2,1,0:T(8,128)S(1)}, u32[]{:S(2)}, u32[]{:S(2)}) collective-permute-start(f32[2,64,256]{2,1,0:T(8,128)S(1)} %get-tuple-element.50.refs_3_), channel_id=1, source_target_pairs={{0,2},{1,3},{2,0},{3,1},{4,6},{5,7},{6,4},{7,5},{8,10},{9,11},{10,... | collective-permute-start | bytes 393224 | tf_op jit(solution)/shard_map/ppermute | solution.py:291
  13.5 1.0 %collective-permute-start.7 = (f32[64,256]{1,0:T(8,128)S(1)}, f32[64,256]{1,0:T(8,128)S(1)}, u32[]{:S(2)}, u32[]{:S(2)}) collective-permute-start(f32[64,256]{1,0:T(8,128)S(1)} %get-tuple-element.49.refs_0_), channel_id=1, source_target_pairs={{0,6},{1,7},{2,4},{3,5},{4,2},{5,3},{6,0},{7,1},{8,14},{9,15},{10,... | collective-permute-start | bytes 196616 | tf_op jit(solution)/shard_map/ppermute | solution.py:291
  14.4 1.0 %collective-permute-start.6 = (f32[64,256]{1,0:T(8,128)S(1)}, f32[64,256]{1,0:T(8,128)S(1)}, u32[]{:S(2)}, u32[]{:S(2)}) collective-permute-start(f32[64,256]{1,0:T(8,128)S(1)} %get-tuple-element.49.refs_0_), channel_id=1, source_target_pairs={{0,4},{1,5},{2,6},{3,7},{4,0},{5,1},{6,2},{7,3},{8,12},{9,13},{10,... | collective-permute-start | bytes 196616 | tf_op jit(solution)/shard_map/ppermute | solution.py:291
  15.8 1.5 %collective-permute-start.17 = (f32[128,256]{1,0:T(8,128)S(1)}, f32[128,256]{1,0:T(8,128)S(1)}, u32[]{:S(2)}, u32[]{:S(2)}) collective-permute-start(f32[128,256]{1,0:T(8,128)S(1)} %get-tuple-element.60.refs_0_), channel_id=1, source_target_pairs={{0,2},{1,3},{2,0},{3,1},{4,6},{5,7},{6,4},{7,5},{8,10},{9,11},{10,... | collective-permute-start | bytes 393224 | tf_op jit(solution)/shard_map/ppermute | solution.py:291
  17.4 1.4 %collective-permute-done.7.refs_3_ = f32[64,256]{1,0:T(8,128)S(1)} collective-permute-done((f32[64,256]{1,0:T(8,128)S(1)}, f32[64,256]{1,0:T(8,128)S(1)}, u32[]{:S(2)}, u32[]{:S(2)}) %collective-permute-start.7) | collective-permute-done | bytes 65568 | tf_op jit(solution)/shard_map/ppermute | solution.py:291
  19.4 1.3 %collective-permute-start.15 = (f32[64,256]{1,0:T(8,128)S(1)}, f32[64,256]{1,0:T(8,128)S(1)}, u32[]{:S(2)}, u32[]{:S(2)}) collective-permute-start(f32[64,256]{1,0:T(8,128)S(1)} %get-tuple-element.59.refs_0_), channel_id=1, source_target_pairs={{0,2},{1,3},{2,0},{3,1},{4,6},{5,7},{6,4},{7,5},{8,10},{9,11},{10,... | collective-permute-start | bytes 196616 | tf_op jit(solution)/shard_map/ppermute | solution.py:291
  20.8 3.0 %collective-permute-start.14 = (f32[64,256]{1,0:T(8,128)S(1)}, f32[64,256]{1,0:T(8,128)S(1)}, u32[]{:S(2)}, u32[]{:S(2)}) collective-permute-start(f32[64,256]{1,0:T(8,128)S(1)} %get-tuple-element.58.refs_0_.refs_2_), channel_id=1, source_target_pairs={{0,12},{1,13},{2,14},{3,15},{4,8},{5,9},{6,10},{7,11},{8,4},{9,5},... | collective-permute-start | bytes 196616 | tf_op jit(solution)/shard_map/ppermute | solution.py:291
  23.8 1.3 %collective-permute-start.12 = (f32[64,256]{1,0:T(8,128)S(1)}, f32[64,256]{1,0:T(8,128)S(1)}, u32[]{:S(2)}, u32[]{:S(2)}) collective-permute-start(f32[64,256]{1,0:T(8,128)S(1)} %get-tuple-element.58.refs_0_.refs_2_), channel_id=1, source_target_pairs={{0,4},{1,5},{2,6},{3,7},{4,0},{5,1},{6,2},{7,3},{8,12},{9,13},{10,... | collective-permute-start | bytes 196616 | tf_op jit(solution)/shard_map/ppermute | solution.py:291
  25.2 0.8 %collective-permute-start.16 = (f32[64,256]{1,0:T(8,128)S(1)}, f32[64,256]{1,0:T(8,128)S(1)}, u32[]{:S(2)}, u32[]{:S(2)}) collective-permute-start(f32[64,256]{1,0:T(8,128)S(1)} %shard_map.60.refs_0_), channel_id=1, source_target_pairs={{0,4},{1,5},{2,6},{3,7},{4,0},{5,1},{6,2},{7,3},{8,12},{9,13},{10,... | collective-permute-start | bytes 196616 | tf_op jit(solution)/shard_map/ppermute | solution.py:291
  26.0 1.0 %collective-permute-done.14.refs_3_ = f32[64,256]{1,0:T(8,128)S(1)} collective-permute-done((f32[64,256]{1,0:T(8,128)S(1)}, f32[64,256]{1,0:T(8,128)S(1)}, u32[]{:S(2)}, u32[]{:S(2)}) %collective-permute-start.14) | collective-permute-done | bytes 65568 | tf_op jit(solution)/shard_map/ppermute | solution.py:291
  27.0 2.5 %collective-permute-done.13.refs_2_ = f32[64,256]{1,0:T(8,128)S(1)} collective-permute-done((f32[64,256]{1,0:T(8,128)S(1)}, f32[64,256]{1,0:T(8,128)S(1)}, u32[]{:S(2)}, u32[]{:S(2)}) %collective-permute-start.13) | collective-permute-done | bytes 65568 | tf_op jit(solution)/shard_map/ppermute | solution.py:291
  30.2 2.8 %collective-permute-start.21 = (f32[64,256]{1,0:T(8,128)S(1)}, f32[64,256]{1,0:T(8,128)S(1)}, u32[]{:S(2)}, u32[]{:S(2)}) collective-permute-start(f32[64,256]{1,0:T(8,128)S(1)} %shard_map.63.refs_3_.refs_0_), channel_id=1, source_target_pairs={{0,24},{1,25},{2,26},{3,27},{4,28},{5,29},{6,30},{7,31},{8,16},{9,... | collective-permute-start | bytes 196616 | tf_op jit(solution)/shard_map/ppermute | solution.py:293
  33.0 1.2 %collective-permute-start.20 = (f32[64,256]{1,0:T(8,128)S(1)}, f32[64,256]{1,0:T(8,128)S(1)}, u32[]{:S(2)}, u32[]{:S(2)}) collective-permute-start(f32[64,256]{1,0:T(8,128)S(1)} %shard_map.63.refs_3_.refs_0_), channel_id=1, source_target_pairs={{0,8},{1,9},{2,10},{3,11},{4,12},{5,13},{6,14},{7,15},{8,0},{9,1},... | collective-permute-start | bytes 196616 | tf_op jit(solution)/shard_map/ppermute | solution.py:291
  34.2 0.6 %collective-permute-start.22 = (f32[64,256]{1,0:T(8,128)S(1)}, f32[64,256]{1,0:T(8,128)S(1)}, u32[]{:S(2)}, u32[]{:S(2)}) collective-permute-start(f32[64,256]{1,0:T(8,128)S(1)} %shard_map.63.refs_3_.refs_0_), channel_id=1, source_target_pairs={{0,16},{1,17},{2,18},{3,19},{4,20},{5,21},{6,22},{7,23},{8,24},{9,... | collective-permute-start | bytes 196616 | tf_op jit(solution)/shard_map/ppermute | solution.py:293
  34.7 3.0 %collective-permute-done.21.refs_2_ = f32[64,256]{1,0:T(8,128)S(1)} collective-permute-done((f32[64,256]{1,0:T(8,128)S(1)}, f32[64,256]{1,0:T(8,128)S(1)}, u32[]{:S(2)}, u32[]{:S(2)}) %collective-permute-start.21) | collective-permute-done | bytes 65568 | tf_op jit(solution)/shard_map/ppermute | solution.py:293
  37.7 1.5 %collective-permute-done.20.refs_1_ = f32[64,256]{1,0:T(8,128)S(1)} collective-permute-done((f32[64,256]{1,0:T(8,128)S(1)}, f32[64,256]{1,0:T(8,128)S(1)}, u32[]{:S(2)}, u32[]{:S(2)}) %collective-permute-start.20) | collective-permute-done | bytes 65568 | tf_op jit(solution)/shard_map/ppermute | solution.py:291
  40.1 0.7 %collective-permute-done.23.other_ref = f32[64,256]{1,0:T(8,128)S(1)} collective-permute-done((f32[64,256]{1,0:T(8,128)S(1)}, f32[64,256]{1,0:T(8,128)S(1)}, u32[]{:S(2)}, u32[]{:S(2)}) %collective-permute-start.23) | collective-permute-done | bytes 65568 | tf_op jit(solution)/shard_map/ppermute | solution.py:291
  40.8 1.0 %shard_map.68 = f32[512,128]{1,0:T(8,128)} custom-call(f32[512,128]{1,0:T(8,128)S(1)} %shard_map.65.partial_ref, f32[64,256]{1,0:T(8,128)S(1)} %shard_map.67.own_ref, f32[64,256]{1,0:T(8,128)S(1)} %collective-permute-done.23.other_ref, bf16[5,512,256]{2,1,0:T(8,128)(2,1)S(1)} %copy-done.1), custom_call_target="tpu_custom_call" | custom-call | tf_op jit(solution)/shard_map/pallas_call | solution.py:234
  (53 shorter events, 6.5 us)
Async XLA Ops:
  1.5 1.5 %collective-permute-start = (f32[128,256]{1,0:T(8,128)S(1)}, f32[128,256]{1,0:T(8,128)S(1)}, u32[]{:S(2)}, u32[]{:S(2)}) collective-permute-start(f32[128,256]{1,0:T(8,128)S(1)} %get-tuple-element.34.refs_0_), channel_id=1, source_target_pairs={{0,1},{1,0},{2,3},{3,2},{4,5},{5,4},{6,7},{7,6},{8,9},{9,8},{10,11... | collective-permute-start | bytes 393224 | tf_op jit(solution)/shard_map/ppermute | solution.py:291
  3.5 1.3 %collective-permute-start.1 = (f32[64,256]{1,0:T(8,128)S(1)}, f32[64,256]{1,0:T(8,128)S(1)}, u32[]{:S(2)}, u32[]{:S(2)}) collective-permute-start(f32[64,256]{1,0:T(8,128)S(1)} %get-tuple-element.43), channel_id=1, source_target_pairs={{0,1},{1,0},{2,3},{3,2},{4,5},{5,4},{6,7},{7,6},{8,9},{9,8},{10,11... | collective-permute-start | bytes 196616 | tf_op jit(solution)/shard_map/ppermute | solution.py:291
  4.9 4.3 %collective-permute-start.8 = (f32[2,128,256]{2,1,0:T(8,128)S(1)}, f32[2,128,256]{2,1,0:T(8,128)S(1)}, u32[]{:S(2)}, u32[]{:S(2)}) collective-permute-start(f32[2,128,256]{2,1,0:T(8,128)S(1)} %get-tuple-element.52), channel_id=1, source_target_pairs={{0,1},{1,0},{2,3},{3,2},{4,5},{5,4},{6,7},{7,6},{8,9},{9,8},{10,11... | collective-permute-start | bytes 786440 | tf_op jit(solution)/shard_map/ppermute | solution.py:291
  5.3 6.1 %collective-permute-start.2 = (f32[64,256]{1,0:T(8,128)S(1)}, f32[64,256]{1,0:T(8,128)S(1)}, u32[]{:S(2)}, u32[]{:S(2)}) collective-permute-start(f32[64,256]{1,0:T(8,128)S(1)} %shard_map.50.refs_0_.refs_4_), channel_id=1, source_target_pairs={{0,2},{1,3},{2,0},{3,1},{4,6},{5,7},{6,4},{7,5},{8,10},{9,11},{10,... | collective-permute-start | bytes 196616 | tf_op jit(solution)/shard_map/ppermute | solution.py:291
  7.9 3.7 %collective-permute-start.3 = (f32[4,256,256]{2,1,0:T(8,128)S(1)}, f32[4,256,256]{2,1,0:T(8,128)S(1)}, u32[]{:S(2)}, u32[]{:S(2)}) collective-permute-start(f32[4,256,256]{2,1,0:T(8,128)S(1)} %get-tuple-element.46.refs_1_), channel_id=1, source_target_pairs={{0,1},{1,0},{2,3},{3,2},{4,5},{5,4},{6,7},{7,6},{8,9},{9,8},{10,11... | collective-permute-start | bytes 3145736 | tf_op jit(solution)/shard_map/ppermute | solution.py:291
  8.6 3.0 %collective-permute-start.4 = (f32[3,64,256]{2,1,0:T(8,128)S(1)}, f32[3,64,256]{2,1,0:T(8,128)S(1)}, u32[]{:S(2)}, u32[]{:S(2)}) collective-permute-start(f32[3,64,256]{2,1,0:T(8,128)S(1)} %get-tuple-element.48), channel_id=1, source_target_pairs={{0,1},{1,0},{2,3},{3,2},{4,5},{5,4},{6,7},{7,6},{8,9},{9,8},{10,11... | collective-permute-start | bytes 589832 | tf_op jit(solution)/shard_map/ppermute | solution.py:291
  9.2 6.5 %collective-permute-start.9 = (f32[128,256]{1,0:T(8,128)S(1)}, f32[128,256]{1,0:T(8,128)S(1)}, u32[]{:S(2)}, u32[]{:S(2)}) collective-permute-start(f32[128,256]{1,0:T(8,128)S(1)} %get-tuple-element.53.refs_0_), channel_id=1, source_target_pairs={{0,2},{1,3},{2,0},{3,1},{4,6},{5,7},{6,4},{7,5},{8,10},{9,11},{10,... | collective-permute-start | bytes 393224 | tf_op jit(solution)/shard_map/ppermute | solution.py:291
  9.4 6.3 %collective-permute-start.10 = (f32[128,256]{1,0:T(8,128)S(1)}, f32[128,256]{1,0:T(8,128)S(1)}, u32[]{:S(2)}, u32[]{:S(2)}) collective-permute-start(f32[128,256]{1,0:T(8,128)S(1)} %get-tuple-element.54.refs_2_), channel_id=1, source_target_pairs={{0,4},{1,5},{2,6},{3,7},{4,0},{5,1},{6,2},{7,3},{8,12},{9,13},{10,... | collective-permute-start | bytes 393224 | tf_op jit(solution)/shard_map/ppermute | solution.py:291
  11.9 7.0 %collective-permute-start.5 = (f32[2,64,256]{2,1,0:T(8,128)S(1)}, f32[2,64,256]{2,1,0:T(8,128)S(1)}, u32[]{:S(2)}, u32[]{:S(2)}) collective-permute-start(f32[2,64,256]{2,1,0:T(8,128)S(1)} %get-tuple-element.50.refs_3_), channel_id=1, source_target_pairs={{0,2},{1,3},{2,0},{3,1},{4,6},{5,7},{6,4},{7,5},{8,10},{9,11},{10,... | collective-permute-start | bytes 393224 | tf_op jit(solution)/shard_map/ppermute | solution.py:291
  13.5 5.3 %collective-permute-start.7 = (f32[64,256]{1,0:T(8,128)S(1)}, f32[64,256]{1,0:T(8,128)S(1)}, u32[]{:S(2)}, u32[]{:S(2)}) collective-permute-start(f32[64,256]{1,0:T(8,128)S(1)} %get-tuple-element.49.refs_0_), channel_id=1, source_target_pairs={{0,6},{1,7},{2,4},{3,5},{4,2},{5,3},{6,0},{7,1},{8,14},{9,15},{10,... | collective-permute-start | bytes 196616 | tf_op jit(solution)/shard_map/ppermute | solution.py:291
  14.4 4.3 %collective-permute-start.6 = (f32[64,256]{1,0:T(8,128)S(1)}, f32[64,256]{1,0:T(8,128)S(1)}, u32[]{:S(2)}, u32[]{:S(2)}) collective-permute-start(f32[64,256]{1,0:T(8,128)S(1)} %get-tuple-element.49.refs_0_), channel_id=1, source_target_pairs={{0,4},{1,5},{2,6},{3,7},{4,0},{5,1},{6,2},{7,3},{8,12},{9,13},{10,... | collective-permute-start | bytes 196616 | tf_op jit(solution)/shard_map/ppermute | solution.py:291
  15.7 3.4 %collective-permute-start.11 = (f32[128,256]{1,0:T(8,128)S(1)}, f32[128,256]{1,0:T(8,128)S(1)}, u32[]{:S(2)}, u32[]{:S(2)}) collective-permute-start(f32[128,256]{1,0:T(8,128)S(1)} %get-tuple-element.56.refs_1_), channel_id=1, source_target_pairs={{0,1},{1,0},{2,3},{3,2},{4,5},{5,4},{6,7},{7,6},{8,9},{9,8},{10,11... | collective-permute-start | bytes 393224 | tf_op jit(solution)/shard_map/ppermute | solution.py:291
  15.8 10.1 %collective-permute-start.17 = (f32[128,256]{1,0:T(8,128)S(1)}, f32[128,256]{1,0:T(8,128)S(1)}, u32[]{:S(2)}, u32[]{:S(2)}) collective-permute-start(f32[128,256]{1,0:T(8,128)S(1)} %get-tuple-element.60.refs_0_), channel_id=1, source_target_pairs={{0,2},{1,3},{2,0},{3,1},{4,6},{5,7},{6,4},{7,5},{8,10},{9,11},{10,... | collective-permute-start | bytes 393224 | tf_op jit(solution)/shard_map/ppermute | solution.py:291
  19.4 5.7 %collective-permute-start.15 = (f32[64,256]{1,0:T(8,128)S(1)}, f32[64,256]{1,0:T(8,128)S(1)}, u32[]{:S(2)}, u32[]{:S(2)}) collective-permute-start(f32[64,256]{1,0:T(8,128)S(1)} %get-tuple-element.59.refs_0_), channel_id=1, source_target_pairs={{0,2},{1,3},{2,0},{3,1},{4,6},{5,7},{6,4},{7,5},{8,10},{9,11},{10,... | collective-permute-start | bytes 196616 | tf_op jit(solution)/shard_map/ppermute | solution.py:291
  20.8 6.2 %collective-permute-start.14 = (f32[64,256]{1,0:T(8,128)S(1)}, f32[64,256]{1,0:T(8,128)S(1)}, u32[]{:S(2)}, u32[]{:S(2)}) collective-permute-start(f32[64,256]{1,0:T(8,128)S(1)} %get-tuple-element.58.refs_0_.refs_2_), channel_id=1, source_target_pairs={{0,12},{1,13},{2,14},{3,15},{4,8},{5,9},{6,10},{7,11},{8,4},{9,5},... | collective-permute-start | bytes 196616 | tf_op jit(solution)/shard_map/ppermute | solution.py:291
  23.8 5.7 %collective-permute-start.13 = (f32[64,256]{1,0:T(8,128)S(1)}, f32[64,256]{1,0:T(8,128)S(1)}, u32[]{:S(2)}, u32[]{:S(2)}) collective-permute-start(f32[64,256]{1,0:T(8,128)S(1)} %get-tuple-element.58.refs_0_.refs_2_), channel_id=1, source_target_pairs={{0,8},{1,9},{2,10},{3,11},{4,12},{5,13},{6,14},{7,15},{8,0},{9,1},... | collective-permute-start | bytes 196616 | tf_op jit(solution)/shard_map/ppermute | solution.py:291
  23.8 5.7 %collective-permute-start.12 = (f32[64,256]{1,0:T(8,128)S(1)}, f32[64,256]{1,0:T(8,128)S(1)}, u32[]{:S(2)}, u32[]{:S(2)}) collective-permute-start(f32[64,256]{1,0:T(8,128)S(1)} %get-tuple-element.58.refs_0_.refs_2_), channel_id=1, source_target_pairs={{0,4},{1,5},{2,6},{3,7},{4,0},{5,1},{6,2},{7,3},{8,12},{9,13},{10,... | collective-permute-start | bytes 196616 | tf_op jit(solution)/shard_map/ppermute | solution.py:291
  25.2 4.8 %collective-permute-start.16 = (f32[64,256]{1,0:T(8,128)S(1)}, f32[64,256]{1,0:T(8,128)S(1)}, u32[]{:S(2)}, u32[]{:S(2)}) collective-permute-start(f32[64,256]{1,0:T(8,128)S(1)} %shard_map.60.refs_0_), channel_id=1, source_target_pairs={{0,4},{1,5},{2,6},{3,7},{4,0},{5,1},{6,2},{7,3},{8,12},{9,13},{10,... | collective-permute-start | bytes 196616 | tf_op jit(solution)/shard_map/ppermute | solution.py:291
  26.0 4.0 %collective-permute-start.18 = (f32[128,256]{1,0:T(8,128)S(1)}, f32[128,256]{1,0:T(8,128)S(1)}, u32[]{:S(2)}, u32[]{:S(2)}) collective-permute-start(f32[128,256]{1,0:T(8,128)S(1)} %shard_map.62.refs_2_), channel_id=1, source_target_pairs={{0,1},{1,0},{2,3},{3,2},{4,5},{5,4},{6,7},{7,6},{8,9},{9,8},{10,11... | collective-permute-start | bytes 393224 | tf_op jit(solution)/shard_map/ppermute | solution.py:291
  30.2 7.5 %collective-permute-start.21 = (f32[64,256]{1,0:T(8,128)S(1)}, f32[64,256]{1,0:T(8,128)S(1)}, u32[]{:S(2)}, u32[]{:S(2)}) collective-permute-start(f32[64,256]{1,0:T(8,128)S(1)} %shard_map.63.refs_3_.refs_0_), channel_id=1, source_target_pairs={{0,24},{1,25},{2,26},{3,27},{4,28},{5,29},{6,30},{7,31},{8,16},{9,... | collective-permute-start | bytes 196616 | tf_op jit(solution)/shard_map/ppermute | solution.py:293
  33.0 6.2 %collective-permute-start.20 = (f32[64,256]{1,0:T(8,128)S(1)}, f32[64,256]{1,0:T(8,128)S(1)}, u32[]{:S(2)}, u32[]{:S(2)}) collective-permute-start(f32[64,256]{1,0:T(8,128)S(1)} %shard_map.63.refs_3_.refs_0_), channel_id=1, source_target_pairs={{0,8},{1,9},{2,10},{3,11},{4,12},{5,13},{6,14},{7,15},{8,0},{9,1},... | collective-permute-start | bytes 196616 | tf_op jit(solution)/shard_map/ppermute | solution.py:291
  34.2 5.0 %collective-permute-start.22 = (f32[64,256]{1,0:T(8,128)S(1)}, f32[64,256]{1,0:T(8,128)S(1)}, u32[]{:S(2)}, u32[]{:S(2)}) collective-permute-start(f32[64,256]{1,0:T(8,128)S(1)} %shard_map.63.refs_3_.refs_0_), channel_id=1, source_target_pairs={{0,16},{1,17},{2,18},{3,19},{4,20},{5,21},{6,22},{7,23},{8,24},{9,... | collective-permute-start | bytes 196616 | tf_op jit(solution)/shard_map/ppermute | solution.py:293
  34.7 4.8 %collective-permute-start.19 = (f32[3,64,256]{2,1,0:T(8,128)S(1)}, f32[3,64,256]{2,1,0:T(8,128)S(1)}, u32[]{:S(2)}, u32[]{:S(2)}) collective-permute-start(f32[3,64,256]{2,1,0:T(8,128)S(1)} %shard_map.64.refs_3_), channel_id=1, source_target_pairs={{0,1},{1,0},{2,3},{3,2},{4,5},{5,4},{6,7},{7,6},{8,9},{9,8},{10,11... | collective-permute-start | bytes 589832 | tf_op jit(solution)/shard_map/ppermute | solution.py:291
  39.4 1.3 %collective-permute-start.23 = (f32[64,256]{1,0:T(8,128)S(1)}, f32[64,256]{1,0:T(8,128)S(1)}, u32[]{:S(2)}, u32[]{:S(2)}) collective-permute-start(f32[64,256]{1,0:T(8,128)S(1)} %shard_map.67.own_ref), channel_id=1, source_target_pairs={{0,1},{1,0},{2,3},{3,2},{4,5},{5,4},{6,7},{7,6},{8,9},{9,8},{10,11... | collective-permute-start | bytes 196616 | tf_op jit(solution)/shard_map/ppermute | solution.py:291
  (3 other events, 9.2 us)

commit v4 on v3

--- a/solution.py
+++ b/solution.py
@@ -110,24 +110,33 @@
         copy.wait()
 
 
-def first_sum_kernel(current_ref, u_ref, v_ref, sum_ref, cross_ref):
+def effect(couple, cross):
+    high, low = split(cross)
+    couple = couple.T
+    return dot(couple, high) + dot(couple, low)
+
+
+def first_sum_kernel(current_ref, u_ref, v_ref, c_ref, sum_ref, effect_ref):
     sum_ref[...] = folded(dot(stacked(current_ref[...]), v_ref[...]))
-    cross_ref[...] = dot(u_ref[...].T, v_ref[...])
-
-
-def pair_kernel(own_ref, other_ref, c_ref, sum_ref, cross_ref, weights_ref, keep_ref, send_ref):
+    effect_ref[...] = effect(c_ref[...], dot(u_ref[...].T, v_ref[...]))
+
+
+def pair_kernel(own_ref, other_ref, sum_ref, effect_ref, keep_ref, send_ref):
     upper_core = bit_is_set("sub", 0)
     half = keep_ref.shape[0]
-    weights = weights_of(*ordered(upper_core, own_ref[...], other_ref[...]), c_ref[...])
-    weights_ref[...] = weights
-    later = sum_ref[...] - correction(weights, cross_ref[...])
+    node = jnp.concatenate(ordered(upper_core, own_ref[...], other_ref[...]), axis=1)
+    later = sum_ref[...] - correction(node, effect_ref[...])
     keep_ref[...], send_ref[...] = ordered(upper_core, later[:half], later[half:])
+
+
+def pair_weights_kernel(own_ref, other_ref, c_ref, weights_ref):
+    weights_ref[...] = weights_of(*ordered(bit_is_set("sub", 0), own_ref[...], other_ref[...]), c_ref[...])
 
 
 def later_sums_kernel(current_ref, weights_ref, u_ref, v_ref, keep_ref, send_ref):
     upper_core = bit_is_set("sub", 0)
     half = keep_ref.shape[1]
-    current = current_ref[...] - folded(dot_transposed(stacked(weights_ref[...]), u_ref[0]))
+    current = current_ref[...] - folded(dot_transposed(stacked(weights_ref[...]), u_ref[...]))
     current = stacked(current)
     for place in range(keep_ref.shape[0]):
         later = folded(dot(current, v_ref[place + 2]))
@@ -301,18 +310,18 @@
 
     current, own, u_first, v_second, couple, right_near = run_start(right_sides, basis_u, basis_v, coupling)
     other = traded(own, 1)
-    first_sum, first_cross = run(first_sum_kernel, [(columns, rank), square], current, u_first, v_second)
-    weights0, keep, send = run(
-        pair_kernel, [(columns, rank), block, block], own, other, couple, first_sum, first_cross
-    )
+    first_sum, first_effect = run(
+        first_sum_kernel, [(columns, rank), (2 * rank, rank)], current, u_first, v_second, couple
+    )
+    keep, send = run(pair_kernel, [block, block], own, other, first_sum, first_effect)
     got = traded(send, 1)
     early, keep_cross, send_cross = run(
-        cross_kernel, [(4,) + square, (2,) + rows, (2,) + rows], basis_u, basis_v, after=[weights0], flops=2 * 10**9
+        cross_kernel, [(4,) + square, (2,) + rows, (2,) + rows], basis_u, basis_v, after=[keep], flops=2 * 10**9
     )
     sum1 = added(keep, got, after=[keep_cross])
+    (weights0,) = run(pair_weights_kernel, [(columns, rank)], own, other, couple, after=[sum1])
     sums, sums_send = run(
-        later_sums_kernel, [(3,) + block, (3,) + block], current, weights0, basis_u, basis_v,
-        after=[sum1], flops=2 * 10**9,
+        later_sums_kernel, [(3,) + block, (3,) + block], current, weights0, u_first, basis_v, flops=2 * 10**9
     )
 
     across = traded(sum1, 2)

time: 41.9 us -> 41.9 us (level)
    pallas_call x21 -> x22, Pallas kernels: 4.55 us -> 4.88 us  [run(): pl.pallas_call(lambda *refs: kernel(*refs[:len(args)], *refs[len(args) +...]
  transfers between devices with their start and end apart: 24 -> 24, of which waited for: 10 -> 10; matrix products, arithmetic and copies ran while one was open for 0% -> 0% of each run, Pallas kernels for 9% -> 10%
where the time goes in v4:
time: 41.9 us; the launch traced here: 41.7 us
  starting transfers between devices  23 us (55%)
  waiting for transfers between devices  11 us (26%)
  Pallas kernels  7.37 us (18%)
    ppermute x22, starting transfers between devices, traded(): lax.ppermute(value, 'sub', [(source, source ^ mask) for source in range(l...  19.6 us
    ppermute x22, waiting for transfers between devices, traded(): lax.ppermute(value, 'sub', [(source, source ^ mask) for source in range(l...  7.98 us
    pallas_call x22, Pallas kernels, run(): pl.pallas_call(lambda *refs: kernel(*refs[:len(args)], *refs[len(args) +...  4.88 us
    ppermute x2, starting transfers between devices, traded(): lax.ppermute(value, AXES, [(source, source ^ mask) for source in range(de...  3.49 us
    ppermute x2, waiting for transfers between devices, traded(): lax.ppermute(value, AXES, [(source, source ^ mask) for source in range(de...  3.04 us
    pallas_call x1, Pallas kernels, run_start(): pl.pallas_call(start_kernel, out_shape=outs, in_specs=[pl.BlockSpec(memor...  1.47 us
    pallas_call x1, Pallas kernels, run_last(): pl.pallas_call(functools.partial(last_kernel, level, chunks), out_shape=j...  1.02 us
  transfers between devices with their start and end apart: 24, of which 10 were waited for; matrix products, arithmetic and copies ran while one was open for 0% of the time, Pallas kernels for 10%

profile of v4, /device:TPU:0, one launch (start us, length us, event | category | flops | bytes accessed | tf_op | source)
XLA Modules:
  0.0 41.7 jit_solution(5345886440065499479)
XLA Ops:
  0.0 1.5 %shard_map.46 = (f32[128,512]{1,0:T(8,128)S(1)}, f32[128,256]{1,0:T(8,128)S(1)}, bf16[512,256]{1,0:T(8,128)(2,1)S(1)}, bf16[512,256]{1,0:T(8,128)(2,1)S(1)}, bf1...) custom-call(f32[512,128]{1,0:T(8,128)} %right_hbm.1, bf16[5,512,256]{2,1,0:T(8,128)(2,1)} %u_ref.1, ...), custom_call_target="tpu_custom_call" | custom-call | tf_op jit(solution)/shard_map/pallas_call | solution.py:284
  2.0 0.6 %shard_map.47 = (f32[128,256]{1,0:T(8,128)S(1)}, f32[512,256]{1,0:T(8,128)S(1)}) custom-call(f32[128,512]{1,0:T(8,128)S(1)} %get-tuple-element.35.refs_0_, bf16[512,256]{1,0:T(8,128)(2,1)S(1)} %get-tuple-element.36.refs_1_.refs_2_, bf16[512,256]{1,0:T(8,128)(2,1)S(1)} %get-tuple-element.37.refs_2_, bf16[256,512]{1,0:T(8,128)(2,1)S(1)} %get-tuple-element.34.refs_3_.refs_2_), custom_call_target="tpu_custom_call" | custom-call | tf_op jit(solution)/shard_map/pallas_call | solution.py:255
  3.7 0.6 %shard_map.49 = (f32[4,256,256]{2,1,0:T(8,128)S(1)}, f32[2,128,256]{2,1,0:T(8,128)S(1)}, f32[2,128,256]{2,1,0:T(8,128)S(1)}) custom-call(bf16[5,512,256]{2,1,0:T(8,128)(2,1)S(1)} %copy-done.1, bf16[5,512,256]{2,1,0:T(8,128)(2,1)S(1)} %copy-done.2, f32[64,256]{1,0:T(8,128)S(1)} %get-tuple-element.40.refs_2_.refs_0_), custom_call_target="tpu_custom_call" | custom-call | flops 2000000000 | tf_op jit(solution)/shard_map/pallas_call | solution.py:255
  5.1 2.6 %collective-permute-start.2 = (f32[64,256]{1,0:T(8,128)S(1)}, f32[64,256]{1,0:T(8,128)S(1)}, u32[]{:S(2)}, u32[]{:S(2)}) collective-permute-start(f32[64,256]{1,0:T(8,128)S(1)} %shard_map.50.refs_3_.refs_0_), channel_id=1, source_target_pairs={{0,2},{1,3},{2,0},{3,1},{4,6},{5,7},{6,4},{7,5},{8,10},{9,11},{10,... | collective-permute-start | bytes 196616 | tf_op jit(solution)/shard_map/ppermute | solution.py:300
  8.1 0.6 %shard_map.53 = (f32[3,64,256]{2,1,0:T(8,128)S(1)}, f32[3,64,256]{2,1,0:T(8,128)S(1)}) custom-call(f32[128,512]{1,0:T(8,128)S(1)} %get-tuple-element.35.refs_0_, f32[128,256]{1,0:T(8,128)S(1)} %shard_map.51.refs_1_.refs_2_, bf16[512,256]{1,0:T(8,128)(2,1)S(1)} %get-tuple-element.36.refs_1_.refs_2_, bf16[5,512,256]{2,1,0:T(8,128)(2,1)S(1)} %copy-done.2), custom_call_target="tpu_custom_call" | custom-call | flops 2000000000 | tf_op jit(solution)/shard_map/pallas_call | solution.py:255
  9.3 2.1 %collective-permute-start.10 = (f32[128,256]{1,0:T(8,128)S(1)}, f32[128,256]{1,0:T(8,128)S(1)}, u32[]{:S(2)}, u32[]{:S(2)}) collective-permute-start(f32[128,256]{1,0:T(8,128)S(1)} %get-tuple-element.52.refs_2_), channel_id=1, source_target_pairs={{0,4},{1,5},{2,6},{3,7},{4,0},{5,1},{6,2},{7,3},{8,12},{9,13},{10,... | collective-permute-start | bytes 393224 | tf_op jit(solution)/shard_map/ppermute | solution.py:300
  11.9 1.6 %collective-permute-start.5 = (f32[2,64,256]{2,1,0:T(8,128)S(1)}, f32[2,64,256]{2,1,0:T(8,128)S(1)}, u32[]{:S(2)}, u32[]{:S(2)}) collective-permute-start(f32[2,64,256]{2,1,0:T(8,128)S(1)} %get-tuple-element.48.refs_3_), channel_id=1, source_target_pairs={{0,2},{1,3},{2,0},{3,1},{4,6},{5,7},{6,4},{7,5},{8,10},{9,11},{10,... | collective-permute-start | bytes 393224 | tf_op jit(solution)/shard_map/ppermute | solution.py:300
  13.5 0.7 %collective-permute-start.7 = (f32[64,256]{1,0:T(8,128)S(1)}, f32[64,256]{1,0:T(8,128)S(1)}, u32[]{:S(2)}, u32[]{:S(2)}) collective-permute-start(f32[64,256]{1,0:T(8,128)S(1)} %get-tuple-element.47.refs_0_), channel_id=1, source_target_pairs={{0,6},{1,7},{2,4},{3,5},{4,2},{5,3},{6,0},{7,1},{8,14},{9,15},{10,... | collective-permute-start | bytes 196616 | tf_op jit(solution)/shard_map/ppermute | solution.py:300
  14.2 1.3 %collective-permute-start.6 = (f32[64,256]{1,0:T(8,128)S(1)}, f32[64,256]{1,0:T(8,128)S(1)}, u32[]{:S(2)}, u32[]{:S(2)}) collective-permute-start(f32[64,256]{1,0:T(8,128)S(1)} %get-tuple-element.47.refs_0_), channel_id=1, source_target_pairs={{0,4},{1,5},{2,6},{3,7},{4,0},{5,1},{6,2},{7,3},{8,12},{9,13},{10,... | collective-permute-start | bytes 196616 | tf_op jit(solution)/shard_map/ppermute | solution.py:300
  15.8 1.6 %collective-permute-start.17 = (f32[128,256]{1,0:T(8,128)S(1)}, f32[128,256]{1,0:T(8,128)S(1)}, u32[]{:S(2)}, u32[]{:S(2)}) collective-permute-start(f32[128,256]{1,0:T(8,128)S(1)} %get-tuple-element.58.refs_0_), channel_id=1, source_target_pairs={{0,2},{1,3},{2,0},{3,1},{4,6},{5,7},{6,4},{7,5},{8,10},{9,11},{10,... | collective-permute-start | bytes 393224 | tf_op jit(solution)/shard_map/ppermute | solution.py:300
  17.4 1.4 %collective-permute-done.7.refs_3_ = f32[64,256]{1,0:T(8,128)S(1)} collective-permute-done((f32[64,256]{1,0:T(8,128)S(1)}, f32[64,256]{1,0:T(8,128)S(1)}, u32[]{:S(2)}, u32[]{:S(2)}) %collective-permute-start.7) | collective-permute-done | bytes 65568 | tf_op jit(solution)/shard_map/ppermute | solution.py:300
  19.5 1.0 %collective-permute-start.15 = (f32[64,256]{1,0:T(8,128)S(1)}, f32[64,256]{1,0:T(8,128)S(1)}, u32[]{:S(2)}, u32[]{:S(2)}) collective-permute-start(f32[64,256]{1,0:T(8,128)S(1)} %get-tuple-element.57.refs_0_), channel_id=1, source_target_pairs={{0,2},{1,3},{2,0},{3,1},{4,6},{5,7},{6,4},{7,5},{8,10},{9,11},{10,... | collective-permute-start | bytes 196616 | tf_op jit(solution)/shard_map/ppermute | solution.py:300
  20.5 3.3 %collective-permute-start.14 = (f32[64,256]{1,0:T(8,128)S(1)}, f32[64,256]{1,0:T(8,128)S(1)}, u32[]{:S(2)}, u32[]{:S(2)}) collective-permute-start(f32[64,256]{1,0:T(8,128)S(1)} %get-tuple-element.56.refs_0_.refs_2_), channel_id=1, source_target_pairs={{0,12},{1,13},{2,14},{3,15},{4,8},{5,9},{6,10},{7,11},{8,4},{9,5},... | collective-permute-start | bytes 196616 | tf_op jit(solution)/shard_map/ppermute | solution.py:300
  23.9 1.1 %collective-permute-start.12 = (f32[64,256]{1,0:T(8,128)S(1)}, f32[64,256]{1,0:T(8,128)S(1)}, u32[]{:S(2)}, u32[]{:S(2)}) collective-permute-start(f32[64,256]{1,0:T(8,128)S(1)} %get-tuple-element.56.refs_0_.refs_2_), channel_id=1, source_target_pairs={{0,4},{1,5},{2,6},{3,7},{4,0},{5,1},{6,2},{7,3},{8,12},{9,13},{10,... | collective-permute-start | bytes 196616 | tf_op jit(solution)/shard_map/ppermute | solution.py:300
  25.0 1.0 %collective-permute-start.16 = (f32[64,256]{1,0:T(8,128)S(1)}, f32[64,256]{1,0:T(8,128)S(1)}, u32[]{:S(2)}, u32[]{:S(2)}) collective-permute-start(f32[64,256]{1,0:T(8,128)S(1)} %shard_map.61.refs_0_), channel_id=1, source_target_pairs={{0,4},{1,5},{2,6},{3,7},{4,0},{5,1},{6,2},{7,3},{8,12},{9,13},{10,... | collective-permute-start | bytes 196616 | tf_op jit(solution)/shard_map/ppermute | solution.py:300
  26.1 0.7 %collective-permute-done.14.refs_3_ = f32[64,256]{1,0:T(8,128)S(1)} collective-permute-done((f32[64,256]{1,0:T(8,128)S(1)}, f32[64,256]{1,0:T(8,128)S(1)}, u32[]{:S(2)}, u32[]{:S(2)}) %collective-permute-start.14) | collective-permute-done | bytes 65568 | tf_op jit(solution)/shard_map/ppermute | solution.py:300
  26.8 2.6 %collective-permute-done.13.refs_2_ = f32[64,256]{1,0:T(8,128)S(1)} collective-permute-done((f32[64,256]{1,0:T(8,128)S(1)}, f32[64,256]{1,0:T(8,128)S(1)}, u32[]{:S(2)}, u32[]{:S(2)}) %collective-permute-start.13) | collective-permute-done | bytes 65568 | tf_op jit(solution)/shard_map/ppermute | solution.py:300
  30.1 2.9 %collective-permute-start.21 = (f32[64,256]{1,0:T(8,128)S(1)}, f32[64,256]{1,0:T(8,128)S(1)}, u32[]{:S(2)}, u32[]{:S(2)}) collective-permute-start(f32[64,256]{1,0:T(8,128)S(1)} %shard_map.64.refs_3_.refs_0_), channel_id=1, source_target_pairs={{0,24},{1,25},{2,26},{3,27},{4,28},{5,29},{6,30},{7,31},{8,16},{9,... | collective-permute-start | bytes 196616 | tf_op jit(solution)/shard_map/ppermute | solution.py:302
  33.0 1.0 %collective-permute-start.20 = (f32[64,256]{1,0:T(8,128)S(1)}, f32[64,256]{1,0:T(8,128)S(1)}, u32[]{:S(2)}, u32[]{:S(2)}) collective-permute-start(f32[64,256]{1,0:T(8,128)S(1)} %shard_map.64.refs_3_.refs_0_), channel_id=1, source_target_pairs={{0,8},{1,9},{2,10},{3,11},{4,12},{5,13},{6,14},{7,15},{8,0},{9,1},... | collective-permute-start | bytes 196616 | tf_op jit(solution)/shard_map/ppermute | solution.py:300
  34.1 0.6 %collective-permute-start.22 = (f32[64,256]{1,0:T(8,128)S(1)}, f32[64,256]{1,0:T(8,128)S(1)}, u32[]{:S(2)}, u32[]{:S(2)}) collective-permute-start(f32[64,256]{1,0:T(8,128)S(1)} %shard_map.64.refs_3_.refs_0_), channel_id=1, source_target_pairs={{0,16},{1,17},{2,18},{3,19},{4,20},{5,21},{6,22},{7,23},{8,24},{9,... | collective-permute-start | bytes 196616 | tf_op jit(solution)/shard_map/ppermute | solution.py:302
  34.6 3.0 %collective-permute-done.21.refs_2_ = f32[64,256]{1,0:T(8,128)S(1)} collective-permute-done((f32[64,256]{1,0:T(8,128)S(1)}, f32[64,256]{1,0:T(8,128)S(1)}, u32[]{:S(2)}, u32[]{:S(2)}) %collective-permute-start.21) | collective-permute-done | bytes 65568 | tf_op jit(solution)/shard_map/ppermute | solution.py:302
  37.7 1.5 %collective-permute-done.20.refs_1_ = f32[64,256]{1,0:T(8,128)S(1)} collective-permute-done((f32[64,256]{1,0:T(8,128)S(1)}, f32[64,256]{1,0:T(8,128)S(1)}, u32[]{:S(2)}, u32[]{:S(2)}) %collective-permute-start.20) | collective-permute-done | bytes 65568 | tf_op jit(solution)/shard_map/ppermute | solution.py:300
  40.0 0.7 %collective-permute-done.23.other_ref = f32[64,256]{1,0:T(8,128)S(1)} collective-permute-done((f32[64,256]{1,0:T(8,128)S(1)}, f32[64,256]{1,0:T(8,128)S(1)}, u32[]{:S(2)}, u32[]{:S(2)}) %collective-permute-start.23) | collective-permute-done | bytes 65568 | tf_op jit(solution)/shard_map/ppermute | solution.py:300
  40.7 1.0 %shard_map.69 = f32[512,128]{1,0:T(8,128)} custom-call(f32[512,128]{1,0:T(8,128)S(1)} %shard_map.66.partial_ref, f32[64,256]{1,0:T(8,128)S(1)} %shard_map.68.own_ref, f32[64,256]{1,0:T(8,128)S(1)} %collective-permute-done.23.other_ref, bf16[5,512,256]{2,1,0:T(8,128)(2,1)S(1)} %copy-done.1), custom_call_target="tpu_custom_call" | custom-call | tf_op jit(solution)/shard_map/pallas_call | solution.py:243
  (54 shorter events, 6.5 us)
Async XLA Ops:
  1.5 1.5 %collective-permute-start = (f32[128,256]{1,0:T(8,128)S(1)}, f32[128,256]{1,0:T(8,128)S(1)}, u32[]{:S(2)}, u32[]{:S(2)}) collective-permute-start(f32[128,256]{1,0:T(8,128)S(1)} %get-tuple-element.33.refs_0_), channel_id=1, source_target_pairs={{0,1},{1,0},{2,3},{3,2},{4,5},{5,4},{6,7},{7,6},{8,9},{9,8},{10,11... | collective-permute-start | bytes 393224 | tf_op jit(solution)/shard_map/ppermute | solution.py:300
  3.3 1.3 %collective-permute-start.1 = (f32[64,256]{1,0:T(8,128)S(1)}, f32[64,256]{1,0:T(8,128)S(1)}, u32[]{:S(2)}, u32[]{:S(2)}) collective-permute-start(f32[64,256]{1,0:T(8,128)S(1)} %get-tuple-element.41), channel_id=1, source_target_pairs={{0,1},{1,0},{2,3},{3,2},{4,5},{5,4},{6,7},{7,6},{8,9},{9,8},{10,11... | collective-permute-start | bytes 196616 | tf_op jit(solution)/shard_map/ppermute | solution.py:300
  4.7 4.5 %collective-permute-start.8 = (f32[2,128,256]{2,1,0:T(8,128)S(1)}, f32[2,128,256]{2,1,0:T(8,128)S(1)}, u32[]{:S(2)}, u32[]{:S(2)}) collective-permute-start(f32[2,128,256]{2,1,0:T(8,128)S(1)} %get-tuple-element.50), channel_id=1, source_target_pairs={{0,1},{1,0},{2,3},{3,2},{4,5},{5,4},{6,7},{7,6},{8,9},{9,8},{10,11... | collective-permute-start | bytes 786440 | tf_op jit(solution)/shard_map/ppermute | solution.py:300
  5.1 6.3 %collective-permute-start.2 = (f32[64,256]{1,0:T(8,128)S(1)}, f32[64,256]{1,0:T(8,128)S(1)}, u32[]{:S(2)}, u32[]{:S(2)}) collective-permute-start(f32[64,256]{1,0:T(8,128)S(1)} %shard_map.50.refs_3_.refs_0_), channel_id=1, source_target_pairs={{0,2},{1,3},{2,0},{3,1},{4,6},{5,7},{6,4},{7,5},{8,10},{9,11},{10,... | collective-permute-start | bytes 196616 | tf_op jit(solution)/shard_map/ppermute | solution.py:300
  7.7 3.9 %collective-permute-start.3 = (f32[4,256,256]{2,1,0:T(8,128)S(1)}, f32[4,256,256]{2,1,0:T(8,128)S(1)}, u32[]{:S(2)}, u32[]{:S(2)}) collective-permute-start(f32[4,256,256]{2,1,0:T(8,128)S(1)} %get-tuple-element.44.refs_1_), channel_id=1, source_target_pairs={{0,1},{1,0},{2,3},{3,2},{4,5},{5,4},{6,7},{7,6},{8,9},{9,8},{10,11... | collective-permute-start | bytes 3145736 | tf_op jit(solution)/shard_map/ppermute | solution.py:300
  8.7 3.0 %collective-permute-start.4 = (f32[3,64,256]{2,1,0:T(8,128)S(1)}, f32[3,64,256]{2,1,0:T(8,128)S(1)}, u32[]{:S(2)}, u32[]{:S(2)}) collective-permute-start(f32[3,64,256]{2,1,0:T(8,128)S(1)} %get-tuple-element.46), channel_id=1, source_target_pairs={{0,1},{1,0},{2,3},{3,2},{4,5},{5,4},{6,7},{7,6},{8,9},{9,8},{10,11... | collective-permute-start | bytes 589832 | tf_op jit(solution)/shard_map/ppermute | solution.py:300
  9.2 6.5 %collective-permute-start.9 = (f32[128,256]{1,0:T(8,128)S(1)}, f32[128,256]{1,0:T(8,128)S(1)}, u32[]{:S(2)}, u32[]{:S(2)}) collective-permute-start(f32[128,256]{1,0:T(8,128)S(1)} %get-tuple-element.51.refs_0_), channel_id=1, source_target_pairs={{0,2},{1,3},{2,0},{3,1},{4,6},{5,7},{6,4},{7,5},{8,10},{9,11},{10,... | collective-permute-start | bytes 393224 | tf_op jit(solution)/shard_map/ppermute | solution.py:300
  9.3 6.4 %collective-permute-start.10 = (f32[128,256]{1,0:T(8,128)S(1)}, f32[128,256]{1,0:T(8,128)S(1)}, u32[]{:S(2)}, u32[]{:S(2)}) collective-permute-start(f32[128,256]{1,0:T(8,128)S(1)} %get-tuple-element.52.refs_2_), channel_id=1, source_target_pairs={{0,4},{1,5},{2,6},{3,7},{4,0},{5,1},{6,2},{7,3},{8,12},{9,13},{10,... | collective-permute-start | bytes 393224 | tf_op jit(solution)/shard_map/ppermute | solution.py:300
  11.9 7.0 %collective-permute-start.5 = (f32[2,64,256]{2,1,0:T(8,128)S(1)}, f32[2,64,256]{2,1,0:T(8,128)S(1)}, u32[]{:S(2)}, u32[]{:S(2)}) collective-permute-start(f32[2,64,256]{2,1,0:T(8,128)S(1)} %get-tuple-element.48.refs_3_), channel_id=1, source_target_pairs={{0,2},{1,3},{2,0},{3,1},{4,6},{5,7},{6,4},{7,5},{8,10},{9,11},{10,... | collective-permute-start | bytes 393224 | tf_op jit(solution)/shard_map/ppermute | solution.py:300
  13.5 5.3 %collective-permute-start.7 = (f32[64,256]{1,0:T(8,128)S(1)}, f32[64,256]{1,0:T(8,128)S(1)}, u32[]{:S(2)}, u32[]{:S(2)}) collective-permute-start(f32[64,256]{1,0:T(8,128)S(1)} %get-tuple-element.47.refs_0_), channel_id=1, source_target_pairs={{0,6},{1,7},{2,4},{3,5},{4,2},{5,3},{6,0},{7,1},{8,14},{9,15},{10,... | collective-permute-start | bytes 196616 | tf_op jit(solution)/shard_map/ppermute | solution.py:300
  14.2 4.6 %collective-permute-start.6 = (f32[64,256]{1,0:T(8,128)S(1)}, f32[64,256]{1,0:T(8,128)S(1)}, u32[]{:S(2)}, u32[]{:S(2)}) collective-permute-start(f32[64,256]{1,0:T(8,128)S(1)} %get-tuple-element.47.refs_0_), channel_id=1, source_target_pairs={{0,4},{1,5},{2,6},{3,7},{4,0},{5,1},{6,2},{7,3},{8,12},{9,13},{10,... | collective-permute-start | bytes 196616 | tf_op jit(solution)/shard_map/ppermute | solution.py:300
  15.8 3.5 %collective-permute-start.11 = (f32[128,256]{1,0:T(8,128)S(1)}, f32[128,256]{1,0:T(8,128)S(1)}, u32[]{:S(2)}, u32[]{:S(2)}) collective-permute-start(f32[128,256]{1,0:T(8,128)S(1)} %get-tuple-element.54.refs_1_), channel_id=1, source_target_pairs={{0,1},{1,0},{2,3},{3,2},{4,5},{5,4},{6,7},{7,6},{8,9},{9,8},{10,11... | collective-permute-start | bytes 393224 | tf_op jit(solution)/shard_map/ppermute | solution.py:300
  15.8 10.1 %collective-permute-start.17 = (f32[128,256]{1,0:T(8,128)S(1)}, f32[128,256]{1,0:T(8,128)S(1)}, u32[]{:S(2)}, u32[]{:S(2)}) collective-permute-start(f32[128,256]{1,0:T(8,128)S(1)} %get-tuple-element.58.refs_0_), channel_id=1, source_target_pairs={{0,2},{1,3},{2,0},{3,1},{4,6},{5,7},{6,4},{7,5},{8,10},{9,11},{10,... | collective-permute-start | bytes 393224 | tf_op jit(solution)/shard_map/ppermute | solution.py:300
  19.5 5.4 %collective-permute-start.15 = (f32[64,256]{1,0:T(8,128)S(1)}, f32[64,256]{1,0:T(8,128)S(1)}, u32[]{:S(2)}, u32[]{:S(2)}) collective-permute-start(f32[64,256]{1,0:T(8,128)S(1)} %get-tuple-element.57.refs_0_), channel_id=1, source_target_pairs={{0,2},{1,3},{2,0},{3,1},{4,6},{5,7},{6,4},{7,5},{8,10},{9,11},{10,... | collective-permute-start | bytes 196616 | tf_op jit(solution)/shard_map/ppermute | solution.py:300
  20.5 6.2 %collective-permute-start.14 = (f32[64,256]{1,0:T(8,128)S(1)}, f32[64,256]{1,0:T(8,128)S(1)}, u32[]{:S(2)}, u32[]{:S(2)}) collective-permute-start(f32[64,256]{1,0:T(8,128)S(1)} %get-tuple-element.56.refs_0_.refs_2_), channel_id=1, source_target_pairs={{0,12},{1,13},{2,14},{3,15},{4,8},{5,9},{6,10},{7,11},{8,4},{9,5},... | collective-permute-start | bytes 196616 | tf_op jit(solution)/shard_map/ppermute | solution.py:300
  23.9 5.5 %collective-permute-start.13 = (f32[64,256]{1,0:T(8,128)S(1)}, f32[64,256]{1,0:T(8,128)S(1)}, u32[]{:S(2)}, u32[]{:S(2)}) collective-permute-start(f32[64,256]{1,0:T(8,128)S(1)} %get-tuple-element.56.refs_0_.refs_2_), channel_id=1, source_target_pairs={{0,8},{1,9},{2,10},{3,11},{4,12},{5,13},{6,14},{7,15},{8,0},{9,1},... | collective-permute-start | bytes 196616 | tf_op jit(solution)/shard_map/ppermute | solution.py:300
  23.9 5.5 %collective-permute-start.12 = (f32[64,256]{1,0:T(8,128)S(1)}, f32[64,256]{1,0:T(8,128)S(1)}, u32[]{:S(2)}, u32[]{:S(2)}) collective-permute-start(f32[64,256]{1,0:T(8,128)S(1)} %get-tuple-element.56.refs_0_.refs_2_), channel_id=1, source_target_pairs={{0,4},{1,5},{2,6},{3,7},{4,0},{5,1},{6,2},{7,3},{8,12},{9,13},{10,... | collective-permute-start | bytes 196616 | tf_op jit(solution)/shard_map/ppermute | solution.py:300
  25.0 4.9 %collective-permute-start.16 = (f32[64,256]{1,0:T(8,128)S(1)}, f32[64,256]{1,0:T(8,128)S(1)}, u32[]{:S(2)}, u32[]{:S(2)}) collective-permute-start(f32[64,256]{1,0:T(8,128)S(1)} %shard_map.61.refs_0_), channel_id=1, source_target_pairs={{0,4},{1,5},{2,6},{3,7},{4,0},{5,1},{6,2},{7,3},{8,12},{9,13},{10,... | collective-permute-start | bytes 196616 | tf_op jit(solution)/shard_map/ppermute | solution.py:300
  26.0 3.9 %collective-permute-start.18 = (f32[128,256]{1,0:T(8,128)S(1)}, f32[128,256]{1,0:T(8,128)S(1)}, u32[]{:S(2)}, u32[]{:S(2)}) collective-permute-start(f32[128,256]{1,0:T(8,128)S(1)} %shard_map.63.refs_2_), channel_id=1, source_target_pairs={{0,1},{1,0},{2,3},{3,2},{4,5},{5,4},{6,7},{7,6},{8,9},{9,8},{10,11... | collective-permute-start | bytes 393224 | tf_op jit(solution)/shard_map/ppermute | solution.py:300
  30.1 7.6 %collective-permute-start.21 = (f32[64,256]{1,0:T(8,128)S(1)}, f32[64,256]{1,0:T(8,128)S(1)}, u32[]{:S(2)}, u32[]{:S(2)}) collective-permute-start(f32[64,256]{1,0:T(8,128)S(1)} %shard_map.64.refs_3_.refs_0_), channel_id=1, source_target_pairs={{0,24},{1,25},{2,26},{3,27},{4,28},{5,29},{6,30},{7,31},{8,16},{9,... | collective-permute-start | bytes 196616 | tf_op jit(solution)/shard_map/ppermute | solution.py:302
  33.0 6.1 %collective-permute-start.20 = (f32[64,256]{1,0:T(8,128)S(1)}, f32[64,256]{1,0:T(8,128)S(1)}, u32[]{:S(2)}, u32[]{:S(2)}) collective-permute-start(f32[64,256]{1,0:T(8,128)S(1)} %shard_map.64.refs_3_.refs_0_), channel_id=1, source_target_pairs={{0,8},{1,9},{2,10},{3,11},{4,12},{5,13},{6,14},{7,15},{8,0},{9,1},... | collective-permute-start | bytes 196616 | tf_op jit(solution)/shard_map/ppermute | solution.py:300
  34.1 5.1 %collective-permute-start.22 = (f32[64,256]{1,0:T(8,128)S(1)}, f32[64,256]{1,0:T(8,128)S(1)}, u32[]{:S(2)}, u32[]{:S(2)}) collective-permute-start(f32[64,256]{1,0:T(8,128)S(1)} %shard_map.64.refs_3_.refs_0_), channel_id=1, source_target_pairs={{0,16},{1,17},{2,18},{3,19},{4,20},{5,21},{6,22},{7,23},{8,24},{9,... | collective-permute-start | bytes 196616 | tf_op jit(solution)/shard_map/ppermute | solution.py:302
  34.6 4.8 %collective-permute-start.19 = (f32[3,64,256]{2,1,0:T(8,128)S(1)}, f32[3,64,256]{2,1,0:T(8,128)S(1)}, u32[]{:S(2)}, u32[]{:S(2)}) collective-permute-start(f32[3,64,256]{2,1,0:T(8,128)S(1)} %shard_map.65.refs_3_), channel_id=1, source_target_pairs={{0,1},{1,0},{2,3},{3,2},{4,5},{5,4},{6,7},{7,6},{8,9},{9,8},{10,11... | collective-permute-start | bytes 589832 | tf_op jit(solution)/shard_map/ppermute | solution.py:300
  39.4 1.3 %collective-permute-start.23 = (f32[64,256]{1,0:T(8,128)S(1)}, f32[64,256]{1,0:T(8,128)S(1)}, u32[]{:S(2)}, u32[]{:S(2)}) collective-permute-start(f32[64,256]{1,0:T(8,128)S(1)} %shard_map.68.own_ref), channel_id=1, source_target_pairs={{0,1},{1,0},{2,3},{3,2},{4,5},{5,4},{6,7},{7,6},{8,9},{9,8},{10,11... | collective-permute-start | bytes 196616 | tf_op jit(solution)/shard_map/ppermute | solution.py:300
  (3 other events, 8.7 us)

commit v5 on v3

--- a/solution.py
+++ b/solution.py
@@ -312,11 +312,11 @@
     sum1 = added(keep, got, after=[keep_cross])
     sums, sums_send = run(
         later_sums_kernel, [(3,) + block, (3,) + block], current, weights0, basis_u, basis_v,
-        after=[sum1], flops=2 * 10**9,
+        after=[sum1], flops=4 * 10**9,
     )
 
     across = traded(sum1, 2)
-    cross_got = traded(tied(send_cross, sum1), 1)
+    cross_got = traded(send_cross, 1)
     early_got = traded(tied(early, sum1), 1)
     sums_got = traded(sums_send, 1)
     cross32, cross43 = run(mix_kernel, [rows, rows], keep_cross, cross_got, flops=2 * 10**9)

time: 41.9 us -> 41.7 us (level)
  no operation moved by 1% of the time
where the time goes in v5:
time: 41.7 us; the launch traced here: 41.6 us
  starting transfers between devices  23.2 us (56%)
  waiting for transfers between devices  11.1 us (27%)
  Pallas kernels  7.05 us (17%)
    ppermute x22, starting transfers between devices, traded(): lax.ppermute(value, 'sub', [(source, source ^ mask) for source in range(l...  19.8 us
    ppermute x22, waiting for transfers between devices, traded(): lax.ppermute(value, 'sub', [(source, source ^ mask) for source in range(l...  8.09 us
    pallas_call x21, Pallas kernels, run(): pl.pallas_call(lambda *refs: kernel(*refs[:len(args)], *refs[len(args) +...  4.55 us
    ppermute x2, starting transfers between devices, traded(): lax.ppermute(value, AXES, [(source, source ^ mask) for source in range(de...  3.4 us
    ppermute x2, waiting for transfers between devices, traded(): lax.ppermute(value, AXES, [(source, source ^ mask) for source in range(de...  3 us
    pallas_call x1, Pallas kernels, run_start(): pl.pallas_call(start_kernel, out_shape=outs, in_specs=[pl.BlockSpec(memor...  1.47 us
    pallas_call x1, Pallas kernels, run_last(): pl.pallas_call(functools.partial(last_kernel, level, chunks), out_shape=j...  1.02 us
  transfers between devices with their start and end apart: 24, of which 10 were waited for; matrix products, arithmetic and copies ran while one was open for 0% of the time, Pallas kernels for 9%

profile of v5, /device:TPU:0, one launch (start us, length us, event | category | flops | bytes accessed | tf_op | source)
XLA Modules:
  0.0 41.6 jit_solution(8602145899751135067)
XLA Ops:
  0.0 1.5 %shard_map.46 = (f32[128,512]{1,0:T(8,128)S(1)}, f32[128,256]{1,0:T(8,128)S(1)}, bf16[512,256]{1,0:T(8,128)(2,1)S(1)}, bf16[512,256]{1,0:T(8,128)(2,1)S(1)}, bf1...) custom-call(f32[512,128]{1,0:T(8,128)} %right_hbm.1, bf16[5,512,256]{2,1,0:T(8,128)(2,1)} %u_ref.1, ...), custom_call_target="tpu_custom_call" | custom-call | tf_op jit(solution)/shard_map/pallas_call | solution.py:275
  2.3 0.7 %collective-permute-done.refs_1_ = f32[128,256]{1,0:T(8,128)S(1)} collective-permute-done((f32[128,256]{1,0:T(8,128)S(1)}, f32[128,256]{1,0:T(8,128)S(1)}, u32[]{:S(2)}, u32[]{:S(2)}) %collective-permute-start) | collective-permute-done | bytes 131104 | tf_op jit(solution)/shard_map/ppermute | solution.py:291
  4.0 0.6 %shard_map.49 = (f32[4,256,256]{2,1,0:T(8,128)S(1)}, f32[2,128,256]{2,1,0:T(8,128)S(1)}, f32[2,128,256]{2,1,0:T(8,128)S(1)}) custom-call(bf16[5,512,256]{2,1,0:T(8,128)(2,1)S(1)} %copy-done.1, bf16[5,512,256]{2,1,0:T(8,128)(2,1)S(1)} %copy-done.2, f32[128,256]{1,0:T(8,128)S(1)} %get-tuple-element.40.refs_2_.refs_1_), custom_call_target="tpu_custom_call" | custom-call | flops 2000000000 | tf_op jit(solution)/shard_map/pallas_call | solution.py:246
  4.9 2.9 %collective-permute-start.2 = (f32[64,256]{1,0:T(8,128)S(1)}, f32[64,256]{1,0:T(8,128)S(1)}, u32[]{:S(2)}, u32[]{:S(2)}) collective-permute-start(f32[64,256]{1,0:T(8,128)S(1)} %shard_map.50.refs_0_.refs_4_), channel_id=1, source_target_pairs={{0,2},{1,3},{2,0},{3,1},{4,6},{5,7},{6,4},{7,5},{8,10},{9,11},{10,... | collective-permute-start | bytes 196616 | tf_op jit(solution)/shard_map/ppermute | solution.py:291
  7.8 0.6 %shard_map.52 = (f32[3,64,256]{2,1,0:T(8,128)S(1)}, f32[3,64,256]{2,1,0:T(8,128)S(1)}) custom-call(f32[128,512]{1,0:T(8,128)S(1)} %get-tuple-element.35.refs_0_, f32[128,256]{1,0:T(8,128)S(1)} %get-tuple-element.40.refs_2_.refs_1_, bf16[5,512,256]{2,1,0:T(8,128)(2,1)S(1)} %copy-done.1, bf16[5,512,256]{2,1,0:T(8,128)(2,1)S(1)} %copy-done.2, ...), custom_call_target="tpu_custom_call" | custom-call | flops 4000000000 | tf_op jit(solution)/shard_map/pallas_call | solution.py:246
  8.4 0.6 %collective-permute-start.4 = (f32[3,64,256]{2,1,0:T(8,128)S(1)}, f32[3,64,256]{2,1,0:T(8,128)S(1)}, u32[]{:S(2)}, u32[]{:S(2)}) collective-permute-start(f32[3,64,256]{2,1,0:T(8,128)S(1)} %get-tuple-element.47), channel_id=1, source_target_pairs={{0,1},{1,0},{2,3},{3,2},{4,5},{5,4},{6,7},{7,6},{8,9},{9,8},{10,11... | collective-permute-start | bytes 589832 | tf_op jit(solution)/shard_map/ppermute | solution.py:291
  9.2 2.0 %collective-permute-start.10 = (f32[128,256]{1,0:T(8,128)S(1)}, f32[128,256]{1,0:T(8,128)S(1)}, u32[]{:S(2)}, u32[]{:S(2)}) collective-permute-start(f32[128,256]{1,0:T(8,128)S(1)} %get-tuple-element.52.refs_2_), channel_id=1, source_target_pairs={{0,4},{1,5},{2,6},{3,7},{4,0},{5,1},{6,2},{7,3},{8,12},{9,13},{10,... | collective-permute-start | bytes 393224 | tf_op jit(solution)/shard_map/ppermute | solution.py:291
  11.7 1.6 %collective-permute-start.5 = (f32[2,64,256]{2,1,0:T(8,128)S(1)}, f32[2,64,256]{2,1,0:T(8,128)S(1)}, u32[]{:S(2)}, u32[]{:S(2)}) collective-permute-start(f32[2,64,256]{2,1,0:T(8,128)S(1)} %get-tuple-element.49.refs_3_), channel_id=1, source_target_pairs={{0,2},{1,3},{2,0},{3,1},{4,6},{5,7},{6,4},{7,5},{8,10},{9,11},{10,... | collective-permute-start | bytes 393224 | tf_op jit(solution)/shard_map/ppermute | solution.py:291
  13.3 0.9 %collective-permute-start.7 = (f32[64,256]{1,0:T(8,128)S(1)}, f32[64,256]{1,0:T(8,128)S(1)}, u32[]{:S(2)}, u32[]{:S(2)}) collective-permute-start(f32[64,256]{1,0:T(8,128)S(1)} %get-tuple-element.48.refs_0_), channel_id=1, source_target_pairs={{0,6},{1,7},{2,4},{3,5},{4,2},{5,3},{6,0},{7,1},{8,14},{9,15},{10,... | collective-permute-start | bytes 196616 | tf_op jit(solution)/shard_map/ppermute | solution.py:291
  14.2 1.1 %collective-permute-start.6 = (f32[64,256]{1,0:T(8,128)S(1)}, f32[64,256]{1,0:T(8,128)S(1)}, u32[]{:S(2)}, u32[]{:S(2)}) collective-permute-start(f32[64,256]{1,0:T(8,128)S(1)} %get-tuple-element.48.refs_0_), channel_id=1, source_target_pairs={{0,4},{1,5},{2,6},{3,7},{4,0},{5,1},{6,2},{7,3},{8,12},{9,13},{10,... | collective-permute-start | bytes 196616 | tf_op jit(solution)/shard_map/ppermute | solution.py:291
  15.6 1.6 %collective-permute-start.17 = (f32[128,256]{1,0:T(8,128)S(1)}, f32[128,256]{1,0:T(8,128)S(1)}, u32[]{:S(2)}, u32[]{:S(2)}) collective-permute-start(f32[128,256]{1,0:T(8,128)S(1)} %get-tuple-element.58.refs_0_), channel_id=1, source_target_pairs={{0,2},{1,3},{2,0},{3,1},{4,6},{5,7},{6,4},{7,5},{8,10},{9,11},{10,... | collective-permute-start | bytes 393224 | tf_op jit(solution)/shard_map/ppermute | solution.py:291
  17.2 1.4 %collective-permute-done.7.refs_3_ = f32[64,256]{1,0:T(8,128)S(1)} collective-permute-done((f32[64,256]{1,0:T(8,128)S(1)}, f32[64,256]{1,0:T(8,128)S(1)}, u32[]{:S(2)}, u32[]{:S(2)}) %collective-permute-start.7) | collective-permute-done | bytes 65568 | tf_op jit(solution)/shard_map/ppermute | solution.py:291
  19.2 1.3 %collective-permute-start.15 = (f32[64,256]{1,0:T(8,128)S(1)}, f32[64,256]{1,0:T(8,128)S(1)}, u32[]{:S(2)}, u32[]{:S(2)}) collective-permute-start(f32[64,256]{1,0:T(8,128)S(1)} %get-tuple-element.57.refs_0_), channel_id=1, source_target_pairs={{0,2},{1,3},{2,0},{3,1},{4,6},{5,7},{6,4},{7,5},{8,10},{9,11},{10,... | collective-permute-start | bytes 196616 | tf_op jit(solution)/shard_map/ppermute | solution.py:291
  20.5 3.1 %collective-permute-start.14 = (f32[64,256]{1,0:T(8,128)S(1)}, f32[64,256]{1,0:T(8,128)S(1)}, u32[]{:S(2)}, u32[]{:S(2)}) collective-permute-start(f32[64,256]{1,0:T(8,128)S(1)} %get-tuple-element.56.refs_0_.refs_2_), channel_id=1, source_target_pairs={{0,12},{1,13},{2,14},{3,15},{4,8},{5,9},{6,10},{7,11},{8,4},{9,5},... | collective-permute-start | bytes 196616 | tf_op jit(solution)/shard_map/ppermute | solution.py:291
  23.7 1.3 %collective-permute-start.12 = (f32[64,256]{1,0:T(8,128)S(1)}, f32[64,256]{1,0:T(8,128)S(1)}, u32[]{:S(2)}, u32[]{:S(2)}) collective-permute-start(f32[64,256]{1,0:T(8,128)S(1)} %get-tuple-element.56.refs_0_.refs_2_), channel_id=1, source_target_pairs={{0,4},{1,5},{2,6},{3,7},{4,0},{5,1},{6,2},{7,3},{8,12},{9,13},{10,... | collective-permute-start | bytes 196616 | tf_op jit(solution)/shard_map/ppermute | solution.py:291
  24.9 0.8 %collective-permute-start.16 = (f32[64,256]{1,0:T(8,128)S(1)}, f32[64,256]{1,0:T(8,128)S(1)}, u32[]{:S(2)}, u32[]{:S(2)}) collective-permute-start(f32[64,256]{1,0:T(8,128)S(1)} %shard_map.60.refs_0_), channel_id=1, source_target_pairs={{0,4},{1,5},{2,6},{3,7},{4,0},{5,1},{6,2},{7,3},{8,12},{9,13},{10,... | collective-permute-start | bytes 196616 | tf_op jit(solution)/shard_map/ppermute | solution.py:291
  25.9 0.9 %collective-permute-done.14.refs_3_ = f32[64,256]{1,0:T(8,128)S(1)} collective-permute-done((f32[64,256]{1,0:T(8,128)S(1)}, f32[64,256]{1,0:T(8,128)S(1)}, u32[]{:S(2)}, u32[]{:S(2)}) %collective-permute-start.14) | collective-permute-done | bytes 65568 | tf_op jit(solution)/shard_map/ppermute | solution.py:291
  26.8 2.5 %collective-permute-done.13.refs_2_ = f32[64,256]{1,0:T(8,128)S(1)} collective-permute-done((f32[64,256]{1,0:T(8,128)S(1)}, f32[64,256]{1,0:T(8,128)S(1)}, u32[]{:S(2)}, u32[]{:S(2)}) %collective-permute-start.13) | collective-permute-done | bytes 65568 | tf_op jit(solution)/shard_map/ppermute | solution.py:291
  30.0 2.8 %collective-permute-start.21 = (f32[64,256]{1,0:T(8,128)S(1)}, f32[64,256]{1,0:T(8,128)S(1)}, u32[]{:S(2)}, u32[]{:S(2)}) collective-permute-start(f32[64,256]{1,0:T(8,128)S(1)} %shard_map.63.refs_3_.refs_0_), channel_id=1, source_target_pairs={{0,24},{1,25},{2,26},{3,27},{4,28},{5,29},{6,30},{7,31},{8,16},{9,... | collective-permute-start | bytes 196616 | tf_op jit(solution)/shard_map/ppermute | solution.py:293
  32.8 1.1 %collective-permute-start.20 = (f32[64,256]{1,0:T(8,128)S(1)}, f32[64,256]{1,0:T(8,128)S(1)}, u32[]{:S(2)}, u32[]{:S(2)}) collective-permute-start(f32[64,256]{1,0:T(8,128)S(1)} %shard_map.63.refs_3_.refs_0_), channel_id=1, source_target_pairs={{0,8},{1,9},{2,10},{3,11},{4,12},{5,13},{6,14},{7,15},{8,0},{9,1},... | collective-permute-start | bytes 196616 | tf_op jit(solution)/shard_map/ppermute | solution.py:291
  34.5 3.0 %collective-permute-done.21.refs_2_ = f32[64,256]{1,0:T(8,128)S(1)} collective-permute-done((f32[64,256]{1,0:T(8,128)S(1)}, f32[64,256]{1,0:T(8,128)S(1)}, u32[]{:S(2)}, u32[]{:S(2)}) %collective-permute-start.21) | collective-permute-done | bytes 65568 | tf_op jit(solution)/shard_map/ppermute | solution.py:293
  37.5 1.5 %collective-permute-done.20.refs_1_ = f32[64,256]{1,0:T(8,128)S(1)} collective-permute-done((f32[64,256]{1,0:T(8,128)S(1)}, f32[64,256]{1,0:T(8,128)S(1)}, u32[]{:S(2)}, u32[]{:S(2)}) %collective-permute-start.20) | collective-permute-done | bytes 65568 | tf_op jit(solution)/shard_map/ppermute | solution.py:291
  39.9 0.7 %collective-permute-done.23.other_ref = f32[64,256]{1,0:T(8,128)S(1)} collective-permute-done((f32[64,256]{1,0:T(8,128)S(1)}, f32[64,256]{1,0:T(8,128)S(1)}, u32[]{:S(2)}, u32[]{:S(2)}) %collective-permute-start.23) | collective-permute-done | bytes 65568 | tf_op jit(solution)/shard_map/ppermute | solution.py:291
  40.5 1.0 %shard_map.68 = f32[512,128]{1,0:T(8,128)} custom-call(f32[512,128]{1,0:T(8,128)S(1)} %shard_map.65.partial_ref, f32[64,256]{1,0:T(8,128)S(1)} %shard_map.67.own_ref, f32[64,256]{1,0:T(8,128)S(1)} %collective-permute-done.23.other_ref, bf16[5,512,256]{2,1,0:T(8,128)(2,1)S(1)} %copy-done.1), custom_call_target="tpu_custom_call" | custom-call | tf_op jit(solution)/shard_map/pallas_call | solution.py:234
  (53 shorter events, 5.9 us)
Async XLA Ops:
  1.5 1.5 %collective-permute-start = (f32[128,256]{1,0:T(8,128)S(1)}, f32[128,256]{1,0:T(8,128)S(1)}, u32[]{:S(2)}, u32[]{:S(2)}) collective-permute-start(f32[128,256]{1,0:T(8,128)S(1)} %get-tuple-element.33.refs_0_), channel_id=1, source_target_pairs={{0,1},{1,0},{2,3},{3,2},{4,5},{5,4},{6,7},{7,6},{8,9},{9,8},{10,11... | collective-permute-start | bytes 393224 | tf_op jit(solution)/shard_map/ppermute | solution.py:291
  3.5 1.3 %collective-permute-start.1 = (f32[64,256]{1,0:T(8,128)S(1)}, f32[64,256]{1,0:T(8,128)S(1)}, u32[]{:S(2)}, u32[]{:S(2)}) collective-permute-start(f32[64,256]{1,0:T(8,128)S(1)} %get-tuple-element.42), channel_id=1, source_target_pairs={{0,1},{1,0},{2,3},{3,2},{4,5},{5,4},{6,7},{7,6},{8,9},{9,8},{10,11... | collective-permute-start | bytes 196616 | tf_op jit(solution)/shard_map/ppermute | solution.py:291
  4.6 4.4 %collective-permute-start.8 = (f32[2,128,256]{2,1,0:T(8,128)S(1)}, f32[2,128,256]{2,1,0:T(8,128)S(1)}, u32[]{:S(2)}, u32[]{:S(2)}) collective-permute-start(f32[2,128,256]{2,1,0:T(8,128)S(1)} %get-tuple-element.50), channel_id=1, source_target_pairs={{0,1},{1,0},{2,3},{3,2},{4,5},{5,4},{6,7},{7,6},{8,9},{9,8},{10,11... | collective-permute-start | bytes 786440 | tf_op jit(solution)/shard_map/ppermute | solution.py:291
  4.9 6.3 %collective-permute-start.2 = (f32[64,256]{1,0:T(8,128)S(1)}, f32[64,256]{1,0:T(8,128)S(1)}, u32[]{:S(2)}, u32[]{:S(2)}) collective-permute-start(f32[64,256]{1,0:T(8,128)S(1)} %shard_map.50.refs_0_.refs_4_), channel_id=1, source_target_pairs={{0,2},{1,3},{2,0},{3,1},{4,6},{5,7},{6,4},{7,5},{8,10},{9,11},{10,... | collective-permute-start | bytes 196616 | tf_op jit(solution)/shard_map/ppermute | solution.py:291
  7.8 3.7 %collective-permute-start.3 = (f32[4,256,256]{2,1,0:T(8,128)S(1)}, f32[4,256,256]{2,1,0:T(8,128)S(1)}, u32[]{:S(2)}, u32[]{:S(2)}) collective-permute-start(f32[4,256,256]{2,1,0:T(8,128)S(1)} %get-tuple-element.45.refs_1_), channel_id=1, source_target_pairs={{0,1},{1,0},{2,3},{3,2},{4,5},{5,4},{6,7},{7,6},{8,9},{9,8},{10,11... | collective-permute-start | bytes 3145736 | tf_op jit(solution)/shard_map/ppermute | solution.py:291
  8.4 3.0 %collective-permute-start.4 = (f32[3,64,256]{2,1,0:T(8,128)S(1)}, f32[3,64,256]{2,1,0:T(8,128)S(1)}, u32[]{:S(2)}, u32[]{:S(2)}) collective-permute-start(f32[3,64,256]{2,1,0:T(8,128)S(1)} %get-tuple-element.47), channel_id=1, source_target_pairs={{0,1},{1,0},{2,3},{3,2},{4,5},{5,4},{6,7},{7,6},{8,9},{9,8},{10,11... | collective-permute-start | bytes 589832 | tf_op jit(solution)/shard_map/ppermute | solution.py:291
  9.0 6.5 %collective-permute-start.9 = (f32[128,256]{1,0:T(8,128)S(1)}, f32[128,256]{1,0:T(8,128)S(1)}, u32[]{:S(2)}, u32[]{:S(2)}) collective-permute-start(f32[128,256]{1,0:T(8,128)S(1)} %get-tuple-element.51.refs_0_), channel_id=1, source_target_pairs={{0,2},{1,3},{2,0},{3,1},{4,6},{5,7},{6,4},{7,5},{8,10},{9,11},{10,... | collective-permute-start | bytes 393224 | tf_op jit(solution)/shard_map/ppermute | solution.py:291
  9.2 6.3 %collective-permute-start.10 = (f32[128,256]{1,0:T(8,128)S(1)}, f32[128,256]{1,0:T(8,128)S(1)}, u32[]{:S(2)}, u32[]{:S(2)}) collective-permute-start(f32[128,256]{1,0:T(8,128)S(1)} %get-tuple-element.52.refs_2_), channel_id=1, source_target_pairs={{0,4},{1,5},{2,6},{3,7},{4,0},{5,1},{6,2},{7,3},{8,12},{9,13},{10,... | collective-permute-start | bytes 393224 | tf_op jit(solution)/shard_map/ppermute | solution.py:291
  11.7 7.0 %collective-permute-start.5 = (f32[2,64,256]{2,1,0:T(8,128)S(1)}, f32[2,64,256]{2,1,0:T(8,128)S(1)}, u32[]{:S(2)}, u32[]{:S(2)}) collective-permute-start(f32[2,64,256]{2,1,0:T(8,128)S(1)} %get-tuple-element.49.refs_3_), channel_id=1, source_target_pairs={{0,2},{1,3},{2,0},{3,1},{4,6},{5,7},{6,4},{7,5},{8,10},{9,11},{10,... | collective-permute-start | bytes 393224 | tf_op jit(solution)/shard_map/ppermute | solution.py:291
  13.3 5.3 %collective-permute-start.7 = (f32[64,256]{1,0:T(8,128)S(1)}, f32[64,256]{1,0:T(8,128)S(1)}, u32[]{:S(2)}, u32[]{:S(2)}) collective-permute-start(f32[64,256]{1,0:T(8,128)S(1)} %get-tuple-element.48.refs_0_), channel_id=1, source_target_pairs={{0,6},{1,7},{2,4},{3,5},{4,2},{5,3},{6,0},{7,1},{8,14},{9,15},{10,... | collective-permute-start | bytes 196616 | tf_op jit(solution)/shard_map/ppermute | solution.py:291
  14.2 4.4 %collective-permute-start.6 = (f32[64,256]{1,0:T(8,128)S(1)}, f32[64,256]{1,0:T(8,128)S(1)}, u32[]{:S(2)}, u32[]{:S(2)}) collective-permute-start(f32[64,256]{1,0:T(8,128)S(1)} %get-tuple-element.48.refs_0_), channel_id=1, source_target_pairs={{0,4},{1,5},{2,6},{3,7},{4,0},{5,1},{6,2},{7,3},{8,12},{9,13},{10,... | collective-permute-start | bytes 196616 | tf_op jit(solution)/shard_map/ppermute | solution.py:291
  15.6 3.4 %collective-permute-start.11 = (f32[128,256]{1,0:T(8,128)S(1)}, f32[128,256]{1,0:T(8,128)S(1)}, u32[]{:S(2)}, u32[]{:S(2)}) collective-permute-start(f32[128,256]{1,0:T(8,128)S(1)} %get-tuple-element.54.refs_1_), channel_id=1, source_target_pairs={{0,1},{1,0},{2,3},{3,2},{4,5},{5,4},{6,7},{7,6},{8,9},{9,8},{10,11... | collective-permute-start | bytes 393224 | tf_op jit(solution)/shard_map/ppermute | solution.py:291
  15.6 10.1 %collective-permute-start.17 = (f32[128,256]{1,0:T(8,128)S(1)}, f32[128,256]{1,0:T(8,128)S(1)}, u32[]{:S(2)}, u32[]{:S(2)}) collective-permute-start(f32[128,256]{1,0:T(8,128)S(1)} %get-tuple-element.58.refs_0_), channel_id=1, source_target_pairs={{0,2},{1,3},{2,0},{3,1},{4,6},{5,7},{6,4},{7,5},{8,10},{9,11},{10,... | collective-permute-start | bytes 393224 | tf_op jit(solution)/shard_map/ppermute | solution.py:291
  19.2 5.7 %collective-permute-start.15 = (f32[64,256]{1,0:T(8,128)S(1)}, f32[64,256]{1,0:T(8,128)S(1)}, u32[]{:S(2)}, u32[]{:S(2)}) collective-permute-start(f32[64,256]{1,0:T(8,128)S(1)} %get-tuple-element.57.refs_0_), channel_id=1, source_target_pairs={{0,2},{1,3},{2,0},{3,1},{4,6},{5,7},{6,4},{7,5},{8,10},{9,11},{10,... | collective-permute-start | bytes 196616 | tf_op jit(solution)/shard_map/ppermute | solution.py:291
  20.5 6.2 %collective-permute-start.14 = (f32[64,256]{1,0:T(8,128)S(1)}, f32[64,256]{1,0:T(8,128)S(1)}, u32[]{:S(2)}, u32[]{:S(2)}) collective-permute-start(f32[64,256]{1,0:T(8,128)S(1)} %get-tuple-element.56.refs_0_.refs_2_), channel_id=1, source_target_pairs={{0,12},{1,13},{2,14},{3,15},{4,8},{5,9},{6,10},{7,11},{8,4},{9,5},... | collective-permute-start | bytes 196616 | tf_op jit(solution)/shard_map/ppermute | solution.py:291
  23.7 5.6 %collective-permute-start.13 = (f32[64,256]{1,0:T(8,128)S(1)}, f32[64,256]{1,0:T(8,128)S(1)}, u32[]{:S(2)}, u32[]{:S(2)}) collective-permute-start(f32[64,256]{1,0:T(8,128)S(1)} %get-tuple-element.56.refs_0_.refs_2_), channel_id=1, source_target_pairs={{0,8},{1,9},{2,10},{3,11},{4,12},{5,13},{6,14},{7,15},{8,0},{9,1},... | collective-permute-start | bytes 196616 | tf_op jit(solution)/shard_map/ppermute | solution.py:291
  23.7 5.6 %collective-permute-start.12 = (f32[64,256]{1,0:T(8,128)S(1)}, f32[64,256]{1,0:T(8,128)S(1)}, u32[]{:S(2)}, u32[]{:S(2)}) collective-permute-start(f32[64,256]{1,0:T(8,128)S(1)} %get-tuple-element.56.refs_0_.refs_2_), channel_id=1, source_target_pairs={{0,4},{1,5},{2,6},{3,7},{4,0},{5,1},{6,2},{7,3},{8,12},{9,13},{10,... | collective-permute-start | bytes 196616 | tf_op jit(solution)/shard_map/ppermute | solution.py:291
  24.9 4.8 %collective-permute-start.16 = (f32[64,256]{1,0:T(8,128)S(1)}, f32[64,256]{1,0:T(8,128)S(1)}, u32[]{:S(2)}, u32[]{:S(2)}) collective-permute-start(f32[64,256]{1,0:T(8,128)S(1)} %shard_map.60.refs_0_), channel_id=1, source_target_pairs={{0,4},{1,5},{2,6},{3,7},{4,0},{5,1},{6,2},{7,3},{8,12},{9,13},{10,... | collective-permute-start | bytes 196616 | tf_op jit(solution)/shard_map/ppermute | solution.py:291
  25.8 4.0 %collective-permute-start.18 = (f32[128,256]{1,0:T(8,128)S(1)}, f32[128,256]{1,0:T(8,128)S(1)}, u32[]{:S(2)}, u32[]{:S(2)}) collective-permute-start(f32[128,256]{1,0:T(8,128)S(1)} %shard_map.62.refs_2_), channel_id=1, source_target_pairs={{0,1},{1,0},{2,3},{3,2},{4,5},{5,4},{6,7},{7,6},{8,9},{9,8},{10,11... | collective-permute-start | bytes 393224 | tf_op jit(solution)/shard_map/ppermute | solution.py:291
  30.0 7.5 %collective-permute-start.21 = (f32[64,256]{1,0:T(8,128)S(1)}, f32[64,256]{1,0:T(8,128)S(1)}, u32[]{:S(2)}, u32[]{:S(2)}) collective-permute-start(f32[64,256]{1,0:T(8,128)S(1)} %shard_map.63.refs_3_.refs_0_), channel_id=1, source_target_pairs={{0,24},{1,25},{2,26},{3,27},{4,28},{5,29},{6,30},{7,31},{8,16},{9,... | collective-permute-start | bytes 196616 | tf_op jit(solution)/shard_map/ppermute | solution.py:293
  32.8 6.2 %collective-permute-start.20 = (f32[64,256]{1,0:T(8,128)S(1)}, f32[64,256]{1,0:T(8,128)S(1)}, u32[]{:S(2)}, u32[]{:S(2)}) collective-permute-start(f32[64,256]{1,0:T(8,128)S(1)} %shard_map.63.refs_3_.refs_0_), channel_id=1, source_target_pairs={{0,8},{1,9},{2,10},{3,11},{4,12},{5,13},{6,14},{7,15},{8,0},{9,1},... | collective-permute-start | bytes 196616 | tf_op jit(solution)/shard_map/ppermute | solution.py:291
  33.9 5.0 %collective-permute-start.22 = (f32[64,256]{1,0:T(8,128)S(1)}, f32[64,256]{1,0:T(8,128)S(1)}, u32[]{:S(2)}, u32[]{:S(2)}) collective-permute-start(f32[64,256]{1,0:T(8,128)S(1)} %shard_map.63.refs_3_.refs_0_), channel_id=1, source_target_pairs={{0,16},{1,17},{2,18},{3,19},{4,20},{5,21},{6,22},{7,23},{8,24},{9,... | collective-permute-start | bytes 196616 | tf_op jit(solution)/shard_map/ppermute | solution.py:293
  34.5 4.8 %collective-permute-start.19 = (f32[3,64,256]{2,1,0:T(8,128)S(1)}, f32[3,64,256]{2,1,0:T(8,128)S(1)}, u32[]{:S(2)}, u32[]{:S(2)}) collective-permute-start(f32[3,64,256]{2,1,0:T(8,128)S(1)} %shard_map.64.refs_3_), channel_id=1, source_target_pairs={{0,1},{1,0},{2,3},{3,2},{4,5},{5,4},{6,7},{7,6},{8,9},{9,8},{10,11... | collective-permute-start | bytes 589832 | tf_op jit(solution)/shard_map/ppermute | solution.py:291
  39.2 1.3 %collective-permute-start.23 = (f32[64,256]{1,0:T(8,128)S(1)}, f32[64,256]{1,0:T(8,128)S(1)}, u32[]{:S(2)}, u32[]{:S(2)}) collective-permute-start(f32[64,256]{1,0:T(8,128)S(1)} %shard_map.67.own_ref), channel_id=1, source_target_pairs={{0,1},{1,0},{2,3},{3,2},{4,5},{5,4},{6,7},{7,6},{8,9},{9,8},{10,11... | collective-permute-start | bytes 196616 | tf_op jit(solution)/shard_map/ppermute | solution.py:291
  (3 other events, 9.3 us)

commit v6 on v4

--- a/solution.py
+++ b/solution.py
@@ -321,11 +321,11 @@
     sum1 = added(keep, got, after=[keep_cross])
     (weights0,) = run(pair_weights_kernel, [(columns, rank)], own, other, couple, after=[sum1])
     sums, sums_send = run(
-        later_sums_kernel, [(3,) + block, (3,) + block], current, weights0, u_first, basis_v, flops=2 * 10**9
+        later_sums_kernel, [(3,) + block, (3,) + block], current, weights0, u_first, basis_v, flops=4 * 10**9
     )
 
     across = traded(sum1, 2)
-    cross_got = traded(tied(send_cross, sum1), 1)
+    cross_got = traded(send_cross, 1)
     early_got = traded(tied(early, sum1), 1)
     sums_got = traded(sums_send, 1)
     cross32, cross43 = run(mix_kernel, [rows, rows], keep_cross, cross_got, flops=2 * 10**9)

time: 41.9 us -> 41 us (0.979)
  waiting for transfers between devices: 11 us -> 10.1 us
    ppermute x22, waiting for transfers between devices: 7.98 us -> 7.02 us  [traded(): lax.ppermute(value, 'sub', [(source, source ^ mask) for source in range(l...]
  transfers between devices with their start and end apart: 24 -> 24, of which waited for: 10 -> 10; matrix products, arithmetic and copies ran while one was open for 0% -> 0% of each run, Pallas kernels for 10% -> 11%
where the time goes in v6:
time: 41 us; the launch traced here: 40.9 us
  starting transfers between devices  23.2 us (57%)
  waiting for transfers between devices  10.1 us (25%)
  Pallas kernels  7.37 us (18%)
    ppermute x22, starting transfers between devices, traded(): lax.ppermute(value, 'sub', [(source, source ^ mask) for source in range(l...  19.7 us
    ppermute x22, waiting for transfers between devices, traded(): lax.ppermute(value, 'sub', [(source, source ^ mask) for source in range(l...  7.02 us
    pallas_call x22, Pallas kernels, run(): pl.pallas_call(lambda *refs: kernel(*refs[:len(args)], *refs[len(args) +...  4.88 us
    ppermute x2, starting transfers between devices, traded(): lax.ppermute(value, AXES, [(source, source ^ mask) for source in range(de...  3.5 us
    ppermute x2, waiting for transfers between devices, traded(): lax.ppermute(value, AXES, [(source, source ^ mask) for source in range(de...  3.03 us
    pallas_call x1, Pallas kernels, run_start(): pl.pallas_call(start_kernel, out_shape=outs, in_specs=[pl.BlockSpec(memor...  1.47 us
    pallas_call x1, Pallas kernels, run_last(): pl.pallas_call(functools.partial(last_kernel, level, chunks), out_shape=j...  1.02 us
  transfers between devices with their start and end apart: 24, of which 10 were waited for; matrix products, arithmetic and copies ran while one was open for 0% of the time, Pallas kernels for 11%

profile of v6, /device:TPU:0, one launch (start us, length us, event | category | flops | bytes accessed | tf_op | source)
XLA Modules:
  0.0 40.9 jit_solution(15655580766039563059)
XLA Ops:
  0.0 1.5 %shard_map.46 = (f32[128,512]{1,0:T(8,128)S(1)}, f32[128,256]{1,0:T(8,128)S(1)}, bf16[512,256]{1,0:T(8,128)(2,1)S(1)}, bf16[512,256]{1,0:T(8,128)(2,1)S(1)}, bf1...) custom-call(f32[512,128]{1,0:T(8,128)} %right_hbm.1, bf16[5,512,256]{2,1,0:T(8,128)(2,1)} %u_ref.1, ...), custom_call_target="tpu_custom_call" | custom-call | tf_op jit(solution)/shard_map/pallas_call | solution.py:284
  2.0 0.6 %shard_map.47 = (f32[128,256]{1,0:T(8,128)S(1)}, f32[512,256]{1,0:T(8,128)S(1)}) custom-call(f32[128,512]{1,0:T(8,128)S(1)} %get-tuple-element.34.refs_0_, bf16[512,256]{1,0:T(8,128)(2,1)S(1)} %get-tuple-element.35.refs_1_.refs_2_, bf16[512,256]{1,0:T(8,128)(2,1)S(1)} %get-tuple-element.36.refs_2_, bf16[256,512]{1,0:T(8,128)(2,1)S(1)} %get-tuple-element.33.refs_3_.refs_2_), custom_call_target="tpu_custom_call" | custom-call | tf_op jit(solution)/shard_map/pallas_call | solution.py:255
  3.7 0.6 %shard_map.49 = (f32[4,256,256]{2,1,0:T(8,128)S(1)}, f32[2,128,256]{2,1,0:T(8,128)S(1)}, f32[2,128,256]{2,1,0:T(8,128)S(1)}) custom-call(bf16[5,512,256]{2,1,0:T(8,128)(2,1)S(1)} %copy-done.1, bf16[5,512,256]{2,1,0:T(8,128)(2,1)S(1)} %copy-done.2, f32[64,256]{1,0:T(8,128)S(1)} %get-tuple-element.39.refs_2_.refs_0_), custom_call_target="tpu_custom_call" | custom-call | flops 2000000000 | tf_op jit(solution)/shard_map/pallas_call | solution.py:255
  4.7 2.9 %collective-permute-start.2 = (f32[64,256]{1,0:T(8,128)S(1)}, f32[64,256]{1,0:T(8,128)S(1)}, u32[]{:S(2)}, u32[]{:S(2)}) collective-permute-start(f32[64,256]{1,0:T(8,128)S(1)} %shard_map.50.refs_3_.refs_0_), channel_id=1, source_target_pairs={{0,2},{1,3},{2,0},{3,1},{4,6},{5,7},{6,4},{7,5},{8,10},{9,11},{10,... | collective-permute-start | bytes 196616 | tf_op jit(solution)/shard_map/ppermute | solution.py:300
  7.8 0.6 %shard_map.53 = (f32[3,64,256]{2,1,0:T(8,128)S(1)}, f32[3,64,256]{2,1,0:T(8,128)S(1)}) custom-call(f32[128,512]{1,0:T(8,128)S(1)} %get-tuple-element.34.refs_0_, f32[128,256]{1,0:T(8,128)S(1)} %shard_map.51.refs_1_.refs_2_, bf16[512,256]{1,0:T(8,128)(2,1)S(1)} %get-tuple-element.35.refs_1_.refs_2_, bf16[5,512,256]{2,1,0:T(8,128)(2,1)S(1)} %copy-done.2), custom_call_target="tpu_custom_call" | custom-call | flops 4000000000 | tf_op jit(solution)/shard_map/pallas_call | solution.py:255
  9.2 2.0 %collective-permute-start.10 = (f32[128,256]{1,0:T(8,128)S(1)}, f32[128,256]{1,0:T(8,128)S(1)}, u32[]{:S(2)}, u32[]{:S(2)}) collective-permute-start(f32[128,256]{1,0:T(8,128)S(1)} %get-tuple-element.50.refs_2_), channel_id=1, source_target_pairs={{0,4},{1,5},{2,6},{3,7},{4,0},{5,1},{6,2},{7,3},{8,12},{9,13},{10,... | collective-permute-start | bytes 393224 | tf_op jit(solution)/shard_map/ppermute | solution.py:300
  11.8 1.6 %collective-permute-start.5 = (f32[2,64,256]{2,1,0:T(8,128)S(1)}, f32[2,64,256]{2,1,0:T(8,128)S(1)}, u32[]{:S(2)}, u32[]{:S(2)}) collective-permute-start(f32[2,64,256]{2,1,0:T(8,128)S(1)} %get-tuple-element.47.refs_3_), channel_id=1, source_target_pairs={{0,2},{1,3},{2,0},{3,1},{4,6},{5,7},{6,4},{7,5},{8,10},{9,11},{10,... | collective-permute-start | bytes 393224 | tf_op jit(solution)/shard_map/ppermute | solution.py:300
  13.3 0.6 %collective-permute-start.7 = (f32[64,256]{1,0:T(8,128)S(1)}, f32[64,256]{1,0:T(8,128)S(1)}, u32[]{:S(2)}, u32[]{:S(2)}) collective-permute-start(f32[64,256]{1,0:T(8,128)S(1)} %get-tuple-element.46.refs_0_), channel_id=1, source_target_pairs={{0,6},{1,7},{2,4},{3,5},{4,2},{5,3},{6,0},{7,1},{8,14},{9,15},{10,... | collective-permute-start | bytes 196616 | tf_op jit(solution)/shard_map/ppermute | solution.py:300
  14.0 1.4 %collective-permute-start.6 = (f32[64,256]{1,0:T(8,128)S(1)}, f32[64,256]{1,0:T(8,128)S(1)}, u32[]{:S(2)}, u32[]{:S(2)}) collective-permute-start(f32[64,256]{1,0:T(8,128)S(1)} %get-tuple-element.46.refs_0_), channel_id=1, source_target_pairs={{0,4},{1,5},{2,6},{3,7},{4,0},{5,1},{6,2},{7,3},{8,12},{9,13},{10,... | collective-permute-start | bytes 196616 | tf_op jit(solution)/shard_map/ppermute | solution.py:300
  15.7 1.6 %collective-permute-start.17 = (f32[128,256]{1,0:T(8,128)S(1)}, f32[128,256]{1,0:T(8,128)S(1)}, u32[]{:S(2)}, u32[]{:S(2)}) collective-permute-start(f32[128,256]{1,0:T(8,128)S(1)} %get-tuple-element.56.refs_0_), channel_id=1, source_target_pairs={{0,2},{1,3},{2,0},{3,1},{4,6},{5,7},{6,4},{7,5},{8,10},{9,11},{10,... | collective-permute-start | bytes 393224 | tf_op jit(solution)/shard_map/ppermute | solution.py:300
  17.2 1.4 %collective-permute-done.7.refs_3_ = f32[64,256]{1,0:T(8,128)S(1)} collective-permute-done((f32[64,256]{1,0:T(8,128)S(1)}, f32[64,256]{1,0:T(8,128)S(1)}, u32[]{:S(2)}, u32[]{:S(2)}) %collective-permute-start.7) | collective-permute-done | bytes 65568 | tf_op jit(solution)/shard_map/ppermute | solution.py:300
  19.3 1.1 %collective-permute-start.15 = (f32[64,256]{1,0:T(8,128)S(1)}, f32[64,256]{1,0:T(8,128)S(1)}, u32[]{:S(2)}, u32[]{:S(2)}) collective-permute-start(f32[64,256]{1,0:T(8,128)S(1)} %get-tuple-element.55.refs_0_), channel_id=1, source_target_pairs={{0,2},{1,3},{2,0},{3,1},{4,6},{5,7},{6,4},{7,5},{8,10},{9,11},{10,... | collective-permute-start | bytes 196616 | tf_op jit(solution)/shard_map/ppermute | solution.py:300
  20.3 3.4 %collective-permute-start.14 = (f32[64,256]{1,0:T(8,128)S(1)}, f32[64,256]{1,0:T(8,128)S(1)}, u32[]{:S(2)}, u32[]{:S(2)}) collective-permute-start(f32[64,256]{1,0:T(8,128)S(1)} %get-tuple-element.54.refs_0_.refs_2_), channel_id=1, source_target_pairs={{0,12},{1,13},{2,14},{3,15},{4,8},{5,9},{6,10},{7,11},{8,4},{9,5},... | collective-permute-start | bytes 196616 | tf_op jit(solution)/shard_map/ppermute | solution.py:300
  23.7 1.0 %collective-permute-start.12 = (f32[64,256]{1,0:T(8,128)S(1)}, f32[64,256]{1,0:T(8,128)S(1)}, u32[]{:S(2)}, u32[]{:S(2)}) collective-permute-start(f32[64,256]{1,0:T(8,128)S(1)} %get-tuple-element.54.refs_0_.refs_2_), channel_id=1, source_target_pairs={{0,4},{1,5},{2,6},{3,7},{4,0},{5,1},{6,2},{7,3},{8,12},{9,13},{10,... | collective-permute-start | bytes 196616 | tf_op jit(solution)/shard_map/ppermute | solution.py:300
  24.8 1.1 %collective-permute-start.16 = (f32[64,256]{1,0:T(8,128)S(1)}, f32[64,256]{1,0:T(8,128)S(1)}, u32[]{:S(2)}, u32[]{:S(2)}) collective-permute-start(f32[64,256]{1,0:T(8,128)S(1)} %shard_map.61.refs_0_), channel_id=1, source_target_pairs={{0,4},{1,5},{2,6},{3,7},{4,0},{5,1},{6,2},{7,3},{8,12},{9,13},{10,... | collective-permute-start | bytes 196616 | tf_op jit(solution)/shard_map/ppermute | solution.py:300
  25.9 0.6 %collective-permute-done.14.refs_3_ = f32[64,256]{1,0:T(8,128)S(1)} collective-permute-done((f32[64,256]{1,0:T(8,128)S(1)}, f32[64,256]{1,0:T(8,128)S(1)}, u32[]{:S(2)}, u32[]{:S(2)}) %collective-permute-start.14) | collective-permute-done | bytes 65568 | tf_op jit(solution)/shard_map/ppermute | solution.py:300
  26.5 2.8 %collective-permute-done.13.refs_2_ = f32[64,256]{1,0:T(8,128)S(1)} collective-permute-done((f32[64,256]{1,0:T(8,128)S(1)}, f32[64,256]{1,0:T(8,128)S(1)}, u32[]{:S(2)}, u32[]{:S(2)}) %collective-permute-start.13) | collective-permute-done | bytes 65568 | tf_op jit(solution)/shard_map/ppermute | solution.py:300
  30.0 2.9 %collective-permute-start.21 = (f32[64,256]{1,0:T(8,128)S(1)}, f32[64,256]{1,0:T(8,128)S(1)}, u32[]{:S(2)}, u32[]{:S(2)}) collective-permute-start(f32[64,256]{1,0:T(8,128)S(1)} %shard_map.64.refs_3_.refs_0_), channel_id=1, source_target_pairs={{0,24},{1,25},{2,26},{3,27},{4,28},{5,29},{6,30},{7,31},{8,16},{9,... | collective-permute-start | bytes 196616 | tf_op jit(solution)/shard_map/ppermute | solution.py:302
  32.8 1.0 %collective-permute-start.20 = (f32[64,256]{1,0:T(8,128)S(1)}, f32[64,256]{1,0:T(8,128)S(1)}, u32[]{:S(2)}, u32[]{:S(2)}) collective-permute-start(f32[64,256]{1,0:T(8,128)S(1)} %shard_map.64.refs_3_.refs_0_), channel_id=1, source_target_pairs={{0,8},{1,9},{2,10},{3,11},{4,12},{5,13},{6,14},{7,15},{8,0},{9,1},... | collective-permute-start | bytes 196616 | tf_op jit(solution)/shard_map/ppermute | solution.py:300
  33.9 0.6 %collective-permute-start.22 = (f32[64,256]{1,0:T(8,128)S(1)}, f32[64,256]{1,0:T(8,128)S(1)}, u32[]{:S(2)}, u32[]{:S(2)}) collective-permute-start(f32[64,256]{1,0:T(8,128)S(1)} %shard_map.64.refs_3_.refs_0_), channel_id=1, source_target_pairs={{0,16},{1,17},{2,18},{3,19},{4,20},{5,21},{6,22},{7,23},{8,24},{9,... | collective-permute-start | bytes 196616 | tf_op jit(solution)/shard_map/ppermute | solution.py:302
  34.5 3.0 %collective-permute-done.21.refs_2_ = f32[64,256]{1,0:T(8,128)S(1)} collective-permute-done((f32[64,256]{1,0:T(8,128)S(1)}, f32[64,256]{1,0:T(8,128)S(1)}, u32[]{:S(2)}, u32[]{:S(2)}) %collective-permute-start.21) | collective-permute-done | bytes 65568 | tf_op jit(solution)/shard_map/ppermute | solution.py:302
  37.5 0.8 %collective-permute-done.20.refs_1_ = f32[64,256]{1,0:T(8,128)S(1)} collective-permute-done((f32[64,256]{1,0:T(8,128)S(1)}, f32[64,256]{1,0:T(8,128)S(1)}, u32[]{:S(2)}, u32[]{:S(2)}) %collective-permute-start.20) | collective-permute-done | bytes 65568 | tf_op jit(solution)/shard_map/ppermute | solution.py:300
  39.2 0.7 %collective-permute-done.23.other_ref = f32[64,256]{1,0:T(8,128)S(1)} collective-permute-done((f32[64,256]{1,0:T(8,128)S(1)}, f32[64,256]{1,0:T(8,128)S(1)}, u32[]{:S(2)}, u32[]{:S(2)}) %collective-permute-start.23) | collective-permute-done | bytes 65568 | tf_op jit(solution)/shard_map/ppermute | solution.py:300
  39.9 1.0 %shard_map.69 = f32[512,128]{1,0:T(8,128)} custom-call(f32[512,128]{1,0:T(8,128)S(1)} %shard_map.66.partial_ref, f32[64,256]{1,0:T(8,128)S(1)} %shard_map.68.own_ref, f32[64,256]{1,0:T(8,128)S(1)} %collective-permute-done.23.other_ref, bf16[5,512,256]{2,1,0:T(8,128)(2,1)S(1)} %copy-done.1), custom_call_target="tpu_custom_call" | custom-call | tf_op jit(solution)/shard_map/pallas_call | solution.py:243
  (54 shorter events, 6.1 us)
Async XLA Ops:
  1.5 1.5 %collective-permute-start = (f32[128,256]{1,0:T(8,128)S(1)}, f32[128,256]{1,0:T(8,128)S(1)}, u32[]{:S(2)}, u32[]{:S(2)}) collective-permute-start(f32[128,256]{1,0:T(8,128)S(1)} %get-tuple-element.32.refs_0_), channel_id=1, source_target_pairs={{0,1},{1,0},{2,3},{3,2},{4,5},{5,4},{6,7},{7,6},{8,9},{9,8},{10,11... | collective-permute-start | bytes 393224 | tf_op jit(solution)/shard_map/ppermute | solution.py:300
  3.3 1.3 %collective-permute-start.1 = (f32[64,256]{1,0:T(8,128)S(1)}, f32[64,256]{1,0:T(8,128)S(1)}, u32[]{:S(2)}, u32[]{:S(2)}) collective-permute-start(f32[64,256]{1,0:T(8,128)S(1)} %get-tuple-element.40), channel_id=1, source_target_pairs={{0,1},{1,0},{2,3},{3,2},{4,5},{5,4},{6,7},{7,6},{8,9},{9,8},{10,11... | collective-permute-start | bytes 196616 | tf_op jit(solution)/shard_map/ppermute | solution.py:300
  4.4 4.7 %collective-permute-start.8 = (f32[2,128,256]{2,1,0:T(8,128)S(1)}, f32[2,128,256]{2,1,0:T(8,128)S(1)}, u32[]{:S(2)}, u32[]{:S(2)}) collective-permute-start(f32[2,128,256]{2,1,0:T(8,128)S(1)} %get-tuple-element.48), channel_id=1, source_target_pairs={{0,1},{1,0},{2,3},{3,2},{4,5},{5,4},{6,7},{7,6},{8,9},{9,8},{10,11... | collective-permute-start | bytes 786440 | tf_op jit(solution)/shard_map/ppermute | solution.py:300
  4.7 6.6 %collective-permute-start.2 = (f32[64,256]{1,0:T(8,128)S(1)}, f32[64,256]{1,0:T(8,128)S(1)}, u32[]{:S(2)}, u32[]{:S(2)}) collective-permute-start(f32[64,256]{1,0:T(8,128)S(1)} %shard_map.50.refs_3_.refs_0_), channel_id=1, source_target_pairs={{0,2},{1,3},{2,0},{3,1},{4,6},{5,7},{6,4},{7,5},{8,10},{9,11},{10,... | collective-permute-start | bytes 196616 | tf_op jit(solution)/shard_map/ppermute | solution.py:300
  7.6 3.9 %collective-permute-start.3 = (f32[4,256,256]{2,1,0:T(8,128)S(1)}, f32[4,256,256]{2,1,0:T(8,128)S(1)}, u32[]{:S(2)}, u32[]{:S(2)}) collective-permute-start(f32[4,256,256]{2,1,0:T(8,128)S(1)} %get-tuple-element.43.refs_1_), channel_id=1, source_target_pairs={{0,1},{1,0},{2,3},{3,2},{4,5},{5,4},{6,7},{7,6},{8,9},{9,8},{10,11... | collective-permute-start | bytes 3145736 | tf_op jit(solution)/shard_map/ppermute | solution.py:300
  8.5 3.0 %collective-permute-start.4 = (f32[3,64,256]{2,1,0:T(8,128)S(1)}, f32[3,64,256]{2,1,0:T(8,128)S(1)}, u32[]{:S(2)}, u32[]{:S(2)}) collective-permute-start(f32[3,64,256]{2,1,0:T(8,128)S(1)} %get-tuple-element.45), channel_id=1, source_target_pairs={{0,1},{1,0},{2,3},{3,2},{4,5},{5,4},{6,7},{7,6},{8,9},{9,8},{10,11... | collective-permute-start | bytes 589832 | tf_op jit(solution)/shard_map/ppermute | solution.py:300
  9.1 6.5 %collective-permute-start.9 = (f32[128,256]{1,0:T(8,128)S(1)}, f32[128,256]{1,0:T(8,128)S(1)}, u32[]{:S(2)}, u32[]{:S(2)}) collective-permute-start(f32[128,256]{1,0:T(8,128)S(1)} %get-tuple-element.49.refs_0_), channel_id=1, source_target_pairs={{0,2},{1,3},{2,0},{3,1},{4,6},{5,7},{6,4},{7,5},{8,10},{9,11},{10,... | collective-permute-start | bytes 393224 | tf_op jit(solution)/shard_map/ppermute | solution.py:300
  9.2 6.3 %collective-permute-start.10 = (f32[128,256]{1,0:T(8,128)S(1)}, f32[128,256]{1,0:T(8,128)S(1)}, u32[]{:S(2)}, u32[]{:S(2)}) collective-permute-start(f32[128,256]{1,0:T(8,128)S(1)} %get-tuple-element.50.refs_2_), channel_id=1, source_target_pairs={{0,4},{1,5},{2,6},{3,7},{4,0},{5,1},{6,2},{7,3},{8,12},{9,13},{10,... | collective-permute-start | bytes 393224 | tf_op jit(solution)/shard_map/ppermute | solution.py:300
  11.8 7.0 %collective-permute-start.5 = (f32[2,64,256]{2,1,0:T(8,128)S(1)}, f32[2,64,256]{2,1,0:T(8,128)S(1)}, u32[]{:S(2)}, u32[]{:S(2)}) collective-permute-start(f32[2,64,256]{2,1,0:T(8,128)S(1)} %get-tuple-element.47.refs_3_), channel_id=1, source_target_pairs={{0,2},{1,3},{2,0},{3,1},{4,6},{5,7},{6,4},{7,5},{8,10},{9,11},{10,... | collective-permute-start | bytes 393224 | tf_op jit(solution)/shard_map/ppermute | solution.py:300
  13.3 5.3 %collective-permute-start.7 = (f32[64,256]{1,0:T(8,128)S(1)}, f32[64,256]{1,0:T(8,128)S(1)}, u32[]{:S(2)}, u32[]{:S(2)}) collective-permute-start(f32[64,256]{1,0:T(8,128)S(1)} %get-tuple-element.46.refs_0_), channel_id=1, source_target_pairs={{0,6},{1,7},{2,4},{3,5},{4,2},{5,3},{6,0},{7,1},{8,14},{9,15},{10,... | collective-permute-start | bytes 196616 | tf_op jit(solution)/shard_map/ppermute | solution.py:300
  14.0 4.6 %collective-permute-start.6 = (f32[64,256]{1,0:T(8,128)S(1)}, f32[64,256]{1,0:T(8,128)S(1)}, u32[]{:S(2)}, u32[]{:S(2)}) collective-permute-start(f32[64,256]{1,0:T(8,128)S(1)} %get-tuple-element.46.refs_0_), channel_id=1, source_target_pairs={{0,4},{1,5},{2,6},{3,7},{4,0},{5,1},{6,2},{7,3},{8,12},{9,13},{10,... | collective-permute-start | bytes 196616 | tf_op jit(solution)/shard_map/ppermute | solution.py:300
  15.6 3.4 %collective-permute-start.11 = (f32[128,256]{1,0:T(8,128)S(1)}, f32[128,256]{1,0:T(8,128)S(1)}, u32[]{:S(2)}, u32[]{:S(2)}) collective-permute-start(f32[128,256]{1,0:T(8,128)S(1)} %get-tuple-element.52.refs_1_), channel_id=1, source_target_pairs={{0,1},{1,0},{2,3},{3,2},{4,5},{5,4},{6,7},{7,6},{8,9},{9,8},{10,11... | collective-permute-start | bytes 393224 | tf_op jit(solution)/shard_map/ppermute | solution.py:300
  15.7 10.1 %collective-permute-start.17 = (f32[128,256]{1,0:T(8,128)S(1)}, f32[128,256]{1,0:T(8,128)S(1)}, u32[]{:S(2)}, u32[]{:S(2)}) collective-permute-start(f32[128,256]{1,0:T(8,128)S(1)} %get-tuple-element.56.refs_0_), channel_id=1, source_target_pairs={{0,2},{1,3},{2,0},{3,1},{4,6},{5,7},{6,4},{7,5},{8,10},{9,11},{10,... | collective-permute-start | bytes 393224 | tf_op jit(solution)/shard_map/ppermute | solution.py:300
  19.3 5.5 %collective-permute-start.15 = (f32[64,256]{1,0:T(8,128)S(1)}, f32[64,256]{1,0:T(8,128)S(1)}, u32[]{:S(2)}, u32[]{:S(2)}) collective-permute-start(f32[64,256]{1,0:T(8,128)S(1)} %get-tuple-element.55.refs_0_), channel_id=1, source_target_pairs={{0,2},{1,3},{2,0},{3,1},{4,6},{5,7},{6,4},{7,5},{8,10},{9,11},{10,... | collective-permute-start | bytes 196616 | tf_op jit(solution)/shard_map/ppermute | solution.py:300
  20.3 6.2 %collective-permute-start.14 = (f32[64,256]{1,0:T(8,128)S(1)}, f32[64,256]{1,0:T(8,128)S(1)}, u32[]{:S(2)}, u32[]{:S(2)}) collective-permute-start(f32[64,256]{1,0:T(8,128)S(1)} %get-tuple-element.54.refs_0_.refs_2_), channel_id=1, source_target_pairs={{0,12},{1,13},{2,14},{3,15},{4,8},{5,9},{6,10},{7,11},{8,4},{9,5},... | collective-permute-start | bytes 196616 | tf_op jit(solution)/shard_map/ppermute | solution.py:300
  23.7 5.6 %collective-permute-start.13 = (f32[64,256]{1,0:T(8,128)S(1)}, f32[64,256]{1,0:T(8,128)S(1)}, u32[]{:S(2)}, u32[]{:S(2)}) collective-permute-start(f32[64,256]{1,0:T(8,128)S(1)} %get-tuple-element.54.refs_0_.refs_2_), channel_id=1, source_target_pairs={{0,8},{1,9},{2,10},{3,11},{4,12},{5,13},{6,14},{7,15},{8,0},{9,1},... | collective-permute-start | bytes 196616 | tf_op jit(solution)/shard_map/ppermute | solution.py:300
  23.7 5.6 %collective-permute-start.12 = (f32[64,256]{1,0:T(8,128)S(1)}, f32[64,256]{1,0:T(8,128)S(1)}, u32[]{:S(2)}, u32[]{:S(2)}) collective-permute-start(f32[64,256]{1,0:T(8,128)S(1)} %get-tuple-element.54.refs_0_.refs_2_), channel_id=1, source_target_pairs={{0,4},{1,5},{2,6},{3,7},{4,0},{5,1},{6,2},{7,3},{8,12},{9,13},{10,... | collective-permute-start | bytes 196616 | tf_op jit(solution)/shard_map/ppermute | solution.py:300
  24.8 5.0 %collective-permute-start.16 = (f32[64,256]{1,0:T(8,128)S(1)}, f32[64,256]{1,0:T(8,128)S(1)}, u32[]{:S(2)}, u32[]{:S(2)}) collective-permute-start(f32[64,256]{1,0:T(8,128)S(1)} %shard_map.61.refs_0_), channel_id=1, source_target_pairs={{0,4},{1,5},{2,6},{3,7},{4,0},{5,1},{6,2},{7,3},{8,12},{9,13},{10,... | collective-permute-start | bytes 196616 | tf_op jit(solution)/shard_map/ppermute | solution.py:300
  25.8 3.9 %collective-permute-start.18 = (f32[128,256]{1,0:T(8,128)S(1)}, f32[128,256]{1,0:T(8,128)S(1)}, u32[]{:S(2)}, u32[]{:S(2)}) collective-permute-start(f32[128,256]{1,0:T(8,128)S(1)} %shard_map.63.refs_2_), channel_id=1, source_target_pairs={{0,1},{1,0},{2,3},{3,2},{4,5},{5,4},{6,7},{7,6},{8,9},{9,8},{10,11... | collective-permute-start | bytes 393224 | tf_op jit(solution)/shard_map/ppermute | solution.py:300
  30.0 7.6 %collective-permute-start.21 = (f32[64,256]{1,0:T(8,128)S(1)}, f32[64,256]{1,0:T(8,128)S(1)}, u32[]{:S(2)}, u32[]{:S(2)}) collective-permute-start(f32[64,256]{1,0:T(8,128)S(1)} %shard_map.64.refs_3_.refs_0_), channel_id=1, source_target_pairs={{0,24},{1,25},{2,26},{3,27},{4,28},{5,29},{6,30},{7,31},{8,16},{9,... | collective-permute-start | bytes 196616 | tf_op jit(solution)/shard_map/ppermute | solution.py:302
  32.8 5.4 %collective-permute-start.20 = (f32[64,256]{1,0:T(8,128)S(1)}, f32[64,256]{1,0:T(8,128)S(1)}, u32[]{:S(2)}, u32[]{:S(2)}) collective-permute-start(f32[64,256]{1,0:T(8,128)S(1)} %shard_map.64.refs_3_.refs_0_), channel_id=1, source_target_pairs={{0,8},{1,9},{2,10},{3,11},{4,12},{5,13},{6,14},{7,15},{8,0},{9,1},... | collective-permute-start | bytes 196616 | tf_op jit(solution)/shard_map/ppermute | solution.py:300
  33.9 4.4 %collective-permute-start.22 = (f32[64,256]{1,0:T(8,128)S(1)}, f32[64,256]{1,0:T(8,128)S(1)}, u32[]{:S(2)}, u32[]{:S(2)}) collective-permute-start(f32[64,256]{1,0:T(8,128)S(1)} %shard_map.64.refs_3_.refs_0_), channel_id=1, source_target_pairs={{0,16},{1,17},{2,18},{3,19},{4,20},{5,21},{6,22},{7,23},{8,24},{9,... | collective-permute-start | bytes 196616 | tf_op jit(solution)/shard_map/ppermute | solution.py:302
  34.5 4.1 %collective-permute-start.19 = (f32[3,64,256]{2,1,0:T(8,128)S(1)}, f32[3,64,256]{2,1,0:T(8,128)S(1)}, u32[]{:S(2)}, u32[]{:S(2)}) collective-permute-start(f32[3,64,256]{2,1,0:T(8,128)S(1)} %shard_map.65.refs_3_), channel_id=1, source_target_pairs={{0,1},{1,0},{2,3},{3,2},{4,5},{5,4},{6,7},{7,6},{8,9},{9,8},{10,11... | collective-permute-start | bytes 589832 | tf_op jit(solution)/shard_map/ppermute | solution.py:300
  38.5 1.3 %collective-permute-start.23 = (f32[64,256]{1,0:T(8,128)S(1)}, f32[64,256]{1,0:T(8,128)S(1)}, u32[]{:S(2)}, u32[]{:S(2)}) collective-permute-start(f32[64,256]{1,0:T(8,128)S(1)} %shard_map.68.own_ref), channel_id=1, source_target_pairs={{0,1},{1,0},{2,3},{3,2},{4,5},{5,4},{6,7},{7,6},{8,9},{9,8},{10,11... | collective-permute-start | bytes 196616 | tf_op jit(solution)/shard_map/ppermute | solution.py:300
  (3 other events, 8.8 us)
